TPU v7x, 128 devices: a whole 4x4x4 slice. The times are simulated.
128 devices in a mesh: grp: 16 (over z_lo, x, core), dev: 8 (over y, z_hi).
Axes of the slice: x: 4, y: 4, z: 4 (z_hi: 2, z_lo: 2; z = z_hi * 2 + z_lo), core: 2. Of those that a mesh axis runs over, the one named last changes fastest.
Arguments:
- inputs: bfloat16 [73728, 1024], P(('grp', 'dev')), may hold values from -6 to 6
- cotangent: bfloat16 [73728, 1024], P(('grp', 'dev')), may hold values from -0.088378906 to 0.088378906
- pre_gelu: bfloat16 [73728, 4096], P(('grp', 'dev')), may hold values from -6 to 6
- w_down: bfloat16 [4096, 1024], P('dev'), may hold values from -0.09375 to 0.09375
- error_feedback: bfloat16 [524288, 1024], P(('grp', 'dev')), may hold values from -0.29882812 to 0.29882812
- a_inverse: bfloat16 [1024, 1024], replicated, as said below
- g_inverse: bfloat16 [4096, 4096], P('dev'), as said below
Outputs:
- preconditioned: float32 [4096, 1024], P('dev')
Inputs may be any that keep to these rules, and one draw needn't show every extreme that they name: `a_inverse`: symmetric. `g_inverse`: symmetric.
All inputs are finite; a program needn't handle non-finite values.
Results may differ from a plain program's by a relative error of at most 0.023.
Values may be sent and summed in bfloat16 or wider, within the bound.
No kernel may reach another device: no remote copies, remote signals or barrier semaphores. Data moves between devices by JAX's collectives and lax.ppermute only.
A program may use at most 128 MiB of HBM per device.

v0:
```python
import math

import jax
import jax.numpy as jnp
from jax import lax
from jax.sharding import PartitionSpec as P


def gelu_slope(value):
    cdf = 0.5 * (1.0 + lax.erf(value * (1.0 / math.sqrt(2.0))))
    density = jnp.exp(-0.5 * value * value) * (1.0 / math.sqrt(2.0 * math.pi))
    return cdf + value * density


def shards(inputs, cotangent, pre_gelu, w_down, error_feedback, a_inverse, g_inverse):
    grad_pre = lax.dot_general(
        cotangent,
        lax.all_gather(w_down, "dev", axis=0, tiled=True),
        (((1,), (1,)), ((), ())),
        preferred_element_type=jnp.float32,
    )
    pre = pre_gelu.astype(jnp.float32)
    hidden = (grad_pre * gelu_slope(pre)).astype(jnp.bfloat16)
    columns = hidden
    part = lax.dot_general(
        columns, inputs, (((0,), (0,)), ((), ())), preferred_element_type=jnp.float32
    )
    carried = error_feedback.astype(jnp.float32)
    rounded = lax.optimization_barrier((part + carried).astype(jnp.bfloat16))
    grad = lax.psum_scatter(
        rounded.astype(jnp.float32), ("grp", "dev"), scatter_dimension=0, tiled=True
    )
    grad_rounded = grad.astype(jnp.bfloat16)
    right = jnp.dot(grad_rounded, a_inverse, preferred_element_type=jnp.float32).astype(
        jnp.bfloat16
    )
    columns = g_inverse
    return jnp.dot(
        columns,
        lax.all_gather(right, ("grp", "dev"), axis=0, tiled=True),
        preferred_element_type=jnp.float32,
    )


def solution(mesh):
    placed = (
        P(("grp", "dev"), None),
        P(("grp", "dev"), None),
        P(("grp", "dev"), None),
        P("dev", None),
        P(("grp", "dev"), None),
        P(),
        P("dev", None),
    )
    return jax.shard_map(
        shards, mesh=mesh, in_specs=placed, out_specs=P("dev", None), check_vma=False
    )
```

profile of v0, /device:TPU:1, one launch (start us, length us, event | category | flops | bytes accessed | tf_op | source)
XLA Modules:
  0.0 1159.3 jit_solution(13432416137442996138)
XLA Ops:
  6.5 0.0 copy-start
  6.5 0.0 all-gather.3.cloned.1.call-start
  6.5 0.7 all-gather.3.cloned.1.call-update
  7.3 0.0 reduce-scatter.2.cloned.1.call-start
  7.3 114.2 %all-gather.3.cloned.1.call-done = bf16[4096,1024]{1,0:T(8,128)(2,1)} async-done(((bf16[512,1024]{1,0:T(8,128)(2,1)}), bf16[4096,1024]{1,0:T(8,128)(2,1)}) %all-gather.3.cloned.1.call-update) | async-done | bytes 8388624 | tf_op jit(solution)/shard_map/all_gather | solution.py:18
  121.5 18.7 %add_convert_fusion = bf16[4096,1024]{1,0:T(8,128)(2,1)} fusion(bf16[4096,1024]{1,0:T(8,128)(2,1)} %param.11, bf16[576,1024]{1,0:T(8,128)(2,1)} %param.7, bf16[576,4096]{1,0:T(8,128)(2,1)} %param.9, bf16[576,1024]{1,0:T(8,128)(2,1)} %param.8, bf16[4096,1024]{1,0:T(8,128)(2,1)} %all-gather.3.cloned.1.call-done), kind=kOutput, calls=%fused_computation | convolution fusion | flops 9702211584 | bytes 32243712 | tf_op jit(solution)/shard_map/dot_general | solution.py:25
  140.3 11.3 convert_element_type.25
  151.5 0.0 reduce-scatter.2.cloned.1.call-update
  151.6 0.0 all-gather.5.cloned.1.call-start
  151.6 670.9 %reduce-scatter.2.cloned.1.call-done = f32[32,1024]{1,0:T(8,128)} async-done(((f32[4096,1024]{1,0:T(8,128)}), f32[32,1024]{1,0:T(8,128)}) %reduce-scatter.2.cloned.1.call-update) | async-done | bytes 131088 | tf_op jit(solution)/shard_map/reduce_scatter | solution.py:30
  822.5 0.0 copy-done
  822.5 2.0 convolution_convert_fusion
  824.5 0.0 all-gather.5.cloned.1.call-update
  824.5 314.8 %all-gather.5.cloned.1.call-done = bf16[4096,1024]{1,0:T(8,128)(2,1)} async-done(((bf16[32,1024]{1,0:T(8,128)(2,1)}), bf16[4096,1024]{1,0:T(8,128)(2,1)}) %all-gather.5.cloned.1.call-update) | async-done | bytes 8388624 | tf_op jit(solution)/shard_map/all_gather | solution.py:40
  1139.4 10.5 convolution_bitcast_fusion
  1149.9 2.9 copy.8
Async XLA Ops:
  6.5 816.0 %copy-start = (bf16[1024,1024]{1,0:T(8,128)(2,1)S(1)}, bf16[1024,1024]{1,0:T(8,128)(2,1)}, u32[]{:S(2)}) copy-start(bf16[1024,1024]{1,0:T(8,128)(2,1)} %param.12) | copy-start | bytes 6291460
  6.5 115.0 %all-gather.3.cloned.1.call-start = ((), (), s32[]{:S(2)}) async-start(), calls=%async_computation.1 | async-start | bytes 9437184 | tf_op jit(solution)/shard_map/all_gather | solution.py:18
  7.3 815.3 %reduce-scatter.2.cloned.1.call-start = ((), (), s32[]{:S(2)}) async-start(), calls=%async_computation.2 | async-start | bytes 16908288 | tf_op jit(solution)/shard_map/reduce_scatter | solution.py:30
  151.6 987.8 %all-gather.5.cloned.1.call-start = ((), (), s32[]{:S(2)}) async-start(), calls=%async_computation.3 | async-start | bytes 8454144 | tf_op jit(solution)/shard_map/all_gather | solution.py:40
Sparse Core Ops, SparseCore 0:
  9.7 111.7 all-gather.2
  151.7 670.7 reduce-scatter.1
  824.7 314.6 all-gather.4
where the time goes:
time: 1160 us
  waiting for transfers between devices  1100 us (95%)
  matrix products  31.2 us (3%)
  between operations  13.1 us (1%)
    reduce_scatter x1, waiting for transfers between devices, shards(): lax.psum_scatter(rounded.astype(jnp.float32), ('grp', 'dev'), scatter_dim...  671 us
    all_gather x1, waiting for transfers between devices, shards(): lax.all_gather(right, ('grp', 'dev'), axis=0, tiled=True)  315 us
    all_gather x1, waiting for transfers between devices, shards(): lax.all_gather(w_down, 'dev', axis=0, tiled=True)  114 us
  transfers between devices with their start and end apart: 3, of which 3 were waited for; matrix products, arithmetic and copies ran while one was open for 0% of the time, Pallas kernels for 0%

commit v1 on v0

v1 whole, which is shorter than its diff:
```python
import functools
import math

import jax
import jax.numpy as jnp
from jax import lax
from jax.experimental import pallas as pl
from jax.experimental.pallas import tpu as pltpu
from jax.sharding import Mesh, PartitionSpec as P

AXES = ("zl", "x", "c", "y", "zh")
SIZES = (2, 4, 2, 4, 2)
BF = jnp.bfloat16
F32 = jnp.float32


def gelu_slope(value):
    cdf = 0.5 * (1.0 + lax.erf(value * (1.0 / math.sqrt(2.0))))
    density = jnp.exp(-0.5 * value * value) * (1.0 / math.sqrt(2.0 * math.pi))
    return cdf + value * density


def slope_kernel(core, pre, out):
    out[...] = gelu_slope(pre[...].astype(F32)).T.astype(BF)


def slopes(core, pre):
    return pl.pallas_call(
        slope_kernel,
        grid_spec=pltpu.PrefetchScalarGridSpec(
            num_scalar_prefetch=1,
            grid=(8,),
            in_specs=[pl.BlockSpec((576, 256), lambda i, s: (0, 2 * i + s[0]))],
            out_specs=pl.BlockSpec((256, 576), lambda i, s: (i, 0)),
        ),
        out_shape=jax.ShapeDtypeStruct((2048, 576), BF),
        cost_estimate=pl.CostEstimate(
            flops=60 * 576 * 2048, bytes_accessed=5 * 2**20, transcendentals=2 * 576 * 2048
        ),
    )(core, pre)


def term_kernel(n, by_columns, place, *refs):
    cot, cot_o, inp, inp_o, slope, slope_o, ef, ef_o = refs[:8]
    ws, outs = refs[8 : 8 + n], refs[8 + n :]
    step = pl.program_id(0)
    w = ws[0][...]
    for i in range(1, n):
        w = jnp.where(step == i, ws[i][...], w)
    hidden = []
    for cots, slope_of in ((cot, slope), (cot_o, slope_o)):
        grad_pre = lax.dot_general(
            w, cots[...], (((1,), (1,)), ((), ())), preferred_element_type=F32
        )
        hidden.append((grad_pre * slope_of[...].astype(F32)).astype(BF))
    for j in range(4):
        if by_columns:
            cols = pl.ds(pl.multiple_of(lax.rem(place[2 * n + 1] + j, 4) * 256, 256), 256)
        else:
            cols = slice(j * 256, (j + 1) * 256)
        total = ef[:, cols].astype(F32) + ef_o[:, cols].astype(F32)
        for h, rows in zip(hidden, (inp, inp_o)):
            total += jnp.dot(h, rows[:, cols], preferred_element_type=F32)
        total = total.astype(BF)
        for k in range(2):
            piece = total[:, k * 128 : (k + 1) * 128]
            if by_columns:
                outs[j][0, k] = piece
            else:
                for i in range(n):

                    @pl.when(step == i)
                    def _():
                        outs[i][2 * j + k] = piece


def terms(by_columns, place, cot, cot_o, inp, inp_o, slope, slope_o, ef, ef_o, ws):
    n = len(ws)
    whole = pl.BlockSpec(cot.shape, lambda i, s: (0, 0))
    block = pl.BlockSpec((256, 1024), lambda i, s: (0, 0))
    slice_of = pl.BlockSpec((256, 576), lambda i, s: (s[i], 0))
    carried = pl.BlockSpec((256, 1024), lambda i, s: (s[i] * 2 + s[2 * n], 0))
    carried_o = pl.BlockSpec((256, 1024), lambda i, s: (s[i], 0))
    if by_columns:
        out_specs = [pl.BlockSpec((1, 2, 256, 128), lambda i, s: (s[n + i], 0, 0, 0))] * 4
        out_shape = [jax.ShapeDtypeStruct((n, 2, 256, 128), BF)] * 4
    else:
        out_specs = [pl.BlockSpec((8, 256, 128), lambda i, s: (0, 0, 0))] * n
        out_shape = [jax.ShapeDtypeStruct((8, 256, 128), BF)] * n
    return pl.pallas_call(
        functools.partial(term_kernel, n, by_columns),
        grid_spec=pltpu.PrefetchScalarGridSpec(
            num_scalar_prefetch=1,
            grid=(n,),
            in_specs=[whole] * 4 + [slice_of] * 2 + [carried, carried_o] + [block] * n,
            out_specs=out_specs,
        ),
        out_shape=out_shape,
        compiler_params=pltpu.CompilerParams(vmem_limit_bytes=60 * 2**20),
        cost_estimate=pl.CostEstimate(
            flops=16 * 1152 * 1024 * 256 * n, bytes_accessed=3 * n * 2**20, transcendentals=0
        ),
    )(place, cot, cot_o, inp, inp_o, slope, slope_o, ef, ef_o, *ws)


def left_kernel(core, g, grads, mine, other, total):
    c, step = core[0], pl.program_id(0)

    @pl.when(step == 0)
    def _():
        total[...] = jnp.zeros_like(total)

    for k in range(2):
        cols = pl.ds(pl.multiple_of(k * 512 + c * 256, 256), 256)
        rows = (grads[k, 0].astype(F32) + grads[1 - k, 1].astype(F32)).astype(BF)
        total[...] += jnp.dot(g[:, cols], rows, preferred_element_type=F32)

    @pl.when(step == 3)
    def _():
        mine[...] = total[pl.ds(pl.multiple_of(c * 256, 256), 256), :]
        other[...] = total[pl.ds(pl.multiple_of((1 - c) * 256, 256), 256), :]


def left_product(core, g, grads):
    rows = pl.BlockSpec((256, 128), lambda i, s: (0, 0))
    return pl.pallas_call(
        left_kernel,
        grid_spec=pltpu.PrefetchScalarGridSpec(
            num_scalar_prefetch=1,
            grid=(4,),
            in_specs=[
                pl.BlockSpec((512, 1024), lambda i, s: (0, i)),
                pl.BlockSpec((2, 2, 256, 128), lambda i, s: (i, 0, 0, 0)),
            ],
            out_specs=[rows, rows],
            scratch_shapes=[pltpu.VMEM((512, 128), F32)],
        ),
        out_shape=[jax.ShapeDtypeStruct((256, 128), F32)] * 2,
        cost_estimate=pl.CostEstimate(
            flops=2 * 512 * 2048 * 128, bytes_accessed=5 * 2**20, transcendentals=0
        ),
    )(core, g, grads)


def shards(inputs, cotangent, pre_gelu, w_down, error_feedback, a_inverse, g_inverse):
    c, y, zh = (lax.axis_index(a) for a in ("c", "y", "zh"))
    x = lax.axis_index("x")
    core = c.astype(jnp.int32).reshape(1)

    def swap(a):
        return lax.ppermute(a, "c", [(0, 1), (1, 0)])

    def across_z(a):
        return lax.ppermute(a, ("zl", "zh"), [(i, 3 - i) for i in range(4)])

    def ring(a, axis, step):
        return lax.ppermute(a, axis, [(i, (i + step) % 4) for i in range(4)])

    w_own = lax.dynamic_slice(w_down, (c * 256, 0), (256, 1024))
    first = [ring(w_own, "y", -1), ring(w_own, "y", 1), swap(pre_gelu)]
    carried = lax.dynamic_index_in_dim(
        error_feedback.reshape(8, 2, 256, 1024), 1 - c, 1, keepdims=False
    ).reshape(2048, 1024)
    w_up, w_low, pre_o, carried, pre, cot, inp, w_own = lax.optimization_barrier(
        (*first, carried, pre_gelu, cotangent, inputs, w_own)
    )
    second = [ring(w_own, "y", 2), across_z(w_own), swap(carried), swap(cot), swap(inp)]
    slope, slope_o = slopes(core, pre), slopes(core, pre_o)
    w_far, w_z, ef_o, cot_o, inp_o, slope, slope_o, w_up, w_low = lax.optimization_barrier(
        (*second, slope, slope_o, w_up, w_low)
    )
    third = [ring(w_z, "y", -1), ring(w_z, "y", 1), across_z(w_far)]

    def product(by_columns, part, ws):
        at = [(lax.rem(y + dy, 4), zh ^ dz) for dy, dz in part]
        place = [a * 2 + b for a, b in at] + [a for a, _ in at] + [c, x]
        return terms(
            by_columns, jnp.stack(place).astype(jnp.int32), cot, cot_o, inp, inp_o,
            slope, slope_o, error_feedback, ef_o, ws,
        )

    def added(parts):
        return sum(p.astype(F32) for p in parts).astype(BF)

    def scattered(a, axes):
        return added(lax.all_to_all(a.reshape(8, 256, 128), axes, 0, 0, tiled=True))

    near = product(True, ((0, 0), (1, 0), (3, 0), (2, 0)), [w_own, w_up, w_low, w_far])
    near, third = lax.optimization_barrier((near, third))
    near = added([near[0]] + [ring(near[j], "x", j) for j in (1, 2, 3)])
    far, up = product(False, ((2, 1), (1, 1)), [third[2], third[0]])
    low, own = product(False, ((3, 1), (0, 1)), [third[1], w_z])
    others = added([own, ring(up, "y", 1), ring(far, "y", 2), ring(low, "y", -1)])
    grad = jnp.stack([scattered(near, ("y", "zl")), scattered(others, ("x", "zl"))])

    grads = lax.all_to_all(
        jnp.broadcast_to(grad[None], (8, 2, 256, 128)), ("y", "zh"), 0, 0, tiled=True
    )
    mine, other = left_product(core, g_inverse, grads)
    left = (mine + swap(other)).astype(BF)
    mine = lax.all_to_all(
        jnp.broadcast_to(left[None], (8, 256, 128)), ("x", "zl"), 0, 0, tiled=True
    ).transpose(1, 0, 2).reshape(256, 1024)
    other = swap(mine)
    both = jnp.where(c == 0, jnp.concatenate([mine, other]), jnp.concatenate([other, mine]))
    return jnp.dot(both, a_inverse, preferred_element_type=F32)


def solution(mesh):
    wide = Mesh(mesh.devices.reshape(SIZES), AXES)
    rows, dev = P(AXES, None), P(("y", "zh"), None)
    return jax.shard_map(
        shards,
        mesh=wide,
        in_specs=(rows, rows, rows, dev, rows, P(), dev),
        out_specs=dev,
        check_vma=False,
    )
```

time: 1160 us -> 165 us (0.14)
  waiting for transfers between devices: 1100 us -> 25.9 us
  Pallas kernels: 0 us -> 53.7 us
  starting transfers between devices: 0.08 us -> 37.6 us
  blocking collectives: 0 us -> 29 us
  matrix products: 31.2 us -> 2.59 us
  between operations: 13.1 us -> 0.16 us
    reduce_scatter x1 -> x0, waiting for transfers between devices: 671 us -> none  [shards(): lax.psum_scatter(rounded.astype(jnp.float32), ('grp', 'dev'), scatter_dim...]
    all_gather x2 -> x0, waiting for transfers between devices: 429 us -> none  [the longest x1 315 us: shards(): lax.all_gather(right, ('grp', 'dev'), axis=0, tiled=True)]
    pallas_call x0 -> x6, Pallas kernels: none -> 53.7 us  [the longest x3 35.4 us: terms(): pl.pallas_call(functools.partial(term_kernel, n, by_columns), grid_spec=p...]
    ppermute x0 -> x19, starting transfers between devices: none -> 30.6 us  [the longest x11 14 us: ring(): return lax.ppermute(a, axis, [(i, (i + step) % 4) for i in range(4)])]
    all_to_all x0 -> x2, blocking collectives: none -> 29 us  [the longest x1 17.3 us: shards(): lax.all_to_all(jnp.broadcast_to(grad[None], (8, 2, 256, 128)), ('y', 'zh'...]
    dot_general x3 -> x1, matrix products: 31.2 us -> 2.59 us  [shards(): return jnp.dot(both, a_inverse, preferred_element_type=F32)]
    ppermute x0 -> x19, waiting for transfers between devices: none -> 16.6 us  [the longest x11 12.7 us: ring(): return lax.ppermute(a, axis, [(i, (i + step) % 4) for i in range(4)])]
  transfers between devices with their start and end apart: 3 -> 21, of which waited for: 3 -> 9; matrix products, arithmetic and copies ran while one was open for 0% -> 8% of each run, Pallas kernels for 0% -> 30%
where the time goes in v1:
time: 165 us; the launch traced here: 164 us
  Pallas kernels  53.7 us (33%)
  starting transfers between devices  37.6 us (23%)
  blocking collectives  29 us (18%)
  waiting for transfers between devices  25.9 us (16%)
  local copies, waits for them, and re-layouts  8.96 us (5%)
  other arithmetic  5.81 us (4%)
  matrix products  2.59 us (2%)
    pallas_call x3, Pallas kernels, terms(): pl.pallas_call(functools.partial(term_kernel, n, by_columns), grid_spec=p...  35.4 us
    all_to_all x1, blocking collectives, shards(): lax.all_to_all(jnp.broadcast_to(grad[None], (8, 2, 256, 128)), ('y', 'zh'...  17.3 us
    ppermute x11, starting transfers between devices, ring(): return lax.ppermute(a, axis, [(i, (i + step) % 4) for i in range(4)])  14 us
    pallas_call x2, Pallas kernels, slopes(): pl.pallas_call(slope_kernel, grid_spec=pltpu.PrefetchScalarGridSpec(num_s...  13.9 us
    ppermute x6, starting transfers between devices, swap(): return lax.ppermute(a, 'c', [(0, 1), (1, 0)])  12.8 us
    ppermute x11, waiting for transfers between devices, ring(): return lax.ppermute(a, axis, [(i, (i + step) % 4) for i in range(4)])  12.7 us
    all_to_all x1, blocking collectives, shards(): lax.all_to_all(jnp.broadcast_to(left[None], (8, 256, 128)), ('x', 'zl'),...  11.7 us
    all_to_all x2, waiting for transfers between devices, scattered(): return added(lax.all_to_all(a.reshape(8, 256, 128), axes, 0, 0, tiled=True))  9.23 us
  transfers between devices with their start and end apart: 21, of which 9 were waited for; matrix products, arithmetic and copies ran while one was open for 8% of the time, Pallas kernels for 30%

profile of v1, /device:TPU:1, one launch (start us, length us, event | category | flops | bytes accessed | tf_op | source)
XLA Modules:
  0.0 163.7 jit_solution(8470307780902066226)
XLA Ops:
  0.0 1.4 collective-permute-start.2
  1.4 1.1 constant_dynamic-slice_fusion.1.refs_8_
  2.5 0.0 copy-start.2
  2.5 2.9 %collective-permute-start = (bf16[256,1024]{1,0:T(8,128)(2,1)S(1)}, bf16[256,1024]{1,0:T(8,128)(2,1)S(1)}, u32[]{:S(2)}, u32[]{:S(2)}) collective-permute-start(bf16[256,1024]{1,0:T(8,128)(2,1)S(1)} %constant_dynamic-slice_fusion.1.refs_8_), channel_id=1, source_target_pairs={{0,6},{2,0},{4,2},{6,4},{1,7},{3,1},{5,3},{7,5},{8,14},{10,8},{12,... | collective-permute-start | bytes 1572872 | tf_op jit(solution)/shard_map/ppermute | solution.py:157
  5.4 0.0 collective-permute-start.1
  5.4 4.7 %constant_dynamic-slice_fusion = bf16[8,1,256,1024]{3,2,1,0:T(8,128)(2,1)} fusion(bf16[8,2,256,1024]{3,2,1,0:T(8,128)(2,1)} %bitcast.23, s32[]{:T(128)S(6)} %select_n.17), kind=kLoop, calls=%fused_computation.14 | loop fusion | bytes 8388612 | tf_op jit(solution)/shard_map/jit(dynamic_index_in_dim)/dynamic_slice | solution.py:161
  10.1 6.5 %collective-permute-done.refs_9_ = bf16[256,1024]{1,0:T(8,128)(2,1)S(1)} collective-permute-done((bf16[256,1024]{1,0:T(8,128)(2,1)S(1)}, bf16[256,1024]{1,0:T(8,128)(2,1)S(1)}, u32[]{:S(2)}, u32[]{:S(2)}) %collective-permute-start) | collective-permute-done | bytes 524320 | tf_op jit(solution)/shard_map/ppermute | solution.py:157
  16.6 3.2 %collective-permute-done.1.refs_10_ = bf16[256,1024]{1,0:T(8,128)(2,1)} collective-permute-done((bf16[256,1024]{1,0:T(8,128)(2,1)S(1)}, bf16[256,1024]{1,0:T(8,128)(2,1)}, u32[]{:S(2)}, u32[]{:S(2)}) %collective-permute-start.1) | collective-permute-done | bytes 524320 | tf_op jit(solution)/shard_map/ppermute | solution.py:157
  19.8 0.0 collective-permute-done.2.pre
  19.8 1.3 collective-permute-start.5
  21.1 0.0 collective-permute-start.6
  21.1 0.5 collective-permute-start.7
  21.6 0.0 collective-permute-start.3
  21.6 3.8 %collective-permute-start.4 = (bf16[256,1024]{1,0:T(8,128)(2,1)S(1)}, bf16[256,1024]{1,0:T(8,128)(2,1)S(1)}, u32[]{:S(2)}, u32[]{:S(2)}) collective-permute-start(bf16[256,1024]{1,0:T(8,128)(2,1)S(1)} %constant_dynamic-slice_fusion.1.refs_8_), channel_id=1, source_target_pairs={{0,65},{1,64},{64,1},{65,0},{2,67},{3,66},{66,3},{67,2},{4,69},{5,... | collective-permute-start | bytes 1572872 | tf_op jit(solution)/shard_map/ppermute | solution.py:154
  25.4 0.7 stack.77.place
  26.1 0.6 stack.74.place
  26.7 0.6 stack.71.place
  27.3 7.0 %shard_map.73.refs_4_ = bf16[2048,576]{1,0:T(8,128)(2,1)} custom-call(s32[1]{0:T(128)} %bitcast.core, bf16[576,4096]{1,0:T(8,128)(2,1)} %pre), custom_call_target="tpu_custom_call" | custom-call | flops 70778880 | bytes 5242880 | tf_op jit(solution)/shard_map/pallas_call | solution.py:28
  34.3 7.0 %shard_map.74.refs_5_ = bf16[2048,576]{1,0:T(8,128)(2,1)} custom-call(s32[1]{0:T(128)} %bitcast.core, bf16[576,4096]{1,0:T(8,128)(2,1)} %collective-permute-done.2.pre), custom_call_target="tpu_custom_call" | custom-call | flops 70778880 | bytes 5242880 | tf_op jit(solution)/shard_map/pallas_call | solution.py:28
  41.2 0.0 collective-permute-done.3.refs_11_
  41.2 0.0 collective-permute-done.4.refs_9_
  41.2 0.0 collective-permute-done.6.refs_1_
  41.2 0.0 collective-permute-done.7.refs_3_
  41.3 0.0 collective-permute-done.5.refs_7_
  41.3 1.2 collective-permute-start.8
  42.4 0.4 collective-permute-start.9
  42.8 0.0 collective-permute-start.10
  42.8 12.9 %shard_map.75 = (bf16[4,2,256,128]{3,2,1,0:T(8,128)(2,1)}, bf16[4,2,256,128]{3,2,1,0:T(8,128)(2,1)}, bf16[4,2,256,128]{3,2,1,0:T(8,128)(2,1)}, bf16[4,2,256,128]{3,2,1,0:T(8,128)(2,1)}) custom-call(s32[10]{0:T(128)} %stack.71.place, bf16[576,1024]{1,0:T(8,128)(2,1)} %refs_0_.2, bf16[576,1024]{1,0:T(8,128)(2,1)} %collective-permute-done.6.refs_1_, ...), custom_call_target="tpu_custom_call" | custom-call | flops 19327352832 | bytes 12582912 | tf_op jit(solution)/shard_map/pallas_call | solution.py:90
  55.7 1.2 collective-permute-done.10.refs_8_
  56.9 0.0 copy-start.5
  56.9 0.8 copy-done.5
  57.8 1.2 collective-permute-start.11
  59.0 2.5 %collective-permute-start.12 = (bf16[4,2,256,128]{3,2,1,0:T(8,128)(2,1)}, bf16[4,2,256,128]{3,2,1,0:T(8,128)(2,1)}, u32[]{:S(2)}, u32[]{:S(2)}) collective-permute-start(bf16[4,2,256,128]{3,2,1,0:T(8,128)(2,1)} %get-tuple-element.62), channel_id=1, source_target_pairs={{0,32},{16,48},{32,0},{48,16},{1,33},{17,49},{33,1},{49,17},{2,34}... | collective-permute-start | bytes 1572872 | tf_op jit(solution)/shard_map/ppermute | solution.py:157
  61.4 1.2 collective-permute-start.13
  62.6 11.2 %shard_map.77 = (bf16[8,256,128]{2,1,0:T(8,128)(2,1)}, bf16[8,256,128]{2,1,0:T(8,128)(2,1)}) custom-call(s32[6]{0:T(128)} %stack.77.place, bf16[576,1024]{1,0:T(8,128)(2,1)} %refs_0_.2, bf16[576,1024]{1,0:T(8,128)(2,1)} %collective-permute-done.6.refs_1_, bf16[576,1024]{1,0:T(8,128)(2,1)} %refs_2_.2, bf16[576,1024]{1,0:T(8,128)(2,1)} %collective-permute-done.7.refs_3_, ...), custom_call_target="tpu_custom_call" | custom-call | flops 9663676416 | bytes 6291456 | tf_op jit(solution)/shard_map/pallas_call | solution.py:90
  73.8 1.2 collective-permute-start.14
  75.0 2.0 %collective-permute-start.15 = (bf16[8,256,128]{2,1,0:T(8,128)(2,1)}, bf16[8,256,128]{2,1,0:T(8,128)(2,1)}, u32[]{:S(2)}, u32[]{:S(2)}) collective-permute-start(bf16[8,256,128]{2,1,0:T(8,128)(2,1)} %get-tuple-element.69), channel_id=1, source_target_pairs={{0,4},{2,6},{4,0},{6,2},{1,5},{3,7},{5,1},{7,3},{8,12},{10,14},{12... | collective-permute-start | bytes 1572872 | tf_op jit(solution)/shard_map/ppermute | solution.py:157
  77.0 11.3 %shard_map.76 = (bf16[8,256,128]{2,1,0:T(8,128)(2,1)}, bf16[8,256,128]{2,1,0:T(8,128)(2,1)}) custom-call(s32[6]{0:T(128)} %stack.74.place, bf16[576,1024]{1,0:T(8,128)(2,1)} %refs_0_.2, bf16[576,1024]{1,0:T(8,128)(2,1)} %collective-permute-done.6.refs_1_, bf16[576,1024]{1,0:T(8,128)(2,1)} %refs_2_.2, bf16[576,1024]{1,0:T(8,128)(2,1)} %collective-permute-done.7.refs_3_, ...), custom_call_target="tpu_custom_call" | custom-call | flops 9663676416 | bytes 6291456 | tf_op jit(solution)/shard_map/pallas_call | solution.py:90
  88.3 0.0 collective-permute-done.11
  88.3 1.5 collective-permute-start.16
  89.8 0.0 collective-permute-done.13
  89.8 2.3 %add_convert_fusion.1 = bf16[4,2,256,128]{3,2,1,0:T(8,128)(2,1)} fusion(bf16[4,2,256,128]{3,2,1,0:T(8,128)(2,1)} %collective-permute-done.13, bf16[4,2,256,128]{3,2,1,0:T(8,128)(2,1)} %collective-permute-done.12, bf16[4,2,256,128]{3,2,1,0:T(8,128)(2,1)S(1)} %collective-permute-done.11, bf16[4,2,256,128]{3,2,1,0:T(8,128)(2,1)S(1)} %copy-done.1), kind=kLoop, calls=%fused_computation.8 | loop fusion | flops 2097152 | bytes 2621440 | tf_op jit(solution)/shard_map/convert_element_type | solution.py:183
  92.1 3.5 %all-to-all-start = ((bf16[8,256,128]{2,1,0:T(8,128)(2,1)}), bf16[8,256,128]{2,1,0:T(8,128)(2,1)S(1)}, u32[]{:S(2)}, u32[]{:S(2)}) async-start(bf16[8,256,128]{2,1,0:T(8,128)(2,1)} %bitcast.12), calls=%async_computation | async-start | bytes 1048576 | tf_op jit(solution)/shard_map/all_to_all | solution.py:186
  95.6 0.0 collective-permute-done.14
  95.6 2.0 %collective-permute-done.15 = bf16[8,256,128]{2,1,0:T(8,128)(2,1)} collective-permute-done((bf16[8,256,128]{2,1,0:T(8,128)(2,1)}, bf16[8,256,128]{2,1,0:T(8,128)(2,1)}, u32[]{:S(2)}, u32[]{:S(2)}) %collective-permute-start.15) | collective-permute-done | bytes 524320 | tf_op jit(solution)/shard_map/ppermute | solution.py:157
  97.6 1.0 collective-permute-done.16
  98.6 2.4 %add_convert_fusion = bf16[8,256,128]{2,1,0:T(8,128)(2,1)} fusion(bf16[8,256,128]{2,1,0:T(8,128)(2,1)} %collective-permute-done.16, bf16[8,256,128]{2,1,0:T(8,128)(2,1)} %collective-permute-done.15, bf16[8,256,128]{2,1,0:T(8,128)(2,1)S(1)} %collective-permute-done.14, bf16[8,256,128]{2,1,0:T(8,128)(2,1)} %get-tuple-element.65), kind=kLoop, calls=%fused_computation.7 | loop fusion | flops 2097152 | bytes 2621440 | tf_op jit(solution)/shard_map/convert_element_type | solution.py:183
  101.1 2.4 %all-to-all-done = bf16[8,256,128]{2,1,0:T(8,128)(2,1)S(1)} async-done(((bf16[8,256,128]{2,1,0:T(8,128)(2,1)}), bf16[8,256,128]{2,1,0:T(8,128)(2,1)S(1)}, u32[]{:S(2)}, u32[]{:S(2)}) %all-to-all-start) | async-done | bytes 524320 | tf_op jit(solution)/shard_map/all_to_all | solution.py:186
  103.4 3.5 %all-to-all-start.1 = ((bf16[8,256,128]{2,1,0:T(8,128)(2,1)}), bf16[8,256,128]{2,1,0:T(8,128)(2,1)S(1)}, u32[]{:S(2)}, u32[]{:S(2)}) async-start(bf16[8,256,128]{2,1,0:T(8,128)(2,1)} %add_convert_fusion), calls=%async_computation.1 | async-start | bytes 1048576 | tf_op jit(solution)/shard_map/all_to_all | solution.py:186
  106.9 0.1 add_convert_fusion.4
  107.0 6.9 %all-to-all-done.1 = bf16[8,256,128]{2,1,0:T(8,128)(2,1)S(1)} async-done(((bf16[8,256,128]{2,1,0:T(8,128)(2,1)}), bf16[8,256,128]{2,1,0:T(8,128)(2,1)S(1)}, u32[]{:S(2)}, u32[]{:S(2)}) %all-to-all-start.1) | async-done | bytes 524320 | tf_op jit(solution)/shard_map/all_to_all | solution.py:186
  113.9 0.1 add_convert_fusion.3
  114.0 0.2 broadcast_in_dim.4
  114.2 17.3 %all_to_all.20.grads = bf16[8,2,256,128]{3,2,1,0:T(8,128)(2,1)} all-to-all(bf16[8,2,256,128]{3,2,1,0:T(8,128)(2,1)S(1)} %broadcast_in_dim.4), channel_id=1, replica_groups=mesh['zl'=2,'x'=4,'c'=2,'y'=4,'zh'=2] {'y','zh'}, dimensions={0} | all-to-all | bytes 2097152 | tf_op jit(solution)/shard_map/all_to_all | solution.py:196
  131.5 4.4 %shard_map.78 = (f32[256,128]{1,0:T(8,128)}, f32[256,128]{1,0:T(8,128)}) custom-call(s32[1]{0:T(128)} %bitcast.core, bf16[512,4096]{1,0:T(8,128)(2,1)} %g.1, bf16[8,2,256,128]{3,2,1,0:T(8,128)(2,1)} %all_to_all.20.grads), custom_call_target="tpu_custom_call" | custom-call | flops 268435456 | bytes 5242880 | tf_op jit(solution)/shard_map/pallas_call | solution.py:126
  135.9 8.1 %collective-permute-start.17 = (f32[256,128]{1,0:T(8,128)}, f32[256,128]{1,0:T(8,128)S(1)}, u32[]{:S(2)}, u32[]{:S(2)}) collective-permute-start(f32[256,128]{1,0:T(8,128)} %get-tuple-element.72), channel_id=1, source_target_pairs={{0,8},{8,0},{1,9},{9,1},{2,10},{10,2},{3,11},{11,3},{4,12},{12,4},... | collective-permute-start | bytes 393224 | tf_op jit(solution)/shard_map/ppermute | solution.py:151
  144.0 1.2 collective-permute-done.17
  145.2 0.9 add_convert_fusion.2
  146.1 0.1 broadcast_in_dim.5
  146.2 11.7 %all_to_all.21 = bf16[8,256,128]{2,1,0:T(8,128)(2,1)S(1)} all-to-all(bf16[8,256,128]{2,1,0:T(8,128)(2,1)S(1)} %broadcast_in_dim.5), channel_id=1, replica_groups=mesh['zl'=2,'x'=4,'c'=2,'y'=4,'zh'=2] {'x','zl'}, dimensions={0} | all-to-all | bytes 1048576 | tf_op jit(solution)/shard_map/all_to_all | solution.py:201
  157.9 0.2 copy.11
  158.1 1.5 collective-permute-start.18
  159.6 1.5 collective-permute-done.18
  161.1 2.6 %fusion = f32[512,1024]{1,0:T(8,128)} fusion(bf16[1024,1024]{1,0:T(8,128)(2,1)S(1)} %copy-done, bf16[256,1024]{0,1:T(8,128)(2,1)S(1)} %collective-permute-done.18, bf16[256,1024]{0,1:T(8,128)(2,1)S(1)} %bitcast.25, pred[]{:T(512)S(6)} %eq.3), kind=kOutput, calls=%fused_computation.1 | convolution fusion | flops 1078460416 | bytes 5242881 | tf_op jit(solution)/shard_map/dot_general | solution.py:206
  (15 shorter events, 0.0 us)
Async XLA Ops:
  0.0 161.1 %copy-start = (bf16[1024,1024]{1,0:T(8,128)(2,1)S(1)}, bf16[1024,1024]{1,0:T(8,128)(2,1)}, u32[]{:S(2)}) copy-start(bf16[1024,1024]{1,0:T(8,128)(2,1)} %param.12) | copy-start | bytes 6291460
  0.0 19.8 %collective-permute-start.2 = (bf16[576,4096]{1,0:T(8,128)(2,1)}, bf16[576,4096]{1,0:T(8,128)(2,1)}, u32[]{:S(2)}, u32[]{:S(2)}) collective-permute-start(bf16[576,4096]{1,0:T(8,128)(2,1)} %pre), channel_id=1, source_target_pairs={{0,8},{8,0},{1,9},{9,1},{2,10},{10,2},{3,11},{11,3},{4,12},{12,4},... | collective-permute-start | bytes 14155784 | tf_op jit(solution)/shard_map/ppermute | solution.py:151
  2.5 19.1 %copy-start.2 = (bf16[256,1024]{1,0:T(8,128)(2,1)}, bf16[256,1024]{1,0:T(8,128)(2,1)S(1)}, u32[]{:S(2)}) copy-start(bf16[256,1024]{1,0:T(8,128)(2,1)S(1)} %constant_dynamic-slice_fusion.1.refs_8_) | copy-start | bytes 1572868
  2.5 14.1 %collective-permute-start = (bf16[256,1024]{1,0:T(8,128)(2,1)S(1)}, bf16[256,1024]{1,0:T(8,128)(2,1)S(1)}, u32[]{:S(2)}, u32[]{:S(2)}) collective-permute-start(bf16[256,1024]{1,0:T(8,128)(2,1)S(1)} %constant_dynamic-slice_fusion.1.refs_8_), channel_id=1, source_target_pairs={{0,6},{2,0},{4,2},{6,4},{1,7},{3,1},{5,3},{7,5},{8,14},{10,8},{12,... | collective-permute-start | bytes 1572872 | tf_op jit(solution)/shard_map/ppermute | solution.py:157
  5.4 14.4 %collective-permute-start.1 = (bf16[256,1024]{1,0:T(8,128)(2,1)S(1)}, bf16[256,1024]{1,0:T(8,128)(2,1)}, u32[]{:S(2)}, u32[]{:S(2)}) collective-permute-start(bf16[256,1024]{1,0:T(8,128)(2,1)S(1)} %constant_dynamic-slice_fusion.1.refs_8_), channel_id=1, source_target_pairs={{0,2},{2,4},{4,6},{6,0},{1,3},{3,5},{5,7},{7,1},{8,10},{10,12},{12... | collective-permute-start | bytes 1572872 | tf_op jit(solution)/shard_map/ppermute | solution.py:157
  16.6 5.0 %copy-start.4 = (bf16[256,1024]{1,0:T(8,128)(2,1)}, bf16[256,1024]{1,0:T(8,128)(2,1)S(1)}, u32[]{:S(2)}) copy-start(bf16[256,1024]{1,0:T(8,128)(2,1)S(1)} %collective-permute-done.refs_9_) | copy-start | bytes 1572868
  19.8 21.5 %collective-permute-start.5 = (bf16[2048,1024]{1,0:T(8,128)(2,1)}, bf16[2048,1024]{1,0:T(8,128)(2,1)}, u32[]{:S(2)}, u32[]{:S(2)}) collective-permute-start(bf16[2048,1024]{1,0:T(8,128)(2,1)} %bitcast.11), channel_id=1, source_target_pairs={{0,8},{8,0},{1,9},{9,1},{2,10},{10,2},{3,11},{11,3},{4,12},{12,4},... | collective-permute-start | bytes 12582920 | tf_op jit(solution)/shard_map/ppermute | solution.py:151
  21.1 20.2 %collective-permute-start.6 = (bf16[576,1024]{1,0:T(8,128)(2,1)}, bf16[576,1024]{1,0:T(8,128)(2,1)}, u32[]{:S(2)}, u32[]{:S(2)}) collective-permute-start(bf16[576,1024]{1,0:T(8,128)(2,1)} %refs_0_.2), channel_id=1, source_target_pairs={{0,8},{8,0},{1,9},{9,1},{2,10},{10,2},{3,11},{11,3},{4,12},{12,4},... | collective-permute-start | bytes 3538952 | tf_op jit(solution)/shard_map/ppermute | solution.py:151
  21.1 20.2 %collective-permute-start.7 = (bf16[576,1024]{1,0:T(8,128)(2,1)}, bf16[576,1024]{1,0:T(8,128)(2,1)}, u32[]{:S(2)}, u32[]{:S(2)}) collective-permute-start(bf16[576,1024]{1,0:T(8,128)(2,1)} %refs_2_.2), channel_id=1, source_target_pairs={{0,8},{8,0},{1,9},{9,1},{2,10},{10,2},{3,11},{11,3},{4,12},{12,4},... | collective-permute-start | bytes 3538952 | tf_op jit(solution)/shard_map/ppermute | solution.py:151
  21.6 19.6 %collective-permute-start.3 = (bf16[256,1024]{1,0:T(8,128)(2,1)S(1)}, bf16[256,1024]{1,0:T(8,128)(2,1)}, u32[]{:S(2)}, u32[]{:S(2)}) collective-permute-start(bf16[256,1024]{1,0:T(8,128)(2,1)S(1)} %constant_dynamic-slice_fusion.1.refs_8_), channel_id=1, source_target_pairs={{0,4},{2,6},{4,0},{6,2},{1,5},{3,7},{5,1},{7,3},{8,12},{10,14},{12... | collective-permute-start | bytes 1572872 | tf_op jit(solution)/shard_map/ppermute | solution.py:157
  21.6 19.6 %collective-permute-start.4 = (bf16[256,1024]{1,0:T(8,128)(2,1)S(1)}, bf16[256,1024]{1,0:T(8,128)(2,1)S(1)}, u32[]{:S(2)}, u32[]{:S(2)}) collective-permute-start(bf16[256,1024]{1,0:T(8,128)(2,1)S(1)} %constant_dynamic-slice_fusion.1.refs_8_), channel_id=1, source_target_pairs={{0,65},{1,64},{64,1},{65,0},{2,67},{3,66},{66,3},{67,2},{4,69},{5,... | collective-permute-start | bytes 1572872 | tf_op jit(solution)/shard_map/ppermute | solution.py:154
  41.2 14.5 %copy-start.3 = (bf16[256,1024]{1,0:T(8,128)(2,1)}, bf16[256,1024]{1,0:T(8,128)(2,1)S(1)}, u32[]{:S(2)}) copy-start(bf16[256,1024]{1,0:T(8,128)(2,1)S(1)} %collective-permute-done.4.refs_9_) | copy-start | bytes 1572868
  41.3 15.7 %collective-permute-start.8 = (bf16[256,1024]{1,0:T(8,128)(2,1)S(1)}, bf16[256,1024]{1,0:T(8,128)(2,1)S(1)}, u32[]{:S(2)}, u32[]{:S(2)}) collective-permute-start(bf16[256,1024]{1,0:T(8,128)(2,1)S(1)} %collective-permute-done.4.refs_9_), channel_id=1, source_target_pairs={{0,6},{2,0},{4,2},{6,4},{1,7},{3,1},{5,3},{7,5},{8,14},{10,8},{12,... | collective-permute-start | bytes 1572872 | tf_op jit(solution)/shard_map/ppermute | solution.py:157
  42.4 14.5 %collective-permute-start.9 = (bf16[256,1024]{1,0:T(8,128)(2,1)S(1)}, bf16[256,1024]{1,0:T(8,128)(2,1)S(1)}, u32[]{:S(2)}, u32[]{:S(2)}) collective-permute-start(bf16[256,1024]{1,0:T(8,128)(2,1)S(1)} %collective-permute-done.4.refs_9_), channel_id=1, source_target_pairs={{0,2},{2,4},{4,6},{6,0},{1,3},{3,5},{5,7},{7,1},{8,10},{10,12},{12... | collective-permute-start | bytes 1572872 | tf_op jit(solution)/shard_map/ppermute | solution.py:157
  42.8 14.1 %collective-permute-start.10 = (bf16[256,1024]{1,0:T(8,128)(2,1)}, bf16[256,1024]{1,0:T(8,128)(2,1)}, u32[]{:S(2)}, u32[]{:S(2)}) collective-permute-start(bf16[256,1024]{1,0:T(8,128)(2,1)} %collective-permute-done.3.refs_11_), channel_id=1, source_target_pairs={{0,65},{1,64},{64,1},{65,0},{2,67},{3,66},{66,3},{67,2},{4,69},{5,... | collective-permute-start | bytes 1572872 | tf_op jit(solution)/shard_map/ppermute | solution.py:154
  56.9 5.7 %copy-start.6 = (bf16[256,1024]{1,0:T(8,128)(2,1)}, bf16[256,1024]{1,0:T(8,128)(2,1)S(1)}, u32[]{:S(2)}) copy-start(bf16[256,1024]{1,0:T(8,128)(2,1)S(1)} %collective-permute-done.8.refs_9_) | copy-start | bytes 1572868
  56.9 0.8 copy-start.5
  57.8 30.5 %collective-permute-start.11 = (bf16[4,2,256,128]{3,2,1,0:T(8,128)(2,1)}, bf16[4,2,256,128]{3,2,1,0:T(8,128)(2,1)S(1)}, u32[]{:S(2)}, u32[]{:S(2)}) collective-permute-start(bf16[4,2,256,128]{3,2,1,0:T(8,128)(2,1)} %get-tuple-element.61), channel_id=1, source_target_pairs={{0,16},{16,32},{32,48},{48,0},{1,17},{17,33},{33,49},{49,1},{2,18}... | collective-permute-start | bytes 1572872 | tf_op jit(solution)/shard_map/ppermute | solution.py:157
  59.0 30.9 %collective-permute-start.12 = (bf16[4,2,256,128]{3,2,1,0:T(8,128)(2,1)}, bf16[4,2,256,128]{3,2,1,0:T(8,128)(2,1)}, u32[]{:S(2)}, u32[]{:S(2)}) collective-permute-start(bf16[4,2,256,128]{3,2,1,0:T(8,128)(2,1)} %get-tuple-element.62), channel_id=1, source_target_pairs={{0,32},{16,48},{32,0},{48,16},{1,33},{17,49},{33,1},{49,17},{2,34}... | collective-permute-start | bytes 1572872 | tf_op jit(solution)/shard_map/ppermute | solution.py:157
  61.4 28.4 %collective-permute-start.13 = (bf16[4,2,256,128]{3,2,1,0:T(8,128)(2,1)}, bf16[4,2,256,128]{3,2,1,0:T(8,128)(2,1)}, u32[]{:S(2)}, u32[]{:S(2)}) collective-permute-start(bf16[4,2,256,128]{3,2,1,0:T(8,128)(2,1)} %get-tuple-element.63), channel_id=1, source_target_pairs={{0,48},{16,0},{32,16},{48,32},{1,49},{17,1},{33,17},{49,33},{2,50}... | collective-permute-start | bytes 1572872 | tf_op jit(solution)/shard_map/ppermute | solution.py:157
  73.8 21.8 %collective-permute-start.14 = (bf16[8,256,128]{2,1,0:T(8,128)(2,1)}, bf16[8,256,128]{2,1,0:T(8,128)(2,1)S(1)}, u32[]{:S(2)}, u32[]{:S(2)}) collective-permute-start(bf16[8,256,128]{2,1,0:T(8,128)(2,1)} %get-tuple-element.68), channel_id=1, source_target_pairs={{0,2},{2,4},{4,6},{6,0},{1,3},{3,5},{5,7},{7,1},{8,10},{10,12},{12... | collective-permute-start | bytes 1572872 | tf_op jit(solution)/shard_map/ppermute | solution.py:157
  75.0 14.8 %copy-start.1 = (bf16[4,2,256,128]{3,2,1,0:T(8,128)(2,1)S(1)}, bf16[4,2,256,128]{3,2,1,0:T(8,128)(2,1)}, u32[]{:S(2)}) copy-start(bf16[4,2,256,128]{3,2,1,0:T(8,128)(2,1)} %get-tuple-element.60) | copy-start | bytes 1572868
  75.0 22.6 %collective-permute-start.15 = (bf16[8,256,128]{2,1,0:T(8,128)(2,1)}, bf16[8,256,128]{2,1,0:T(8,128)(2,1)}, u32[]{:S(2)}, u32[]{:S(2)}) collective-permute-start(bf16[8,256,128]{2,1,0:T(8,128)(2,1)} %get-tuple-element.69), channel_id=1, source_target_pairs={{0,4},{2,6},{4,0},{6,2},{1,5},{3,7},{5,1},{7,3},{8,12},{10,14},{12... | collective-permute-start | bytes 1572872 | tf_op jit(solution)/shard_map/ppermute | solution.py:157
  88.3 10.3 %collective-permute-start.16 = (bf16[8,256,128]{2,1,0:T(8,128)(2,1)}, bf16[8,256,128]{2,1,0:T(8,128)(2,1)}, u32[]{:S(2)}, u32[]{:S(2)}) collective-permute-start(bf16[8,256,128]{2,1,0:T(8,128)(2,1)} %get-tuple-element.70), channel_id=1, source_target_pairs={{0,6},{2,0},{4,2},{6,4},{1,7},{3,1},{5,3},{7,5},{8,14},{10,8},{12,... | collective-permute-start | bytes 1572872 | tf_op jit(solution)/shard_map/ppermute | solution.py:157
  92.1 11.3 %all-to-all-start = ((bf16[8,256,128]{2,1,0:T(8,128)(2,1)}), bf16[8,256,128]{2,1,0:T(8,128)(2,1)S(1)}, u32[]{:S(2)}, u32[]{:S(2)}) async-start(bf16[8,256,128]{2,1,0:T(8,128)(2,1)} %bitcast.12), calls=%async_computation | async-start | bytes 1048576 | tf_op jit(solution)/shard_map/all_to_all | solution.py:186
  103.4 10.4 %all-to-all-start.1 = ((bf16[8,256,128]{2,1,0:T(8,128)(2,1)}), bf16[8,256,128]{2,1,0:T(8,128)(2,1)S(1)}, u32[]{:S(2)}, u32[]{:S(2)}) async-start(bf16[8,256,128]{2,1,0:T(8,128)(2,1)} %add_convert_fusion), calls=%async_computation.1 | async-start | bytes 1048576 | tf_op jit(solution)/shard_map/all_to_all | solution.py:186
  135.9 9.3 %collective-permute-start.17 = (f32[256,128]{1,0:T(8,128)}, f32[256,128]{1,0:T(8,128)S(1)}, u32[]{:S(2)}, u32[]{:S(2)}) collective-permute-start(f32[256,128]{1,0:T(8,128)} %get-tuple-element.72), channel_id=1, source_target_pairs={{0,8},{8,0},{1,9},{9,1},{2,10},{10,2},{3,11},{11,3},{4,12},{12,4},... | collective-permute-start | bytes 393224 | tf_op jit(solution)/shard_map/ppermute | solution.py:151
  158.1 3.0 %collective-permute-start.18 = (bf16[256,1024]{0,1:T(8,128)(2,1)S(1)}, bf16[256,1024]{0,1:T(8,128)(2,1)S(1)}, u32[]{:S(2)}, u32[]{:S(2)}) collective-permute-start(bf16[256,1024]{0,1:T(8,128)(2,1)S(1)} %bitcast.24), channel_id=1, source_target_pairs={{0,8},{8,0},{1,9},{9,1},{2,10},{10,2},{3,11},{11,3},{4,12},{12,4},... | collective-permute-start | bytes 1572872 | tf_op jit(solution)/shard_map/ppermute | solution.py:151

commit v2 on v0

v2 whole, which is shorter than its diff:
```python
import functools
import math

import jax
import jax.numpy as jnp
from jax import lax
from jax.experimental import pallas as pl
from jax.experimental.pallas import tpu as pltpu
from jax.sharding import Mesh, PartitionSpec as P

AXES = ("zl", "x", "c", "y", "zh")
SIZES = (2, 4, 2, 4, 2)
BF = jnp.bfloat16
F32 = jnp.float32


def gelu_slope(value):
    cdf = 0.5 * (1.0 + lax.erf(value * (1.0 / math.sqrt(2.0))))
    density = jnp.exp(-0.5 * value * value) * (1.0 / math.sqrt(2.0 * math.pi))
    return cdf + value * density


def prepare_kernel(here, pre, cot, *refs):
    with_ef = len(refs) == 11
    ef, (slope, cot_t), carried = refs[0], refs[with_ef : with_ef + 2], refs[3]
    pre_v, cot_v, ef_v, slope_v, cot_tv, sem, out_sem = refs[-7:]
    c = here[0]

    def start(source, target, semaphore):
        copy = pltpu.make_async_copy(source, target, semaphore)
        copy.start()
        return copy

    reads = [
        start(
            pre.at[:, pl.ds(pl.multiple_of((2 * i + c) * 256, 256), 256)], pre_v.at[i], sem.at[i]
        )
        for i in range(8)
    ]
    reads.append(start(cot, cot_v, sem.at[8]))
    if with_ef:
        for i in range(8):
            rows = pl.ds(pl.multiple_of((2 * i + 1 - c) * 256, 256), 256)
            reads.append(start(ef.at[rows], ef_v.at[i], sem.at[9 + i]))
    writes = []

    def write(source, target):
        writes.append(start(source, target, out_sem.at[len(writes)]))

    for i in range(8):
        reads[i].wait()
        slope_v[i] = gelu_slope(pre_v[i].astype(F32)).astype(BF).T
        write(slope_v.at[i], slope.at[pl.ds(i * 256, 256)])
        if with_ef:
            reads[9 + i].wait()
            write(ef_v.at[i], carried.at[pl.ds(i * 256, 256)])
    reads[8].wait()
    cot_tv[...] = cot_v[...].T
    write(cot_tv, cot_t)
    for copy in writes:
        copy.wait()


def prepare(here, pre, cot, ef=None):
    out_shape = [
        jax.ShapeDtypeStruct((2048, 576), BF),
        jax.ShapeDtypeStruct((1024, 576), BF),
    ]
    args = [here, pre, cot]
    if ef is not None:
        args.append(ef)
        out_shape.append(jax.ShapeDtypeStruct((2048, 1024), BF))
    return pl.pallas_call(
        prepare_kernel,
        in_specs=[pl.BlockSpec(memory_space=pltpu.SMEM)]
        + [pl.BlockSpec(memory_space=pl.ANY)] * (len(args) - 1),
        out_specs=[pl.BlockSpec(memory_space=pl.ANY)] * len(out_shape),
        out_shape=out_shape,
        scratch_shapes=[
            pltpu.VMEM((8, 576, 256), BF),
            pltpu.VMEM((576, 1024), BF),
            pltpu.VMEM((8, 256, 1024), BF),
            pltpu.VMEM((8, 256, 576), BF),
            pltpu.VMEM((1024, 576), BF),
            pltpu.SemaphoreType.DMA((17,)),
            pltpu.SemaphoreType.DMA((17,)),
        ],
        compiler_params=pltpu.CompilerParams(vmem_limit_bytes=60 * 2**20),
        cost_estimate=pl.CostEstimate(
            flops=60 * 576 * 2048, bytes_accessed=5 * 2**20, transcendentals=2 * 576 * 2048
        ),
    )(*args)


def cut_kernel(upper, lower, upper_out, lower_out):
    upper_out[...] = upper[...]
    lower_out[...] = lower[...]


def cut(a, b):
    half = (128, 1024)
    return pl.pallas_call(
        cut_kernel,
        grid=(1,),
        in_specs=[pl.BlockSpec(half, lambda i: (0, 0)), pl.BlockSpec(half, lambda i: (1, 0))],
        out_specs=[pl.BlockSpec(half, lambda i: (0, 0))] * 2,
        out_shape=[jax.ShapeDtypeStruct(half, BF)] * 2,
    )(a, b)


def term_kernel(by_columns, part, here, *refs):
    n = len(part)
    cot, cot_o, inp, inp_o, slope, slope_o, ef, ef_o = refs[:8]
    n_out = 4 if by_columns else n
    ws, outs = refs[8 : 8 + n], refs[8 + n : 8 + n + n_out]
    w_v, cot_v, inp_v, slope_v, ef_v, out_v, sem, out_sem = refs[8 + n + n_out :]
    core, x, y, zh = (here[k] for k in range(4))
    blocks = [lax.rem(y + dy, 4) * 2 + (1 - zh if dz else zh) for dy, dz in part]

    def rows(ref, block):
        return ref.at[pl.ds(pl.multiple_of(block * 256, 256), 256)]

    reads = {}

    def read(name, source, target):
        reads[name] = pltpu.make_async_copy(source, target, sem.at[len(reads)])
        reads[name].start()

    for i in range(n):
        block = blocks[i]
        read(("w", i), ws[i], w_v.at[i])
        if i == 0:
            read("cot", cot, cot_v.at[0])
            read("cot_o", cot_o, cot_v.at[1])
        read(("slope", i), rows(slope, block), slope_v.at[i, 0])
        read(("slope_o", i), rows(slope_o, block), slope_v.at[i, 1])
        if i == 0:
            read("inp", inp, inp_v.at[0])
            read("inp_o", inp_o, inp_v.at[1])
        read(("ef", i), rows(ef, block * 2 + core), ef_v.at[i, 0])
        read(("ef_o", i), rows(ef_o, block), ef_v.at[i, 1])

    writes = []
    for i in range(n):
        reads["w", i].wait()
        hidden = []
        for k, suffix in enumerate(("", "_o")):
            if i == 0:
                reads["cot" + suffix].wait()
            grad_pre = jnp.dot(w_v[i], cot_v[k], preferred_element_type=F32)
            reads["slope" + suffix, i].wait()
            hidden.append((grad_pre * slope_v[i, k].astype(F32)).astype(BF))
        for k, suffix in enumerate(("", "_o")):
            if i == 0:
                reads["inp" + suffix].wait()
            reads["ef" + suffix, i].wait()
        for j in range(4):
            if by_columns:
                cols = pl.ds(pl.multiple_of(lax.rem(x + j, 4) * 256, 256), 256)
            else:
                cols = slice(j * 256, (j + 1) * 256)
            total = ef_v[i, 0, :, cols].astype(F32) + ef_v[i, 1, :, cols].astype(F32)
            for k in range(2):
                total += jnp.dot(hidden[k], inp_v[k, :, cols], preferred_element_type=F32)
            total = total.astype(BF)
            for k in range(2):
                out_v[i, 2 * j + k] = total[:, k * 128 : (k + 1) * 128]
            if by_columns:
                writes.append(
                    pltpu.make_async_copy(
                        out_v.at[i, pl.ds(2 * j, 2)], outs[j].at[lax.rem(y + part[i][0], 4)], out_sem.at[len(writes)]
                    )
                )
                writes[-1].start()
        if not by_columns:
            writes.append(pltpu.make_async_copy(out_v.at[i], outs[i], out_sem.at[i]))
            writes[-1].start()
    for write in writes:
        write.wait()


def terms(by_columns, part, here, cot, cot_o, inp, inp_o, slope, slope_o, ef, ef_o, ws):
    n = len(ws)
    if by_columns:
        out_shape = [jax.ShapeDtypeStruct((n, 2, 256, 128), BF)] * 4
    else:
        out_shape = [jax.ShapeDtypeStruct((8, 256, 128), BF)] * n
    return pl.pallas_call(
        functools.partial(term_kernel, by_columns, part),
        in_specs=[pl.BlockSpec(memory_space=pltpu.SMEM)]
        + [pl.BlockSpec(memory_space=pl.ANY)] * (8 + n),
        out_specs=[pl.BlockSpec(memory_space=pl.ANY)] * len(out_shape),
        out_shape=out_shape,
        scratch_shapes=[
            pltpu.VMEM((n, 256, 1024), BF),
            pltpu.VMEM((2, 1024, 576), BF),
            pltpu.VMEM((2, 576, 1024), BF),
            pltpu.VMEM((n, 2, 256, 576), BF),
            pltpu.VMEM((n, 2, 256, 1024), BF),
            pltpu.VMEM((n, 8, 256, 128), BF),
            pltpu.SemaphoreType.DMA((4 + 5 * n,)),
            pltpu.SemaphoreType.DMA((4 * n if by_columns else n,)),
        ],
        compiler_params=pltpu.CompilerParams(vmem_limit_bytes=60 * 2**20),
        cost_estimate=pl.CostEstimate(
            flops=16 * 1152 * 1024 * 256 * n, bytes_accessed=3 * n * 2**20, transcendentals=0
        ),
    )(here, cot, cot_o, inp, inp_o, slope, slope_o, ef, ef_o, *ws)


def left_kernel(here, g, *refs):
    grads, (mine, other), (g_v, grad_v, total, sem) = refs[:4], refs[4:6], refs[6:]
    c, _, y, zh = (here[k] for k in range(4))
    reads = []
    for i, dy in enumerate((0, 1, 3, 2)):
        for k in range(2):
            block = lax.rem(y + dy, 4) * 2 + (1 - zh if k else zh)
            cols = pl.ds(pl.multiple_of((2 * block + c) * 256, 256), 256)
            reads.append(pltpu.make_async_copy(g.at[:, cols], g_v.at[2 * i + k], sem.at[2 * i + k]))
            reads[-1].start()
    for i in range(4):
        reads.append(pltpu.make_async_copy(grads[i], grad_v.at[i], sem.at[8 + i]))
        reads[-1].start()
    product = 0.0
    for i in range(4):
        reads[8 + i].wait()
        for k in range(2):
            reads[2 * i + k].wait()
            product += jnp.dot(g_v[2 * i + k], grad_v[i, k], preferred_element_type=F32)
    total[...] = product
    mine[...] = total[pl.ds(pl.multiple_of(c * 256, 256), 256), :]
    other[...] = total[pl.ds(pl.multiple_of((1 - c) * 256, 256), 256), :]


def left_product(here, g, grads):
    whole = pl.BlockSpec(memory_space=pltpu.VMEM)
    return pl.pallas_call(
        left_kernel,
        in_specs=[pl.BlockSpec(memory_space=pltpu.SMEM)] + [pl.BlockSpec(memory_space=pl.ANY)] * 5,
        out_specs=[whole, whole],
        out_shape=[jax.ShapeDtypeStruct((256, 128), F32)] * 2,
        scratch_shapes=[
            pltpu.VMEM((8, 512, 256), BF),
            pltpu.VMEM((4, 2, 256, 128), BF),
            pltpu.VMEM((512, 128), F32),
            pltpu.SemaphoreType.DMA((12,)),
        ],
        cost_estimate=pl.CostEstimate(
            flops=2 * 512 * 2048 * 128, bytes_accessed=3 * 2**20, transcendentals=0
        ),
    )(here, g, *grads)


def shards(inputs, cotangent, pre_gelu, w_down, error_feedback, a_inverse, g_inverse):
    c, x, y, zh = (lax.axis_index(a) for a in ("c", "x", "y", "zh"))
    here = jnp.stack([c, x, y, zh]).astype(jnp.int32)

    def swap(a):
        return lax.ppermute(a, "c", [(0, 1), (1, 0)])

    def across_z(a):
        return lax.ppermute(a, ("zl", "zh"), [(i, 3 - i) for i in range(4)])

    def ring(a, axis, step):
        return lax.ppermute(a, axis, [(i, (i + step) % 4) for i in range(4)])

    w_own = lax.dynamic_slice(w_down, (c * 256, 0), (256, 1024))
    first = [ring(w_own, "y", -1), ring(w_own, "y", 1), across_z(w_own)]
    first += [swap(a) for a in (pre_gelu, cotangent)]
    slope, cot, carried = prepare(here, pre_gelu, cotangent, error_feedback)
    w_up, w_low, w_z, pre_o, cot_o, slope, cot, carried, inp = lax.optimization_barrier(
        (*first, slope, cot, carried, inputs)
    )
    upper, lower = cut(w_up, w_low)
    second = [ring(upper, "y", -1), ring(lower, "y", 1), swap(carried), swap(inp)]
    slope_o, cot_o = prepare(here, pre_o, cot_o)
    upper, lower, ef_o, inp_o, slope_o, cot_o, w_up, w_low, w_z = lax.optimization_barrier(
        (*second, slope_o, cot_o, w_up, w_low, w_z)
    )
    w_far = jnp.concatenate([upper, lower])
    third = [ring(w_z, "y", -1), ring(w_z, "y", 1), across_z(w_far)]

    def product(by_columns, part, ws):
        return terms(
            by_columns, part, here, cot, cot_o, inputs, inp_o,
            slope, slope_o, error_feedback, ef_o, ws,
        )

    def added(parts):
        return sum(p.astype(F32) for p in parts).astype(BF)

    def scattered(a, axes):
        return added(lax.all_to_all(a.reshape(8, 256, 128), axes, 0, 0, tiled=True))

    near = product(True, ((0, 0), (1, 0), (3, 0), (2, 0)), [w_own, w_up, w_low, w_far])
    near, third = lax.optimization_barrier((near, third))
    near = added([near[0]] + [ring(near[j], "x", j) for j in (1, 2, 3)])
    far, up, low = product(False, ((2, 1), (1, 1), (3, 1)), [third[2], third[0], third[1]])
    (own,) = product(False, ((0, 1),), [w_z])
    others = added([own, ring(up, "y", 1), ring(far, "y", 2), ring(low, "y", -1)])
    near, others = lax.optimization_barrier((scattered(near, ("y", "zl")), others))
    others = scattered(others, ("x", "zl"))
    theirs = lax.ppermute(jnp.stack([others, near]), "zh", [(0, 1), (1, 0)])
    grad = added([jnp.stack([near, others]), theirs])
    grads = [grad, ring(grad, "y", -1), ring(grad, "y", 1), ring(grad, "y", 2)]
    mine, other = left_product(here, g_inverse, grads)
    left = (mine + swap(other)).astype(BF)
    mine = lax.all_to_all(
        jnp.broadcast_to(left[None], (8, 256, 128)), ("x", "zl"), 0, 0, tiled=True
    ).transpose(1, 0, 2).reshape(256, 1024)
    other = swap(mine)
    both = jnp.where(c == 0, jnp.concatenate([mine, other]), jnp.concatenate([other, mine]))
    return jnp.dot(both, a_inverse, preferred_element_type=F32)


def solution(mesh):
    wide = Mesh(mesh.devices.reshape(SIZES), AXES)
    rows, dev = P(AXES, None), P(("y", "zh"), None)
    return jax.shard_map(
        shards,
        mesh=wide,
        in_specs=(rows, rows, rows, dev, rows, P(), dev),
        out_specs=dev,
        check_vma=False,
    )
```

time: 1160 us -> 159 us (0.14)
  waiting for transfers between devices: 1100 us -> 33.1 us
  Pallas kernels: 0 us -> 48.2 us
  starting transfers between devices: 0.08 us -> 41.8 us
  matrix products: 31.2 us -> 2.59 us
  blocking collectives: 0 us -> 21.3 us
  between operations: 13.1 us -> 0.25 us
    reduce_scatter x1 -> x0, waiting for transfers between devices: 671 us -> none  [shards(): lax.psum_scatter(rounded.astype(jnp.float32), ('grp', 'dev'), scatter_dim...]
    all_gather x2 -> x0, waiting for transfers between devices: 429 us -> none  [the longest x1 315 us: shards(): lax.all_gather(right, ('grp', 'dev'), axis=0, tiled=True)]
    pallas_call x0 -> x7, Pallas kernels: none -> 48.2 us  [the longest x3 28.8 us: terms(): pl.pallas_call(functools.partial(term_kernel, by_columns, part), in_specs...]
    ppermute x0 -> x24, starting transfers between devices: none -> 38.3 us  [the longest x15 19.7 us: ring(): return lax.ppermute(a, axis, [(i, (i + step) % 4) for i in range(4)])]
    ppermute x0 -> x24, waiting for transfers between devices: none -> 29.5 us  [the longest x15 20.7 us: ring(): return lax.ppermute(a, axis, [(i, (i + step) % 4) for i in range(4)])]
    dot_general x3 -> x1, matrix products: 31.2 us -> 2.59 us  [shards(): return jnp.dot(both, a_inverse, preferred_element_type=F32)]
    all_to_all x0 -> x2, blocking collectives: none -> 21.3 us  [the longest x1 11.2 us: shards(): lax.all_to_all(jnp.broadcast_to(left[None], (8, 256, 128)), ('x', 'zl'),...]
  transfers between devices with their start and end apart: 3 -> 25, of which waited for: 3 -> 12; matrix products, arithmetic and copies ran while one was open for 0% -> 4% of each run, Pallas kernels for 0% -> 28%
where the time goes in v2:
time: 159 us; the launch traced here: 158 us
  Pallas kernels  48.2 us (30%)
  starting transfers between devices  41.8 us (26%)
  waiting for transfers between devices  33.1 us (21%)
  blocking collectives  21.3 us (13%)
  other arithmetic  5.88 us (4%)
  local copies, waits for them, and re-layouts  5.08 us (3%)
  matrix products  2.59 us (2%)
    pallas_call x3, Pallas kernels, terms(): pl.pallas_call(functools.partial(term_kernel, by_columns, part), in_specs...  28.8 us
    ppermute x15, waiting for transfers between devices, ring(): return lax.ppermute(a, axis, [(i, (i + step) % 4) for i in range(4)])  20.7 us
    ppermute x15, starting transfers between devices, ring(): return lax.ppermute(a, axis, [(i, (i + step) % 4) for i in range(4)])  19.7 us
    pallas_call x2, Pallas kernels, prepare(): pl.pallas_call(prepare_kernel, in_specs=[pl.BlockSpec(memory_space=pltpu....  12.8 us
    all_to_all x1, blocking collectives, shards(): lax.all_to_all(jnp.broadcast_to(left[None], (8, 256, 128)), ('x', 'zl'),...  11.2 us
    ppermute x6, starting transfers between devices, swap(): return lax.ppermute(a, 'c', [(0, 1), (1, 0)])  11.2 us
    all_to_all x1, blocking collectives, scattered(): return added(lax.all_to_all(a.reshape(8, 256, 128), axes, 0, 0, tiled=True))  10.1 us
    ppermute x2, starting transfers between devices, across_z(): return lax.ppermute(a, ('zl', 'zh'), [(i, 3 - i) for i in range(4)])  6.66 us
  transfers between devices with their start and end apart: 25, of which 12 were waited for; matrix products, arithmetic and copies ran while one was open for 4% of the time, Pallas kernels for 28%

profile of v2, /device:TPU:1, one launch (start us, length us, event | category | flops | bytes accessed | tf_op | source)
XLA Modules:
  0.0 158.1 jit_solution(11266445194011248071)
XLA Ops:
  0.0 1.4 collective-permute-start.3
  1.4 0.0 collective-permute-start.4
  1.4 1.9 %constant_dynamic-slice_fusion.refs_8_ = bf16[256,1024]{1,0:T(8,128)(2,1)} fusion(bf16[512,1024]{1,0:T(8,128)(2,1)} %param.10, s32[]{:T(128)S(6)} %select_n.12), kind=kLoop, calls=%fused_computation.19 | loop fusion | bytes 1048580 | tf_op jit(solution)/shard_map/dynamic_slice | solution.py:267
  3.3 2.9 %collective-permute-start = (bf16[256,1024]{1,0:T(8,128)(2,1)}, bf16[256,1024]{1,0:T(8,128)(2,1)}, u32[]{:S(2)}, u32[]{:S(2)}) collective-permute-start(bf16[256,1024]{1,0:T(8,128)(2,1)} %constant_dynamic-slice_fusion.refs_8_), channel_id=1, source_target_pairs={{0,6},{2,0},{4,2},{6,4},{1,7},{3,1},{5,3},{7,5},{8,14},{10,8},{12,... | collective-permute-start | bytes 1572872 | tf_op jit(solution)/shard_map/ppermute | solution.py:265
  6.2 0.0 collective-permute-start.1
  6.2 3.8 %collective-permute-start.2 = (bf16[256,1024]{1,0:T(8,128)(2,1)}, bf16[256,1024]{1,0:T(8,128)(2,1)}, u32[]{:S(2)}, u32[]{:S(2)}) collective-permute-start(bf16[256,1024]{1,0:T(8,128)(2,1)} %constant_dynamic-slice_fusion.refs_8_), channel_id=1, source_target_pairs={{0,65},{1,64},{64,1},{65,0},{2,67},{3,66},{66,3},{67,2},{4,69},{5,... | collective-permute-start | bytes 1572872 | tf_op jit(solution)/shard_map/ppermute | solution.py:262
  10.0 0.7 pad_add_fusion.here
  10.6 6.9 %shard_map.73 = (bf16[2048,576]{1,0:T(8,128)(2,1)}, bf16[1024,576]{1,0:T(8,128)(2,1)}, bf16[2048,1024]{1,0:T(8,128)(2,1)}) custom-call(s32[4]{0:T(128)} %pad_add_fusion.here, bf16[576,4096]{1,0:T(8,128)(2,1)} %pre.1, bf16[576,1024]{1,0:T(8,128)(2,1)} %cot.1, bf16[4096,1024]{1,0:T(8,128)(2,1)} %refs_6_.5), custom_call_target="tpu_custom_call" | custom-call | flops 70778880 | bytes 5242880 | tf_op jit(solution)/shard_map/pallas_call | solution.py:73
  17.6 0.0 collective-permute-done.upper.refs_9_
  17.6 2.8 %collective-permute-done.1.lower.refs_10_ = bf16[256,1024]{1,0:T(8,128)(2,1)} collective-permute-done((bf16[256,1024]{1,0:T(8,128)(2,1)}, bf16[256,1024]{1,0:T(8,128)(2,1)}, u32[]{:S(2)}, u32[]{:S(2)}) %collective-permute-start.1) | collective-permute-done | bytes 524320 | tf_op jit(solution)/shard_map/ppermute | solution.py:265
  20.4 1.5 collective-permute-done.2.refs_8_
  21.8 0.0 collective-permute-done.4.cot
  21.8 0.0 collective-permute-done.3.pre
  21.8 1.4 collective-permute-start.7
  23.2 0.1 collective-permute-start.8
  23.3 1.9 %shard_map.74 = (bf16[128,1024]{1,0:T(8,128)(2,1)}, bf16[128,1024]{1,0:T(8,128)(2,1)}) custom-call(bf16[256,1024]{1,0:T(8,128)(2,1)} %collective-permute-done.upper.refs_9_, bf16[256,1024]{1,0:T(8,128)(2,1)} %collective-permute-done.1.lower.refs_10_), custom_call_target="tpu_custom_call" | custom-call | tf_op jit(solution)/shard_map/pallas_call | solution.py:102
  25.2 2.6 %collective-permute-start.5 = (bf16[128,1024]{1,0:T(8,128)(2,1)}, bf16[128,1024]{1,0:T(8,128)(2,1)S(1)}, u32[]{:S(2)}, u32[]{:S(2)}) collective-permute-start(bf16[128,1024]{1,0:T(8,128)(2,1)} %get-tuple-element.54), channel_id=1, source_target_pairs={{0,6},{2,0},{4,2},{6,4},{1,7},{3,1},{5,3},{7,5},{8,14},{10,8},{12,... | collective-permute-start | bytes 786440 | tf_op jit(solution)/shard_map/ppermute | solution.py:265
  27.9 0.0 collective-permute-start.6
  27.9 5.9 %shard_map.75 = (bf16[2048,576]{1,0:T(8,128)(2,1)}, bf16[1024,576]{1,0:T(8,128)(2,1)}) custom-call(s32[4]{0:T(128)} %pad_add_fusion.here, bf16[576,4096]{1,0:T(8,128)(2,1)} %collective-permute-done.3.pre, bf16[576,1024]{1,0:T(8,128)(2,1)} %collective-permute-done.4.cot), custom_call_target="tpu_custom_call" | custom-call | flops 70778880 | bytes 5242880 | tf_op jit(solution)/shard_map/pallas_call | solution.py:73
  33.8 2.7 %collective-permute-done.6 = bf16[128,1024]{1,0:T(8,128)(2,1)S(1)} collective-permute-done((bf16[128,1024]{1,0:T(8,128)(2,1)}, bf16[128,1024]{1,0:T(8,128)(2,1)S(1)}, u32[]{:S(2)}, u32[]{:S(2)}) %collective-permute-start.6) | collective-permute-done | bytes 262176 | tf_op jit(solution)/shard_map/ppermute | solution.py:265
  36.5 2.7 %collective-permute-start.9 = (bf16[256,1024]{1,0:T(8,128)(2,1)}, bf16[256,1024]{1,0:T(8,128)(2,1)}, u32[]{:S(2)}, u32[]{:S(2)}) collective-permute-start(bf16[256,1024]{1,0:T(8,128)(2,1)} %collective-permute-done.2.refs_8_), channel_id=1, source_target_pairs={{0,6},{2,0},{4,2},{6,4},{1,7},{3,1},{5,3},{7,5},{8,14},{10,8},{12,... | collective-permute-start | bytes 1572872 | tf_op jit(solution)/shard_map/ppermute | solution.py:265
  39.2 2.9 %collective-permute-start.11 = (bf16[256,1024]{1,0:T(8,128)(2,1)S(1)}, bf16[256,1024]{1,0:T(8,128)(2,1)S(1)}, u32[]{:S(2)}, u32[]{:S(2)}) collective-permute-start(bf16[256,1024]{1,0:T(8,128)(2,1)S(1)} %constant_dynamic-update-slice_fusion.refs_11_), channel_id=1, source_target_pairs={{0,65},{1,64},{64,1},{65,0},{2,67},{3,66},{66,3},{67,2},{4,69},{5,... | collective-permute-start | bytes 1572872 | tf_op jit(solution)/shard_map/ppermute | solution.py:262
  42.1 12.9 %shard_map.76 = (bf16[4,2,256,128]{3,2,1,0:T(8,128)(2,1)}, bf16[4,2,256,128]{3,2,1,0:T(8,128)(2,1)}, bf16[4,2,256,128]{3,2,1,0:T(8,128)(2,1)}, bf16[4,2,256,128]{3,2,1,0:T(8,128)(2,1)}) custom-call(s32[4]{0:T(128)} %pad_add_fusion.here, bf16[1024,576]{1,0:T(8,128)(2,1)} %get-tuple-element.51.refs_0_, bf16[1024,576]{1,0:T(8,128)(2,1)} %get-tuple-element.63.refs_1_, ...), custom_call_target="tpu_custom_call" | custom-call | flops 19327352832 | bytes 12582912 | tf_op jit(solution)/shard_map/pallas_call | solution.py:188
  55.0 0.8 copy-done.10
  55.8 1.2 collective-permute-start.12
  57.0 2.4 %collective-permute-start.13 = (bf16[4,2,256,128]{3,2,1,0:T(8,128)(2,1)}, bf16[4,2,256,128]{3,2,1,0:T(8,128)(2,1)}, u32[]{:S(2)}, u32[]{:S(2)}) collective-permute-start(bf16[4,2,256,128]{3,2,1,0:T(8,128)(2,1)} %get-tuple-element.79), channel_id=1, source_target_pairs={{0,32},{16,48},{32,0},{48,16},{1,33},{17,49},{33,1},{49,17},{2,34}... | collective-permute-start | bytes 1572872 | tf_op jit(solution)/shard_map/ppermute | solution.py:265
  59.5 1.2 collective-permute-start.14
  60.6 10.4 %shard_map.78 = (bf16[8,256,128]{2,1,0:T(8,128)(2,1)}, bf16[8,256,128]{2,1,0:T(8,128)(2,1)}, bf16[8,256,128]{2,1,0:T(8,128)(2,1)}) custom-call(s32[4]{0:T(128)} %pad_add_fusion.here, bf16[1024,576]{1,0:T(8,128)(2,1)} %get-tuple-element.51.refs_0_, bf16[1024,576]{1,0:T(8,128)(2,1)} %get-tuple-element.63.refs_1_, bf16[576,1024]{1,0:T(8,128)(2,1)} %refs_2_.5, ...), custom_call_target="tpu_custom_call" | custom-call | flops 14495514624 | bytes 9437184 | tf_op jit(solution)/shard_map/pallas_call | solution.py:188
  71.0 0.1 collective-permute-start.15
  71.1 1.2 collective-permute-start.16
  72.3 1.5 collective-permute-start.17
  73.8 6.8 %collective-permute-done.13 = bf16[4,2,256,128]{3,2,1,0:T(8,128)(2,1)} collective-permute-done((bf16[4,2,256,128]{3,2,1,0:T(8,128)(2,1)}, bf16[4,2,256,128]{3,2,1,0:T(8,128)(2,1)}, u32[]{:S(2)}, u32[]{:S(2)}) %collective-permute-start.13) | collective-permute-done | bytes 524320 | tf_op jit(solution)/shard_map/ppermute | solution.py:265
  80.6 1.4 collective-permute-done.14
  82.0 2.3 %add_convert_fusion.1 = bf16[4,2,256,128]{3,2,1,0:T(8,128)(2,1)} fusion(bf16[4,2,256,128]{3,2,1,0:T(8,128)(2,1)} %collective-permute-done.14, bf16[4,2,256,128]{3,2,1,0:T(8,128)(2,1)} %collective-permute-done.13, bf16[4,2,256,128]{3,2,1,0:T(8,128)(2,1)S(1)} %collective-permute-done.12, bf16[4,2,256,128]{3,2,1,0:T(8,128)(2,1)S(1)} %copy-done.2), kind=kLoop, calls=%fused_computation.8 | loop fusion | flops 2097152 | bytes 2621440 | tf_op jit(solution)/shard_map/convert_element_type | solution.py:290
  84.3 3.5 %all-to-all-start = ((bf16[8,256,128]{2,1,0:T(8,128)(2,1)}), bf16[8,256,128]{2,1,0:T(8,128)(2,1)S(1)}, u32[]{:S(2)}, u32[]{:S(2)}) async-start(bf16[8,256,128]{2,1,0:T(8,128)(2,1)} %bitcast.4), calls=%async_computation | async-start | bytes 1048576 | tf_op jit(solution)/shard_map/all_to_all | solution.py:293
  87.8 5.6 %shard_map.77 = bf16[8,256,128]{2,1,0:T(8,128)(2,1)} custom-call(s32[4]{0:T(128)} %pad_add_fusion.here, bf16[1024,576]{1,0:T(8,128)(2,1)} %get-tuple-element.51.refs_0_, bf16[1024,576]{1,0:T(8,128)(2,1)} %get-tuple-element.63.refs_1_, bf16[576,1024]{1,0:T(8,128)(2,1)} %refs_2_.5, bf16[576,1024]{1,0:T(8,128)(2,1)} %collective-permute-done.8.refs_3_, ...), custom_call_target="tpu_custom_call" | custom-call | flops 4831838208 | bytes 3145728 | tf_op jit(solution)/shard_map/pallas_call | solution.py:188
  93.4 0.0 copy-start.3
  93.4 0.8 copy-done.3
  94.2 2.3 %collective-permute-done.17 = bf16[8,256,128]{2,1,0:T(8,128)(2,1)} collective-permute-done((bf16[8,256,128]{2,1,0:T(8,128)(2,1)}, bf16[8,256,128]{2,1,0:T(8,128)(2,1)}, u32[]{:S(2)}, u32[]{:S(2)}) %collective-permute-start.17) | collective-permute-done | bytes 524320 | tf_op jit(solution)/shard_map/ppermute | solution.py:265
  96.5 1.8 %add_convert_fusion = bf16[8,256,128]{2,1,0:T(8,128)(2,1)S(1)} fusion(bf16[8,256,128]{2,1,0:T(8,128)(2,1)} %collective-permute-done.17, bf16[8,256,128]{2,1,0:T(8,128)(2,1)} %collective-permute-done.16, bf16[8,256,128]{2,1,0:T(8,128)(2,1)} %copy-done.3, bf16[8,256,128]{2,1,0:T(8,128)(2,1)} %shard_map.77), kind=kLoop, calls=%fused_computation.7 | loop fusion | flops 2097152 | bytes 2621440 | tf_op jit(solution)/shard_map/convert_element_type | solution.py:290
  98.3 3.6 %all-to-all-done = bf16[8,256,128]{2,1,0:T(8,128)(2,1)S(1)} async-done(((bf16[8,256,128]{2,1,0:T(8,128)(2,1)}), bf16[8,256,128]{2,1,0:T(8,128)(2,1)S(1)}, u32[]{:S(2)}, u32[]{:S(2)}) %all-to-all-start) | async-done | bytes 524320 | tf_op jit(solution)/shard_map/all_to_all | solution.py:293
  101.9 0.1 fusion.7
  102.0 10.1 %all_to_all.15 = bf16[8,256,128]{2,1,0:T(8,128)(2,1)S(1)} all-to-all(bf16[8,256,128]{2,1,0:T(8,128)(2,1)S(1)} %add_convert_fusion), channel_id=1, replica_groups=mesh['zl'=2,'x'=4,'c'=2,'y'=4,'zh'=2] {'x','zl'}, dimensions={0} | all-to-all | bytes 1048576 | tf_op jit(solution)/shard_map/all_to_all | solution.py:293
  112.1 0.1 add_convert_fusion.5
  112.2 0.8 collective-permute-start.18
  113.0 4.6 %collective-permute-done.18 = bf16[2,256,128]{2,1,0:T(8,128)(2,1)S(1)} collective-permute-done((bf16[2,256,128]{2,1,0:T(8,128)(2,1)S(1)}, bf16[2,256,128]{2,1,0:T(8,128)(2,1)S(1)}, u32[]{:S(2)}, u32[]{:S(2)}) %collective-permute-start.18) | collective-permute-done | bytes 131104 | tf_op jit(solution)/shard_map/ppermute | solution.py:303
  117.6 0.0 copy-start.4
  117.7 2.1 %collective-permute-start.19 = (bf16[2,256,128]{2,1,0:T(8,128)(2,1)S(1)}, bf16[2,256,128]{2,1,0:T(8,128)(2,1)S(1)}, u32[]{:S(2)}, u32[]{:S(2)}) collective-permute-start(bf16[2,256,128]{2,1,0:T(8,128)(2,1)S(1)} %add_convert_fusion.2.refs_0_), channel_id=1, source_target_pairs={{0,6},{2,0},{4,2},{6,4},{1,7},{3,1},{5,3},{7,5},{8,14},{10,8},{12,... | collective-permute-start | bytes 393224 | tf_op jit(solution)/shard_map/ppermute | solution.py:265
  119.8 0.1 collective-permute-start.20
  119.8 1.7 %collective-permute-start.21 = (bf16[2,256,128]{2,1,0:T(8,128)(2,1)S(1)}, bf16[2,256,128]{2,1,0:T(8,128)(2,1)S(1)}, u32[]{:S(2)}, u32[]{:S(2)}) collective-permute-start(bf16[2,256,128]{2,1,0:T(8,128)(2,1)S(1)} %add_convert_fusion.2.refs_0_), channel_id=1, source_target_pairs={{0,4},{2,6},{4,0},{6,2},{1,5},{3,7},{5,1},{7,3},{8,12},{10,14},{12... | collective-permute-start | bytes 393224 | tf_op jit(solution)/shard_map/ppermute | solution.py:265
  121.5 0.6 collective-permute-done.19.refs_1_
  122.1 4.1 %collective-permute-done.20.refs_2_ = bf16[2,256,128]{2,1,0:T(8,128)(2,1)S(1)} collective-permute-done((bf16[2,256,128]{2,1,0:T(8,128)(2,1)S(1)}, bf16[2,256,128]{2,1,0:T(8,128)(2,1)S(1)}, u32[]{:S(2)}, u32[]{:S(2)}) %collective-permute-start.20) | collective-permute-done | bytes 131104 | tf_op jit(solution)/shard_map/ppermute | solution.py:265
  126.2 0.6 copy-done.6
  126.8 0.7 copy-done.7
  127.5 4.6 %shard_map.79 = (f32[256,128]{1,0:T(8,128)}, f32[256,128]{1,0:T(8,128)}) custom-call(s32[4]{0:T(128)} %pad_add_fusion.here, bf16[512,4096]{1,0:T(8,128)(2,1)} %g.1, bf16[2,256,128]{2,1,0:T(8,128)(2,1)} %copy-done.4, bf16[2,256,128]{2,1,0:T(8,128)(2,1)} %copy-done.5, bf16[2,256,128]{2,1,0:T(8,128)(2,1)} %copy-done.6, bf16[2,256,128]{2,1,0:T(8,128)(2,1)} %copy-done.7), custom_call_target="tpu_custom_call" | custom-call | flops 268435456 | bytes 3145728 | tf_op jit(solution)/shard_map/pallas_call | solution.py:237
  132.1 6.1 %collective-permute-start.22 = (f32[256,128]{1,0:T(8,128)}, f32[256,128]{1,0:T(8,128)S(1)}, u32[]{:S(2)}, u32[]{:S(2)}) collective-permute-start(f32[256,128]{1,0:T(8,128)} %get-tuple-element.90), channel_id=1, source_target_pairs={{0,8},{8,0},{1,9},{9,1},{2,10},{10,2},{3,11},{11,3},{4,12},{12,4},... | collective-permute-start | bytes 393224 | tf_op jit(solution)/shard_map/ppermute | solution.py:259
  138.2 1.2 collective-permute-done.22
  139.4 0.9 add_convert_fusion.4
  140.4 0.1 broadcast_in_dim.2
  140.4 11.2 %all_to_all.16 = bf16[8,256,128]{2,1,0:T(8,128)(2,1)S(1)} all-to-all(bf16[8,256,128]{2,1,0:T(8,128)(2,1)S(1)} %broadcast_in_dim.2), channel_id=1, replica_groups=mesh['zl'=2,'x'=4,'c'=2,'y'=4,'zh'=2] {'x','zl'}, dimensions={0} | all-to-all | bytes 1048576 | tf_op jit(solution)/shard_map/all_to_all | solution.py:308
  151.6 0.2 copy.8
  151.8 2.1 %collective-permute-start.23 = (bf16[256,1024]{0,1:T(8,128)(2,1)S(1)}, bf16[256,1024]{0,1:T(8,128)(2,1)S(1)}, u32[]{:S(2)}, u32[]{:S(2)}) collective-permute-start(bf16[256,1024]{0,1:T(8,128)(2,1)S(1)} %bitcast.14), channel_id=1, source_target_pairs={{0,8},{8,0},{1,9},{9,1},{2,10},{10,2},{3,11},{11,3},{4,12},{12,4},... | collective-permute-start | bytes 1572872 | tf_op jit(solution)/shard_map/ppermute | solution.py:259
  154.0 1.5 collective-permute-done.23
  155.5 2.6 %fusion = f32[512,1024]{1,0:T(8,128)} fusion(bf16[1024,1024]{1,0:T(8,128)(2,1)S(1)} %copy-done, bf16[256,1024]{0,1:T(8,128)(2,1)S(1)} %collective-permute-done.23, bf16[256,1024]{0,1:T(8,128)(2,1)S(1)} %bitcast.15, pred[]{:T(512)S(6)} %eq.3), kind=kOutput, calls=%fused_computation.1 | convolution fusion | flops 1078460416 | bytes 5242881 | tf_op jit(solution)/shard_map/dot_general | solution.py:313
  (31 shorter events, 0.2 us)
Async XLA Ops:
  0.0 155.5 %copy-start = (bf16[1024,1024]{1,0:T(8,128)(2,1)S(1)}, bf16[1024,1024]{1,0:T(8,128)(2,1)}, u32[]{:S(2)}) copy-start(bf16[1024,1024]{1,0:T(8,128)(2,1)} %param.12) | copy-start | bytes 6291460
  0.0 21.8 %collective-permute-start.3 = (bf16[576,4096]{1,0:T(8,128)(2,1)}, bf16[576,4096]{1,0:T(8,128)(2,1)}, u32[]{:S(2)}, u32[]{:S(2)}) collective-permute-start(bf16[576,4096]{1,0:T(8,128)(2,1)} %pre.1), channel_id=1, source_target_pairs={{0,8},{8,0},{1,9},{9,1},{2,10},{10,2},{3,11},{11,3},{4,12},{12,4},... | collective-permute-start | bytes 14155784 | tf_op jit(solution)/shard_map/ppermute | solution.py:259
  1.4 20.4 %collective-permute-start.4 = (bf16[576,1024]{1,0:T(8,128)(2,1)}, bf16[576,1024]{1,0:T(8,128)(2,1)}, u32[]{:S(2)}, u32[]{:S(2)}) collective-permute-start(bf16[576,1024]{1,0:T(8,128)(2,1)} %cot.1), channel_id=1, source_target_pairs={{0,8},{8,0},{1,9},{9,1},{2,10},{10,2},{3,11},{11,3},{4,12},{12,4},... | collective-permute-start | bytes 3538952 | tf_op jit(solution)/shard_map/ppermute | solution.py:259
  3.3 14.2 %collective-permute-start = (bf16[256,1024]{1,0:T(8,128)(2,1)}, bf16[256,1024]{1,0:T(8,128)(2,1)}, u32[]{:S(2)}, u32[]{:S(2)}) collective-permute-start(bf16[256,1024]{1,0:T(8,128)(2,1)} %constant_dynamic-slice_fusion.refs_8_), channel_id=1, source_target_pairs={{0,6},{2,0},{4,2},{6,4},{1,7},{3,1},{5,3},{7,5},{8,14},{10,8},{12,... | collective-permute-start | bytes 1572872 | tf_op jit(solution)/shard_map/ppermute | solution.py:265
  6.2 14.1 %collective-permute-start.1 = (bf16[256,1024]{1,0:T(8,128)(2,1)}, bf16[256,1024]{1,0:T(8,128)(2,1)}, u32[]{:S(2)}, u32[]{:S(2)}) collective-permute-start(bf16[256,1024]{1,0:T(8,128)(2,1)} %constant_dynamic-slice_fusion.refs_8_), channel_id=1, source_target_pairs={{0,2},{2,4},{4,6},{6,0},{1,3},{3,5},{5,7},{7,1},{8,10},{10,12},{12... | collective-permute-start | bytes 1572872 | tf_op jit(solution)/shard_map/ppermute | solution.py:265
  6.2 15.6 %collective-permute-start.2 = (bf16[256,1024]{1,0:T(8,128)(2,1)}, bf16[256,1024]{1,0:T(8,128)(2,1)}, u32[]{:S(2)}, u32[]{:S(2)}) collective-permute-start(bf16[256,1024]{1,0:T(8,128)(2,1)} %constant_dynamic-slice_fusion.refs_8_), channel_id=1, source_target_pairs={{0,65},{1,64},{64,1},{65,0},{2,67},{3,66},{66,3},{67,2},{4,69},{5,... | collective-permute-start | bytes 1572872 | tf_op jit(solution)/shard_map/ppermute | solution.py:262
  10.6 12.6 %copy-start.1 = (bf16[576,1024]{1,0:T(8,128)(2,1)S(1)}, bf16[576,1024]{1,0:T(8,128)(2,1)}, u32[]{:S(2)}) copy-start(bf16[576,1024]{1,0:T(8,128)(2,1)} %refs_2_.5) | copy-start | bytes 3538948
  21.8 14.6 %collective-permute-start.7 = (bf16[2048,1024]{1,0:T(8,128)(2,1)}, bf16[2048,1024]{1,0:T(8,128)(2,1)}, u32[]{:S(2)}, u32[]{:S(2)}) collective-permute-start(bf16[2048,1024]{1,0:T(8,128)(2,1)} %get-tuple-element.56), channel_id=1, source_target_pairs={{0,8},{8,0},{1,9},{9,1},{2,10},{10,2},{3,11},{11,3},{4,12},{12,4},... | collective-permute-start | bytes 12582920 | tf_op jit(solution)/shard_map/ppermute | solution.py:259
  23.2 13.2 %collective-permute-start.8 = (bf16[576,1024]{1,0:T(8,128)(2,1)S(1)}, bf16[576,1024]{1,0:T(8,128)(2,1)}, u32[]{:S(2)}, u32[]{:S(2)}) collective-permute-start(bf16[576,1024]{1,0:T(8,128)(2,1)S(1)} %copy-done.1), channel_id=1, source_target_pairs={{0,8},{8,0},{1,9},{9,1},{2,10},{10,2},{3,11},{11,3},{4,12},{12,4},... | collective-permute-start | bytes 3538952 | tf_op jit(solution)/shard_map/ppermute | solution.py:259
  25.2 8.5 %collective-permute-start.5 = (bf16[128,1024]{1,0:T(8,128)(2,1)}, bf16[128,1024]{1,0:T(8,128)(2,1)S(1)}, u32[]{:S(2)}, u32[]{:S(2)}) collective-permute-start(bf16[128,1024]{1,0:T(8,128)(2,1)} %get-tuple-element.54), channel_id=1, source_target_pairs={{0,6},{2,0},{4,2},{6,4},{1,7},{3,1},{5,3},{7,5},{8,14},{10,8},{12,... | collective-permute-start | bytes 786440 | tf_op jit(solution)/shard_map/ppermute | solution.py:265
  27.9 8.6 %collective-permute-start.6 = (bf16[128,1024]{1,0:T(8,128)(2,1)}, bf16[128,1024]{1,0:T(8,128)(2,1)S(1)}, u32[]{:S(2)}, u32[]{:S(2)}) collective-permute-start(bf16[128,1024]{1,0:T(8,128)(2,1)} %get-tuple-element.55), channel_id=1, source_target_pairs={{0,2},{2,4},{4,6},{6,0},{1,3},{3,5},{5,7},{7,1},{8,10},{10,12},{12... | collective-permute-start | bytes 786440 | tf_op jit(solution)/shard_map/ppermute | solution.py:265
  36.5 18.6 %collective-permute-start.10 = (bf16[256,1024]{1,0:T(8,128)(2,1)}, bf16[256,1024]{1,0:T(8,128)(2,1)S(1)}, u32[]{:S(2)}, u32[]{:S(2)}) collective-permute-start(bf16[256,1024]{1,0:T(8,128)(2,1)} %collective-permute-done.2.refs_8_), channel_id=1, source_target_pairs={{0,2},{2,4},{4,6},{6,0},{1,3},{3,5},{5,7},{7,1},{8,10},{10,12},{12... | collective-permute-start | bytes 1572872 | tf_op jit(solution)/shard_map/ppermute | solution.py:265
  36.5 18.6 %collective-permute-start.9 = (bf16[256,1024]{1,0:T(8,128)(2,1)}, bf16[256,1024]{1,0:T(8,128)(2,1)}, u32[]{:S(2)}, u32[]{:S(2)}) collective-permute-start(bf16[256,1024]{1,0:T(8,128)(2,1)} %collective-permute-done.2.refs_8_), channel_id=1, source_target_pairs={{0,6},{2,0},{4,2},{6,4},{1,7},{3,1},{5,3},{7,5},{8,14},{10,8},{12,... | collective-permute-start | bytes 1572872 | tf_op jit(solution)/shard_map/ppermute | solution.py:265
  39.2 2.9 %copy-start.8 = (bf16[256,1024]{1,0:T(8,128)(2,1)}, bf16[256,1024]{1,0:T(8,128)(2,1)S(1)}, u32[]{:S(2)}) copy-start(bf16[256,1024]{1,0:T(8,128)(2,1)S(1)} %constant_dynamic-update-slice_fusion.refs_11_) | copy-start | bytes 1572868
  39.2 15.8 %collective-permute-start.11 = (bf16[256,1024]{1,0:T(8,128)(2,1)S(1)}, bf16[256,1024]{1,0:T(8,128)(2,1)S(1)}, u32[]{:S(2)}, u32[]{:S(2)}) collective-permute-start(bf16[256,1024]{1,0:T(8,128)(2,1)S(1)} %constant_dynamic-update-slice_fusion.refs_11_), channel_id=1, source_target_pairs={{0,65},{1,64},{64,1},{65,0},{2,67},{3,66},{66,3},{67,2},{4,69},{5,... | collective-permute-start | bytes 1572872 | tf_op jit(solution)/shard_map/ppermute | solution.py:262
  55.0 0.8 copy-start.10
  55.0 5.6 %copy-start.9 = (bf16[256,1024]{1,0:T(8,128)(2,1)}, bf16[256,1024]{1,0:T(8,128)(2,1)S(1)}, u32[]{:S(2)}) copy-start(bf16[256,1024]{1,0:T(8,128)(2,1)S(1)} %collective-permute-done.10.refs_10_) | copy-start | bytes 1572868
  55.8 26.2 %copy-start.2 = (bf16[4,2,256,128]{3,2,1,0:T(8,128)(2,1)S(1)}, bf16[4,2,256,128]{3,2,1,0:T(8,128)(2,1)}, u32[]{:S(2)}) copy-start(bf16[4,2,256,128]{3,2,1,0:T(8,128)(2,1)} %get-tuple-element.77) | copy-start | bytes 1572868
  55.8 16.4 %collective-permute-start.12 = (bf16[4,2,256,128]{3,2,1,0:T(8,128)(2,1)}, bf16[4,2,256,128]{3,2,1,0:T(8,128)(2,1)S(1)}, u32[]{:S(2)}, u32[]{:S(2)}) collective-permute-start(bf16[4,2,256,128]{3,2,1,0:T(8,128)(2,1)} %get-tuple-element.78), channel_id=1, source_target_pairs={{0,16},{16,32},{32,48},{48,0},{1,17},{17,33},{33,49},{49,1},{2,18}... | collective-permute-start | bytes 1572872 | tf_op jit(solution)/shard_map/ppermute | solution.py:265
  57.0 23.5 %collective-permute-start.13 = (bf16[4,2,256,128]{3,2,1,0:T(8,128)(2,1)}, bf16[4,2,256,128]{3,2,1,0:T(8,128)(2,1)}, u32[]{:S(2)}, u32[]{:S(2)}) collective-permute-start(bf16[4,2,256,128]{3,2,1,0:T(8,128)(2,1)} %get-tuple-element.79), channel_id=1, source_target_pairs={{0,32},{16,48},{32,0},{48,16},{1,33},{17,49},{33,1},{49,17},{2,34}... | collective-permute-start | bytes 1572872 | tf_op jit(solution)/shard_map/ppermute | solution.py:265
  59.5 22.5 %collective-permute-start.14 = (bf16[4,2,256,128]{3,2,1,0:T(8,128)(2,1)}, bf16[4,2,256,128]{3,2,1,0:T(8,128)(2,1)}, u32[]{:S(2)}, u32[]{:S(2)}) collective-permute-start(bf16[4,2,256,128]{3,2,1,0:T(8,128)(2,1)} %get-tuple-element.80), channel_id=1, source_target_pairs={{0,48},{16,0},{32,16},{48,32},{1,49},{17,1},{33,17},{49,33},{2,50}... | collective-permute-start | bytes 1572872 | tf_op jit(solution)/shard_map/ppermute | solution.py:265
  71.0 22.4 %collective-permute-start.15 = (bf16[8,256,128]{2,1,0:T(8,128)(2,1)}, bf16[8,256,128]{2,1,0:T(8,128)(2,1)S(1)}, u32[]{:S(2)}, u32[]{:S(2)}) collective-permute-start(bf16[8,256,128]{2,1,0:T(8,128)(2,1)} %get-tuple-element.84), channel_id=1, source_target_pairs={{0,2},{2,4},{4,6},{6,0},{1,3},{3,5},{5,7},{7,1},{8,10},{10,12},{12... | collective-permute-start | bytes 1572872 | tf_op jit(solution)/shard_map/ppermute | solution.py:265
  71.1 22.3 %collective-permute-start.16 = (bf16[8,256,128]{2,1,0:T(8,128)(2,1)}, bf16[8,256,128]{2,1,0:T(8,128)(2,1)}, u32[]{:S(2)}, u32[]{:S(2)}) collective-permute-start(bf16[8,256,128]{2,1,0:T(8,128)(2,1)} %get-tuple-element.85), channel_id=1, source_target_pairs={{0,4},{2,6},{4,0},{6,2},{1,5},{3,7},{5,1},{7,3},{8,12},{10,14},{12... | collective-permute-start | bytes 1572872 | tf_op jit(solution)/shard_map/ppermute | solution.py:265
  72.3 24.2 %collective-permute-start.17 = (bf16[8,256,128]{2,1,0:T(8,128)(2,1)}, bf16[8,256,128]{2,1,0:T(8,128)(2,1)}, u32[]{:S(2)}, u32[]{:S(2)}) collective-permute-start(bf16[8,256,128]{2,1,0:T(8,128)(2,1)} %get-tuple-element.86), channel_id=1, source_target_pairs={{0,6},{2,0},{4,2},{6,4},{1,7},{3,1},{5,3},{7,5},{8,14},{10,8},{12,... | collective-permute-start | bytes 1572872 | tf_op jit(solution)/shard_map/ppermute | solution.py:265
  84.3 17.6 %all-to-all-start = ((bf16[8,256,128]{2,1,0:T(8,128)(2,1)}), bf16[8,256,128]{2,1,0:T(8,128)(2,1)S(1)}, u32[]{:S(2)}, u32[]{:S(2)}) async-start(bf16[8,256,128]{2,1,0:T(8,128)(2,1)} %bitcast.4), calls=%async_computation | async-start | bytes 1048576 | tf_op jit(solution)/shard_map/all_to_all | solution.py:293
  93.4 0.8 copy-start.3
  112.2 5.4 %collective-permute-start.18 = (bf16[2,256,128]{2,1,0:T(8,128)(2,1)S(1)}, bf16[2,256,128]{2,1,0:T(8,128)(2,1)S(1)}, u32[]{:S(2)}, u32[]{:S(2)}) collective-permute-start(bf16[2,256,128]{2,1,0:T(8,128)(2,1)S(1)} %pad_maximum_fusion), channel_id=1, source_target_pairs={{0,1},{1,0},{2,3},{3,2},{4,5},{5,4},{6,7},{7,6},{8,9},{9,8},{10,11... | collective-permute-start | bytes 393224 | tf_op jit(solution)/shard_map/ppermute | solution.py:303
  117.6 8.6 %copy-start.4 = (bf16[2,256,128]{2,1,0:T(8,128)(2,1)}, bf16[2,256,128]{2,1,0:T(8,128)(2,1)S(1)}, u32[]{:S(2)}) copy-start(bf16[2,256,128]{2,1,0:T(8,128)(2,1)S(1)} %add_convert_fusion.2.refs_0_) | copy-start | bytes 393220
  117.7 4.4 %collective-permute-start.19 = (bf16[2,256,128]{2,1,0:T(8,128)(2,1)S(1)}, bf16[2,256,128]{2,1,0:T(8,128)(2,1)S(1)}, u32[]{:S(2)}, u32[]{:S(2)}) collective-permute-start(bf16[2,256,128]{2,1,0:T(8,128)(2,1)S(1)} %add_convert_fusion.2.refs_0_), channel_id=1, source_target_pairs={{0,6},{2,0},{4,2},{6,4},{1,7},{3,1},{5,3},{7,5},{8,14},{10,8},{12,... | collective-permute-start | bytes 393224 | tf_op jit(solution)/shard_map/ppermute | solution.py:265
  119.8 6.4 %collective-permute-start.20 = (bf16[2,256,128]{2,1,0:T(8,128)(2,1)S(1)}, bf16[2,256,128]{2,1,0:T(8,128)(2,1)S(1)}, u32[]{:S(2)}, u32[]{:S(2)}) collective-permute-start(bf16[2,256,128]{2,1,0:T(8,128)(2,1)S(1)} %add_convert_fusion.2.refs_0_), channel_id=1, source_target_pairs={{0,2},{2,4},{4,6},{6,0},{1,3},{3,5},{5,7},{7,1},{8,10},{10,12},{12... | collective-permute-start | bytes 393224 | tf_op jit(solution)/shard_map/ppermute | solution.py:265
  119.8 6.4 %collective-permute-start.21 = (bf16[2,256,128]{2,1,0:T(8,128)(2,1)S(1)}, bf16[2,256,128]{2,1,0:T(8,128)(2,1)S(1)}, u32[]{:S(2)}, u32[]{:S(2)}) collective-permute-start(bf16[2,256,128]{2,1,0:T(8,128)(2,1)S(1)} %add_convert_fusion.2.refs_0_), channel_id=1, source_target_pairs={{0,4},{2,6},{4,0},{6,2},{1,5},{3,7},{5,1},{7,3},{8,12},{10,14},{12... | collective-permute-start | bytes 393224 | tf_op jit(solution)/shard_map/ppermute | solution.py:265
  122.1 4.1 %copy-start.5 = (bf16[2,256,128]{2,1,0:T(8,128)(2,1)}, bf16[2,256,128]{2,1,0:T(8,128)(2,1)S(1)}, u32[]{:S(2)}) copy-start(bf16[2,256,128]{2,1,0:T(8,128)(2,1)S(1)} %collective-permute-done.19.refs_1_) | copy-start | bytes 393220
  126.2 0.6 copy-start.6
  126.8 0.7 copy-start.7
  132.1 7.3 %collective-permute-start.22 = (f32[256,128]{1,0:T(8,128)}, f32[256,128]{1,0:T(8,128)S(1)}, u32[]{:S(2)}, u32[]{:S(2)}) collective-permute-start(f32[256,128]{1,0:T(8,128)} %get-tuple-element.90), channel_id=1, source_target_pairs={{0,8},{8,0},{1,9},{9,1},{2,10},{10,2},{3,11},{11,3},{4,12},{12,4},... | collective-permute-start | bytes 393224 | tf_op jit(solution)/shard_map/ppermute | solution.py:259
  151.8 3.7 %collective-permute-start.23 = (bf16[256,1024]{0,1:T(8,128)(2,1)S(1)}, bf16[256,1024]{0,1:T(8,128)(2,1)S(1)}, u32[]{:S(2)}, u32[]{:S(2)}) collective-permute-start(bf16[256,1024]{0,1:T(8,128)(2,1)S(1)} %bitcast.14), channel_id=1, source_target_pairs={{0,8},{8,0},{1,9},{9,1},{2,10},{10,2},{3,11},{11,3},{4,12},{12,4},... | collective-permute-start | bytes 1572872 | tf_op jit(solution)/shard_map/ppermute | solution.py:259

commit v3 on v2

--- a/solution.py
+++ b/solution.py
@@ -112,8 +112,8 @@
     n = len(part)
     cot, cot_o, inp, inp_o, slope, slope_o, ef, ef_o = refs[:8]
     n_out = 4 if by_columns else n
-    ws, outs = refs[8 : 8 + n], refs[8 + n : 8 + n + n_out]
-    w_v, cot_v, inp_v, slope_v, ef_v, out_v, sem, out_sem = refs[8 + n + n_out :]
+    ws, outs = refs[8 : -8 - n_out], refs[-8 - n_out : -8]
+    w_v, cot_v, inp_v, slope_v, ef_v, out_v, sem, out_sem = refs[-8:]
     core, x, y, zh = (here[k] for k in range(4))
     blocks = [lax.rem(y + dy, 4) * 2 + (1 - zh if dz else zh) for dy, dz in part]
 
@@ -128,7 +128,10 @@
 
     for i in range(n):
         block = blocks[i]
-        read(("w", i), ws[i], w_v.at[i])
+        halves = i == n - 1 and len(ws) > n
+        read(("w", i), ws[i], w_v.at[i, pl.ds(0, 128)] if halves else w_v.at[i])
+        if halves:
+            read("lower", ws[n], w_v.at[i, pl.ds(128, 128)])
         if i == 0:
             read("cot", cot, cot_v.at[0])
             read("cot_o", cot_o, cot_v.at[1])
@@ -143,6 +146,8 @@
     writes = []
     for i in range(n):
         reads["w", i].wait()
+        if i == n - 1 and len(ws) > n:
+            reads["lower"].wait()
         hidden = []
         for k, suffix in enumerate(("", "_o")):
             if i == 0:
@@ -180,7 +185,7 @@
 
 
 def terms(by_columns, part, here, cot, cot_o, inp, inp_o, slope, slope_o, ef, ef_o, ws):
-    n = len(ws)
+    n = len(part)
     if by_columns:
         out_shape = [jax.ShapeDtypeStruct((n, 2, 256, 128), BF)] * 4
     else:
@@ -188,7 +193,7 @@
     return pl.pallas_call(
         functools.partial(term_kernel, by_columns, part),
         in_specs=[pl.BlockSpec(memory_space=pltpu.SMEM)]
-        + [pl.BlockSpec(memory_space=pl.ANY)] * (8 + n),
+        + [pl.BlockSpec(memory_space=pl.ANY)] * (8 + len(ws)),
         out_specs=[pl.BlockSpec(memory_space=pl.ANY)] * len(out_shape),
         out_shape=out_shape,
         scratch_shapes=[
@@ -198,57 +203,43 @@
             pltpu.VMEM((n, 2, 256, 576), BF),
             pltpu.VMEM((n, 2, 256, 1024), BF),
             pltpu.VMEM((n, 8, 256, 128), BF),
-            pltpu.SemaphoreType.DMA((4 + 5 * n,)),
+            pltpu.SemaphoreType.DMA((5 + 5 * n,)),
             pltpu.SemaphoreType.DMA((4 * n if by_columns else n,)),
         ],
         compiler_params=pltpu.CompilerParams(vmem_limit_bytes=60 * 2**20),
         cost_estimate=pl.CostEstimate(
-            flops=16 * 1152 * 1024 * 256 * n, bytes_accessed=3 * n * 2**20, transcendentals=0
+            flops=(16 if n == 4 else 4) * 1152 * 1024 * 256 * n, bytes_accessed=3 * n * 2**20, transcendentals=0
         ),
     )(here, cot, cot_o, inp, inp_o, slope, slope_o, ef, ef_o, *ws)
 
 
-def left_kernel(here, g, *refs):
-    grads, (mine, other), (g_v, grad_v, total, sem) = refs[:4], refs[4:6], refs[6:]
+def columns_kernel(here, g, out, sem):
     c, _, y, zh = (here[k] for k in range(4))
-    reads = []
+    copies = []
     for i, dy in enumerate((0, 1, 3, 2)):
         for k in range(2):
             block = lax.rem(y + dy, 4) * 2 + (1 - zh if k else zh)
             cols = pl.ds(pl.multiple_of((2 * block + c) * 256, 256), 256)
-            reads.append(pltpu.make_async_copy(g.at[:, cols], g_v.at[2 * i + k], sem.at[2 * i + k]))
-            reads[-1].start()
-    for i in range(4):
-        reads.append(pltpu.make_async_copy(grads[i], grad_v.at[i], sem.at[8 + i]))
-        reads[-1].start()
-    product = 0.0
-    for i in range(4):
-        reads[8 + i].wait()
-        for k in range(2):
-            reads[2 * i + k].wait()
-            product += jnp.dot(g_v[2 * i + k], grad_v[i, k], preferred_element_type=F32)
-    total[...] = product
-    mine[...] = total[pl.ds(pl.multiple_of(c * 256, 256), 256), :]
-    other[...] = total[pl.ds(pl.multiple_of((1 - c) * 256, 256), 256), :]
-
-
-def left_product(here, g, grads):
-    whole = pl.BlockSpec(memory_space=pltpu.VMEM)
+            n = 2 * i + k
+            copies.append(
+                pltpu.make_async_copy(
+                    g.at[:, cols], out.at[:, n * 256 : (n + 1) * 256], sem.at[n]
+                )
+            )
+            copies[-1].start()
+    for copy in copies:
+        copy.wait()
+
+
+def own_columns(here, g):
     return pl.pallas_call(
-        left_kernel,
-        in_specs=[pl.BlockSpec(memory_space=pltpu.SMEM)] + [pl.BlockSpec(memory_space=pl.ANY)] * 5,
-        out_specs=[whole, whole],
-        out_shape=[jax.ShapeDtypeStruct((256, 128), F32)] * 2,
-        scratch_shapes=[
-            pltpu.VMEM((8, 512, 256), BF),
-            pltpu.VMEM((4, 2, 256, 128), BF),
-            pltpu.VMEM((512, 128), F32),
-            pltpu.SemaphoreType.DMA((12,)),
-        ],
-        cost_estimate=pl.CostEstimate(
-            flops=2 * 512 * 2048 * 128, bytes_accessed=3 * 2**20, transcendentals=0
-        ),
-    )(here, g, *grads)
+        columns_kernel,
+        in_specs=[pl.BlockSpec(memory_space=pltpu.SMEM), pl.BlockSpec(memory_space=pl.ANY)],
+        out_specs=pl.BlockSpec(memory_space=pltpu.VMEM),
+        out_shape=jax.ShapeDtypeStruct((512, 2048), BF),
+        scratch_shapes=[pltpu.SemaphoreType.DMA((8,))],
+        cost_estimate=pl.CostEstimate(flops=0, bytes_accessed=4 * 2**20, transcendentals=0),
+    )(here, g)
 
 
 def shards(inputs, cotangent, pre_gelu, w_down, error_feedback, a_inverse, g_inverse):
@@ -268,8 +259,9 @@
     first = [ring(w_own, "y", -1), ring(w_own, "y", 1), across_z(w_own)]
     first += [swap(a) for a in (pre_gelu, cotangent)]
     slope, cot, carried = prepare(here, pre_gelu, cotangent, error_feedback)
-    w_up, w_low, w_z, pre_o, cot_o, slope, cot, carried, inp = lax.optimization_barrier(
-        (*first, slope, cot, carried, inputs)
+    g_half = own_columns(here, g_inverse)
+    w_up, w_low, w_z, pre_o, cot_o, slope, cot, carried, inp, g_half = lax.optimization_barrier(
+        (*first, slope, cot, carried, inputs, g_half)
     )
     upper, lower = cut(w_up, w_low)
     second = [ring(upper, "y", -1), ring(lower, "y", 1), swap(carried), swap(inp)]
@@ -277,8 +269,7 @@
     upper, lower, ef_o, inp_o, slope_o, cot_o, w_up, w_low, w_z = lax.optimization_barrier(
         (*second, slope_o, cot_o, w_up, w_low, w_z)
     )
-    w_far = jnp.concatenate([upper, lower])
-    third = [ring(w_z, "y", -1), ring(w_z, "y", 1), across_z(w_far)]
+    third = [ring(w_z, "y", -1), ring(w_z, "y", 1), across_z(upper), across_z(lower)]
 
     def product(by_columns, part, ws):
         return terms(
@@ -289,21 +280,25 @@
     def added(parts):
         return sum(p.astype(F32) for p in parts).astype(BF)
 
-    def scattered(a, axes):
-        return added(lax.all_to_all(a.reshape(8, 256, 128), axes, 0, 0, tiled=True))
-
-    near = product(True, ((0, 0), (1, 0), (3, 0), (2, 0)), [w_own, w_up, w_low, w_far])
+    def exchanged(a, axes):
+        return lax.all_to_all(a.reshape(8, 256, 128), axes, 0, 0, tiled=True)
+
+    near = product(True, ((0, 0), (1, 0), (3, 0), (2, 0)), [w_own, w_up, w_low, upper, lower])
     near, third = lax.optimization_barrier((near, third))
     near = added([near[0]] + [ring(near[j], "x", j) for j in (1, 2, 3)])
-    far, up, low = product(False, ((2, 1), (1, 1), (3, 1)), [third[2], third[0], third[1]])
+    (far,) = product(False, ((2, 1),), third[2:])
+    up, low = product(False, ((1, 1), (3, 1)), [third[0], third[1]])
     (own,) = product(False, ((0, 1),), [w_z])
     others = added([own, ring(up, "y", 1), ring(far, "y", 2), ring(low, "y", -1)])
-    near, others = lax.optimization_barrier((scattered(near, ("y", "zl")), others))
-    others = scattered(others, ("x", "zl"))
+    near, others = lax.optimization_barrier((exchanged(near, ("y", "zl")), others))
+    near, others = added(near), added(exchanged(others, ("x", "zl")))
     theirs = lax.ppermute(jnp.stack([others, near]), "zh", [(0, 1), (1, 0)])
     grad = added([jnp.stack([near, others]), theirs])
     grads = [grad, ring(grad, "y", -1), ring(grad, "y", 1), ring(grad, "y", 2)]
-    mine, other = left_product(here, g_inverse, grads)
+    part = jnp.dot(
+        g_half, jnp.concatenate(grads).reshape(2048, 128), preferred_element_type=F32
+    ).reshape(2, 256, 128)
+    mine, other = (lax.dynamic_index_in_dim(part, k, 0, keepdims=False) for k in (c, 1 - c))
     left = (mine + swap(other)).astype(BF)
     mine = lax.all_to_all(
         jnp.broadcast_to(left[None], (8, 256, 128)), ("x", "zl"), 0, 0, tiled=True

time: 159 us -> 152 us (0.956)
  blocking collectives: 21.3 us -> 12 us
  waiting for transfers between devices: 33.1 us -> 28.7 us
  starting transfers between devices: 41.8 us -> 46.1 us
  matrix products: 2.59 us -> 4.9 us
  local copies, waits for them, and re-layouts: 5.08 us -> 2.91 us
  Pallas kernels: 48.2 us -> 50.3 us
    all_to_all x1 -> x0, blocking collectives: 10.1 us -> none  [scattered(): return added(lax.all_to_all(a.reshape(8, 256, 128), axes, 0, 0, tiled=True))]
    ppermute x15, waiting for transfers between devices: 20.7 us -> 12.1 us  [ring(): return lax.ppermute(a, axis, [(i, (i + step) % 4) for i in range(4)])]
    all_to_all x1 -> x2, waiting for transfers between devices: 3.59 us -> 9.68 us  [exchanged(): return lax.all_to_all(a.reshape(8, 256, 128), axes, 0, 0, tiled=True)]
    all_to_all x1 -> x2, starting transfers between devices: 3.49 us -> 8.17 us  [exchanged(): return lax.all_to_all(a.reshape(8, 256, 128), axes, 0, 0, tiled=True)]
    pallas_call x3 -> x4, Pallas kernels: 28.8 us -> 32 us  [terms(): pl.pallas_call(functools.partial(term_kernel, by_columns, part), in_specs...]
    dot_general x0 -> x1, matrix products: none -> 2.31 us  [shards(): jnp.dot(g_half, jnp.concatenate(grads).reshape(2048, 128), preferred_elem...]
    unnamed x23 -> x18, local copies, waits for them, and re-layouts: 2.89 us -> 0.74 us
    ppermute x2 -> x3, starting transfers between devices: 6.66 us -> 6.45 us  [across_z(): return lax.ppermute(a, ('zl', 'zh'), [(i, 3 - i) for i in range(4)])]
  transfers between devices with their start and end apart: 25 -> 27, of which waited for: 12 -> 11; matrix products, arithmetic and copies ran while one was open for 4% -> 5% of each run, Pallas kernels for 28% -> 33%
where the time goes in v3:
time: 152 us; the launch traced here: 151 us
  Pallas kernels  50.3 us (33%)
  starting transfers between devices  46.1 us (30%)
  waiting for transfers between devices  28.7 us (19%)
  blocking collectives  12 us (8%)
  other arithmetic  5.82 us (4%)
  matrix products  4.9 us (3%)
  local copies, waits for them, and re-layouts  2.91 us (2%)
    pallas_call x4, Pallas kernels, terms(): pl.pallas_call(functools.partial(term_kernel, by_columns, part), in_specs...  32 us
    ppermute x15, starting transfers between devices, ring(): return lax.ppermute(a, axis, [(i, (i + step) % 4) for i in range(4)])  19.8 us
    pallas_call x2, Pallas kernels, prepare(): pl.pallas_call(prepare_kernel, in_specs=[pl.BlockSpec(memory_space=pltpu....  12.8 us
    ppermute x15, waiting for transfers between devices, ring(): return lax.ppermute(a, axis, [(i, (i + step) % 4) for i in range(4)])  12.1 us
    all_to_all x1, blocking collectives, shards(): lax.all_to_all(jnp.broadcast_to(left[None], (8, 256, 128)), ('x', 'zl'),...  12 us
    ppermute x6, starting transfers between devices, swap(): return lax.ppermute(a, 'c', [(0, 1), (1, 0)])  10.1 us
    all_to_all x2, waiting for transfers between devices, exchanged(): return lax.all_to_all(a.reshape(8, 256, 128), axes, 0, 0, tiled=True)  9.68 us
    all_to_all x2, starting transfers between devices, exchanged(): return lax.all_to_all(a.reshape(8, 256, 128), axes, 0, 0, tiled=True)  8.17 us
  transfers between devices with their start and end apart: 27, of which 11 were waited for; matrix products, arithmetic and copies ran while one was open for 5% of the time, Pallas kernels for 33%

profile of v3, /device:TPU:1, one launch (start us, length us, event | category | flops | bytes accessed | tf_op | source)
XLA Modules:
  0.0 151.0 jit_solution(17605582117990298030)
XLA Ops:
  0.0 1.4 collective-permute-start.3
  1.4 0.0 collective-permute-start.4
  1.4 1.9 %constant_dynamic-slice_fusion.refs_8_ = bf16[256,1024]{1,0:T(8,128)(2,1)} fusion(bf16[512,1024]{1,0:T(8,128)(2,1)} %param.10, s32[]{:T(128)S(6)} %select_n.19), kind=kLoop, calls=%fused_computation.18 | loop fusion | bytes 1048580 | tf_op jit(solution)/shard_map/dynamic_slice | solution.py:258
  3.3 2.9 %collective-permute-start = (bf16[256,1024]{1,0:T(8,128)(2,1)}, bf16[256,1024]{1,0:T(8,128)(2,1)}, u32[]{:S(2)}, u32[]{:S(2)}) collective-permute-start(bf16[256,1024]{1,0:T(8,128)(2,1)} %constant_dynamic-slice_fusion.refs_8_), channel_id=1, source_target_pairs={{0,6},{2,0},{4,2},{6,4},{1,7},{3,1},{5,3},{7,5},{8,14},{10,8},{12,... | collective-permute-start | bytes 1572872 | tf_op jit(solution)/shard_map/ppermute | solution.py:256
  6.2 0.0 collective-permute-start.1
  6.2 3.8 %collective-permute-start.2 = (bf16[256,1024]{1,0:T(8,128)(2,1)}, bf16[256,1024]{1,0:T(8,128)(2,1)}, u32[]{:S(2)}, u32[]{:S(2)}) collective-permute-start(bf16[256,1024]{1,0:T(8,128)(2,1)} %constant_dynamic-slice_fusion.refs_8_), channel_id=1, source_target_pairs={{0,65},{1,64},{64,1},{65,0},{2,67},{3,66},{66,3},{67,2},{4,69},{5,... | collective-permute-start | bytes 1572872 | tf_op jit(solution)/shard_map/ppermute | solution.py:253
  10.0 0.7 pad_add_fusion.here
  10.6 3.6 %shard_map.74 = bf16[512,2048]{1,0:T(8,128)(2,1)} custom-call(s32[4]{0:T(128)} %pad_add_fusion.here, bf16[512,4096]{1,0:T(8,128)(2,1)} %g.1), custom_call_target="tpu_custom_call" | custom-call | bytes 4194304 | tf_op jit(solution)/shard_map/pallas_call | solution.py:235
  14.2 0.0 copy-start.1
  14.2 6.9 %shard_map.73 = (bf16[2048,576]{1,0:T(8,128)(2,1)}, bf16[1024,576]{1,0:T(8,128)(2,1)}, bf16[2048,1024]{1,0:T(8,128)(2,1)}) custom-call(s32[4]{0:T(128)} %pad_add_fusion.here, bf16[576,4096]{1,0:T(8,128)(2,1)} %pre.1, bf16[576,1024]{1,0:T(8,128)(2,1)} %cot.1, bf16[4096,1024]{1,0:T(8,128)(2,1)} %refs_6_.7), custom_call_target="tpu_custom_call" | custom-call | flops 70778880 | bytes 5242880 | tf_op jit(solution)/shard_map/pallas_call | solution.py:73
  21.2 0.0 collective-permute-done.upper.refs_9_
  21.2 0.0 collective-permute-done.1.lower.refs_10_
  21.2 0.6 collective-permute-done.2.refs_8_
  21.8 0.0 collective-permute-done.4.cot
  21.8 0.0 collective-permute-done.3.pre
  21.8 1.4 collective-permute-start.7
  23.2 0.1 collective-permute-start.8
  23.3 1.9 %shard_map.75 = (bf16[128,1024]{1,0:T(8,128)(2,1)}, bf16[128,1024]{1,0:T(8,128)(2,1)}) custom-call(bf16[256,1024]{1,0:T(8,128)(2,1)} %collective-permute-done.upper.refs_9_, bf16[256,1024]{1,0:T(8,128)(2,1)} %collective-permute-done.1.lower.refs_10_), custom_call_target="tpu_custom_call" | custom-call | tf_op jit(solution)/shard_map/pallas_call | solution.py:102
  25.2 2.6 %collective-permute-start.5 = (bf16[128,1024]{1,0:T(8,128)(2,1)}, bf16[128,1024]{1,0:T(8,128)(2,1)S(1)}, u32[]{:S(2)}, u32[]{:S(2)}) collective-permute-start(bf16[128,1024]{1,0:T(8,128)(2,1)} %get-tuple-element.54), channel_id=1, source_target_pairs={{0,6},{2,0},{4,2},{6,4},{1,7},{3,1},{5,3},{7,5},{8,14},{10,8},{12,... | collective-permute-start | bytes 786440 | tf_op jit(solution)/shard_map/ppermute | solution.py:256
  27.8 5.9 %shard_map.76 = (bf16[2048,576]{1,0:T(8,128)(2,1)}, bf16[1024,576]{1,0:T(8,128)(2,1)}) custom-call(s32[4]{0:T(128)} %pad_add_fusion.here, bf16[576,4096]{1,0:T(8,128)(2,1)} %collective-permute-done.3.pre, bf16[576,1024]{1,0:T(8,128)(2,1)} %collective-permute-done.4.cot), custom_call_target="tpu_custom_call" | custom-call | flops 70778880 | bytes 5242880 | tf_op jit(solution)/shard_map/pallas_call | solution.py:73
  33.7 0.0 collective-permute-done.5.refs_11_
  33.7 2.6 %collective-permute-done.6.refs_12_ = bf16[128,1024]{1,0:T(8,128)(2,1)S(1)} collective-permute-done((bf16[128,1024]{1,0:T(8,128)(2,1)}, bf16[128,1024]{1,0:T(8,128)(2,1)S(1)}, u32[]{:S(2)}, u32[]{:S(2)}) %collective-permute-start.6) | collective-permute-done | bytes 262176 | tf_op jit(solution)/shard_map/ppermute | solution.py:256
  36.4 0.0 collective-permute-done.8.refs_3_
  36.4 0.0 collective-permute-done.7.refs_7_
  36.4 0.7 copy-done.8
  37.1 2.7 %collective-permute-start.9 = (bf16[256,1024]{1,0:T(8,128)(2,1)}, bf16[256,1024]{1,0:T(8,128)(2,1)S(1)}, u32[]{:S(2)}, u32[]{:S(2)}) collective-permute-start(bf16[256,1024]{1,0:T(8,128)(2,1)} %collective-permute-done.2.refs_8_), channel_id=1, source_target_pairs={{0,6},{2,0},{4,2},{6,4},{1,7},{3,1},{5,3},{7,5},{8,14},{10,8},{12,... | collective-permute-start | bytes 1572872 | tf_op jit(solution)/shard_map/ppermute | solution.py:256
  39.8 2.6 %collective-permute-start.11 = (bf16[128,1024]{1,0:T(8,128)(2,1)S(1)}, bf16[128,1024]{1,0:T(8,128)(2,1)S(1)}, u32[]{:S(2)}, u32[]{:S(2)}) collective-permute-start(bf16[128,1024]{1,0:T(8,128)(2,1)S(1)} %collective-permute-done.5.refs_11_), channel_id=1, source_target_pairs={{0,65},{1,64},{64,1},{65,0},{2,67},{3,66},{66,3},{67,2},{4,69},{5,... | collective-permute-start | bytes 786440 | tf_op jit(solution)/shard_map/ppermute | solution.py:253
  42.4 0.1 collective-permute-start.12
  42.5 12.9 %shard_map.77 = (bf16[4,2,256,128]{3,2,1,0:T(8,128)(2,1)}, bf16[4,2,256,128]{3,2,1,0:T(8,128)(2,1)}, bf16[4,2,256,128]{3,2,1,0:T(8,128)(2,1)}, bf16[4,2,256,128]{3,2,1,0:T(8,128)(2,1)}) custom-call(s32[4]{0:T(128)} %pad_add_fusion.here, bf16[1024,576]{1,0:T(8,128)(2,1)} %get-tuple-element.51.refs_0_, bf16[1024,576]{1,0:T(8,128)(2,1)} %get-tuple-element.63.refs_1_, ...), custom_call_target="tpu_custom_call" | custom-call | flops 19327352832 | bytes 12582912 | tf_op jit(solution)/shard_map/pallas_call | solution.py:193
  55.4 1.3 collective-permute-start.13
  56.7 2.4 %collective-permute-start.14 = (bf16[4,2,256,128]{3,2,1,0:T(8,128)(2,1)}, bf16[4,2,256,128]{3,2,1,0:T(8,128)(2,1)}, u32[]{:S(2)}, u32[]{:S(2)}) collective-permute-start(bf16[4,2,256,128]{3,2,1,0:T(8,128)(2,1)} %get-tuple-element.79), channel_id=1, source_target_pairs={{0,32},{16,48},{32,0},{48,16},{1,33},{17,49},{33,1},{49,17},{2,34}... | collective-permute-start | bytes 1572872 | tf_op jit(solution)/shard_map/ppermute | solution.py:256
  59.2 1.2 collective-permute-start.15
  60.3 5.6 %shard_map.80 = bf16[8,256,128]{2,1,0:T(8,128)(2,1)} custom-call(s32[4]{0:T(128)} %pad_add_fusion.here, bf16[1024,576]{1,0:T(8,128)(2,1)} %get-tuple-element.51.refs_0_, bf16[1024,576]{1,0:T(8,128)(2,1)} %get-tuple-element.63.refs_1_, bf16[576,1024]{1,0:T(8,128)(2,1)} %refs_2_.7, bf16[576,1024]{1,0:T(8,128)(2,1)} %collective-permute-done.8.refs_3_, ...), custom_call_target="tpu_custom_call" | custom-call | flops 1207959552 | bytes 3145728 | tf_op jit(solution)/shard_map/pallas_call | solution.py:193
  65.9 0.3 collective-permute-start.17
  66.3 8.0 %shard_map.79 = (bf16[8,256,128]{2,1,0:T(8,128)(2,1)}, bf16[8,256,128]{2,1,0:T(8,128)(2,1)}) custom-call(s32[4]{0:T(128)} %pad_add_fusion.here, bf16[1024,576]{1,0:T(8,128)(2,1)} %get-tuple-element.51.refs_0_, bf16[1024,576]{1,0:T(8,128)(2,1)} %get-tuple-element.63.refs_1_, bf16[576,1024]{1,0:T(8,128)(2,1)} %refs_2_.7, ...), custom_call_target="tpu_custom_call" | custom-call | flops 2415919104 | bytes 6291456 | tf_op jit(solution)/shard_map/pallas_call | solution.py:193
  74.2 0.7 collective-permute-start.16
  74.9 2.1 %collective-permute-start.18 = (bf16[8,256,128]{2,1,0:T(8,128)(2,1)}, bf16[8,256,128]{2,1,0:T(8,128)(2,1)}, u32[]{:S(2)}, u32[]{:S(2)}) collective-permute-start(bf16[8,256,128]{2,1,0:T(8,128)(2,1)} %get-tuple-element.86), channel_id=1, source_target_pairs={{0,6},{2,0},{4,2},{6,4},{1,7},{3,1},{5,3},{7,5},{8,14},{10,8},{12,... | collective-permute-start | bytes 1572872 | tf_op jit(solution)/shard_map/ppermute | solution.py:256
  77.0 3.0 %collective-permute-done.14 = bf16[4,2,256,128]{3,2,1,0:T(8,128)(2,1)} collective-permute-done((bf16[4,2,256,128]{3,2,1,0:T(8,128)(2,1)}, bf16[4,2,256,128]{3,2,1,0:T(8,128)(2,1)}, u32[]{:S(2)}, u32[]{:S(2)}) %collective-permute-start.14) | collective-permute-done | bytes 524320 | tf_op jit(solution)/shard_map/ppermute | solution.py:256
  80.0 1.7 %collective-permute-done.15 = bf16[4,2,256,128]{3,2,1,0:T(8,128)(2,1)} collective-permute-done((bf16[4,2,256,128]{3,2,1,0:T(8,128)(2,1)}, bf16[4,2,256,128]{3,2,1,0:T(8,128)(2,1)}, u32[]{:S(2)}, u32[]{:S(2)}) %collective-permute-start.15) | collective-permute-done | bytes 524320 | tf_op jit(solution)/shard_map/ppermute | solution.py:256
  81.7 2.4 %add_convert_fusion.1 = bf16[4,2,256,128]{3,2,1,0:T(8,128)(2,1)} fusion(bf16[4,2,256,128]{3,2,1,0:T(8,128)(2,1)} %collective-permute-done.15, bf16[4,2,256,128]{3,2,1,0:T(8,128)(2,1)} %collective-permute-done.14, bf16[4,2,256,128]{3,2,1,0:T(8,128)(2,1)} %collective-permute-done.13, bf16[4,2,256,128]{3,2,1,0:T(8,128)(2,1)S(1)} %copy-done.2), kind=kLoop, calls=%fused_computation.8 | loop fusion | flops 2097152 | bytes 2621440 | tf_op jit(solution)/shard_map/convert_element_type | solution.py:281
  84.1 3.5 %all-to-all-start = ((bf16[8,256,128]{2,1,0:T(8,128)(2,1)}), bf16[8,256,128]{2,1,0:T(8,128)(2,1)S(1)}, u32[]{:S(2)}, u32[]{:S(2)}) async-start(bf16[8,256,128]{2,1,0:T(8,128)(2,1)} %bitcast.5), calls=%async_computation | async-start | bytes 1048576 | tf_op jit(solution)/shard_map/all_to_all | solution.py:284
  87.6 5.6 %shard_map.78 = bf16[8,256,128]{2,1,0:T(8,128)(2,1)} custom-call(s32[4]{0:T(128)} %pad_add_fusion.here, bf16[1024,576]{1,0:T(8,128)(2,1)} %get-tuple-element.51.refs_0_, bf16[1024,576]{1,0:T(8,128)(2,1)} %get-tuple-element.63.refs_1_, bf16[576,1024]{1,0:T(8,128)(2,1)} %refs_2_.7, bf16[576,1024]{1,0:T(8,128)(2,1)} %collective-permute-done.8.refs_3_, ...), custom_call_target="tpu_custom_call" | custom-call | flops 1207959552 | bytes 3145728 | tf_op jit(solution)/shard_map/pallas_call | solution.py:193
  93.2 2.4 %add_convert_fusion = bf16[8,256,128]{2,1,0:T(8,128)(2,1)} fusion(bf16[8,256,128]{2,1,0:T(8,128)(2,1)} %collective-permute-done.18, bf16[8,256,128]{2,1,0:T(8,128)(2,1)S(1)} %collective-permute-done.17, bf16[8,256,128]{2,1,0:T(8,128)(2,1)} %collective-permute-done.16, bf16[8,256,128]{2,1,0:T(8,128)(2,1)} %shard_map.78), kind=kLoop, calls=%fused_computation.7 | loop fusion | flops 2097152 | bytes 2621440 | tf_op jit(solution)/shard_map/convert_element_type | solution.py:281
  95.7 1.9 %all-to-all-done = bf16[8,256,128]{2,1,0:T(8,128)(2,1)S(1)} async-done(((bf16[8,256,128]{2,1,0:T(8,128)(2,1)}), bf16[8,256,128]{2,1,0:T(8,128)(2,1)S(1)}, u32[]{:S(2)}, u32[]{:S(2)}) %all-to-all-start) | async-done | bytes 524320 | tf_op jit(solution)/shard_map/all_to_all | solution.py:284
  97.5 4.7 %all-to-all-start.1 = ((bf16[8,256,128]{2,1,0:T(8,128)(2,1)}), bf16[8,256,128]{2,1,0:T(8,128)(2,1)S(1)}, u32[]{:S(2)}, u32[]{:S(2)}) async-start(bf16[8,256,128]{2,1,0:T(8,128)(2,1)} %add_convert_fusion), calls=%async_computation.1 | async-start | bytes 1048576 | tf_op jit(solution)/shard_map/all_to_all | solution.py:284
  102.2 0.1 add_convert_fusion.4
  102.3 7.8 %all-to-all-done.1 = bf16[8,256,128]{2,1,0:T(8,128)(2,1)S(1)} async-done(((bf16[8,256,128]{2,1,0:T(8,128)(2,1)}), bf16[8,256,128]{2,1,0:T(8,128)(2,1)S(1)}, u32[]{:S(2)}, u32[]{:S(2)}) %all-to-all-start.1) | async-done | bytes 524320 | tf_op jit(solution)/shard_map/all_to_all | solution.py:284
  110.1 0.1 add_convert_fusion.3
  110.2 1.6 %collective-permute-start.19 = (bf16[2,256,128]{2,1,0:T(8,128)(2,1)S(1)}, bf16[2,256,128]{2,1,0:T(8,128)(2,1)S(1)}, u32[]{:S(2)}, u32[]{:S(2)}) collective-permute-start(bf16[2,256,128]{2,1,0:T(8,128)(2,1)S(1)} %pad_maximum_fusion.1), channel_id=1, source_target_pairs={{0,1},{1,0},{2,3},{3,2},{4,5},{5,4},{6,7},{7,6},{8,9},{9,8},{10,11... | collective-permute-start | bytes 393224 | tf_op jit(solution)/shard_map/ppermute | solution.py:295
  111.8 3.8 %collective-permute-done.19 = bf16[2,256,128]{2,1,0:T(8,128)(2,1)S(1)} collective-permute-done((bf16[2,256,128]{2,1,0:T(8,128)(2,1)S(1)}, bf16[2,256,128]{2,1,0:T(8,128)(2,1)S(1)}, u32[]{:S(2)}, u32[]{:S(2)}) %collective-permute-start.19) | collective-permute-done | bytes 131104 | tf_op jit(solution)/shard_map/ppermute | solution.py:295
  115.6 1.9 %collective-permute-start.20 = (bf16[2,256,128]{2,1,0:T(8,128)(2,1)S(1)}, bf16[2,256,128]{2,1,0:T(8,128)(2,1)S(1)}, u32[]{:S(2)}, u32[]{:S(2)}) collective-permute-start(bf16[2,256,128]{2,1,0:T(8,128)(2,1)S(1)} %add_convert_fusion.2), channel_id=1, source_target_pairs={{0,6},{2,0},{4,2},{6,4},{1,7},{3,1},{5,3},{7,5},{8,14},{10,8},{12,... | collective-permute-start | bytes 393224 | tf_op jit(solution)/shard_map/ppermute | solution.py:256
  117.5 1.7 %collective-permute-start.22 = (bf16[2,256,128]{2,1,0:T(8,128)(2,1)S(1)}, bf16[2,256,128]{2,1,0:T(8,128)(2,1)S(1)}, u32[]{:S(2)}, u32[]{:S(2)}) collective-permute-start(bf16[2,256,128]{2,1,0:T(8,128)(2,1)S(1)} %add_convert_fusion.2), channel_id=1, source_target_pairs={{0,4},{2,6},{4,0},{6,2},{1,5},{3,7},{5,1},{7,3},{8,12},{10,14},{12... | collective-permute-start | bytes 393224 | tf_op jit(solution)/shard_map/ppermute | solution.py:256
  119.3 0.3 collective-permute-done.20
  119.5 4.4 %collective-permute-done.21 = bf16[2,256,128]{2,1,0:T(8,128)(2,1)S(1)} collective-permute-done((bf16[2,256,128]{2,1,0:T(8,128)(2,1)S(1)}, bf16[2,256,128]{2,1,0:T(8,128)(2,1)S(1)}, u32[]{:S(2)}, u32[]{:S(2)}) %collective-permute-start.21) | collective-permute-done | bytes 131104 | tf_op jit(solution)/shard_map/ppermute | solution.py:256
  124.0 0.1 pad_maximum_fusion
  124.0 2.3 %fusion.9 = f32[2,256,128]{2,1,0:T(8,128)S(1)} fusion(bf16[2,256,2048]{2,1,0:T(8,128)(2,1)} %bitcast.21, bf16[2048,128,1]{1,0,2:T(8,128)(2,1)S(1)} %bitcast.22), kind=kOutput, calls=%fused_computation.21 | convolution fusion | flops 268435456 | bytes 2883584 | tf_op jit(solution)/shard_map/dot_general | solution.py:298
  126.4 5.0 %collective-permute-start.23 = (f32[256,128]{1,0:T(8,128)S(1)}, f32[256,128]{1,0:T(8,128)S(1)}, u32[]{:S(2)}, u32[]{:S(2)}) collective-permute-start(f32[256,128]{1,0:T(8,128)S(1)} %dynamic-slice_bitcast_fusion), channel_id=1, source_target_pairs={{0,8},{8,0},{1,9},{9,1},{2,10},{10,2},{3,11},{11,3},{4,12},{12,4},... | collective-permute-start | bytes 393224 | tf_op jit(solution)/shard_map/ppermute | solution.py:250
  131.4 1.0 collective-permute-done.23
  132.4 0.1 broadcast_in_dim.2
  132.5 12.0 %all_to_all.15 = bf16[8,256,128]{2,1,0:T(8,128)(2,1)S(1)} all-to-all(bf16[8,256,128]{2,1,0:T(8,128)(2,1)S(1)} %broadcast_in_dim.2), channel_id=1, replica_groups=mesh['zl'=2,'x'=4,'c'=2,'y'=4,'zh'=2] {'x','zl'}, dimensions={0} | all-to-all | bytes 1048576 | tf_op jit(solution)/shard_map/all_to_all | solution.py:303
  144.5 0.2 copy.8
  144.7 2.1 %collective-permute-start.24 = (bf16[256,1024]{0,1:T(8,128)(2,1)S(1)}, bf16[256,1024]{0,1:T(8,128)(2,1)S(1)}, u32[]{:S(2)}, u32[]{:S(2)}) collective-permute-start(bf16[256,1024]{0,1:T(8,128)(2,1)S(1)} %bitcast.23), channel_id=1, source_target_pairs={{0,8},{8,0},{1,9},{9,1},{2,10},{10,2},{3,11},{11,3},{4,12},{12,4},... | collective-permute-start | bytes 1572872 | tf_op jit(solution)/shard_map/ppermute | solution.py:250
  146.9 1.5 %collective-permute-done.24 = bf16[256,1024]{0,1:T(8,128)(2,1)S(1)} collective-permute-done((bf16[256,1024]{0,1:T(8,128)(2,1)S(1)}, bf16[256,1024]{0,1:T(8,128)(2,1)S(1)}, u32[]{:S(2)}, u32[]{:S(2)}) %collective-permute-start.24) | collective-permute-done | bytes 524320 | tf_op jit(solution)/shard_map/ppermute | solution.py:250
  148.4 2.6 %fusion = f32[512,1024]{1,0:T(8,128)} fusion(bf16[1024,1024]{1,0:T(8,128)(2,1)S(1)} %copy-done, bf16[256,1024]{0,1:T(8,128)(2,1)S(1)} %collective-permute-done.24, bf16[256,1024]{0,1:T(8,128)(2,1)S(1)} %bitcast.24, pred[]{:T(512)S(6)} %eq.3), kind=kOutput, calls=%fused_computation.1 | convolution fusion | flops 1078460416 | bytes 5242881 | tf_op jit(solution)/shard_map/dot_general | solution.py:308
  (32 shorter events, 0.2 us)
Async XLA Ops:
  0.0 148.4 %copy-start = (bf16[1024,1024]{1,0:T(8,128)(2,1)S(1)}, bf16[1024,1024]{1,0:T(8,128)(2,1)}, u32[]{:S(2)}) copy-start(bf16[1024,1024]{1,0:T(8,128)(2,1)} %param.12) | copy-start | bytes 6291460
  0.0 21.8 %collective-permute-start.3 = (bf16[576,4096]{1,0:T(8,128)(2,1)}, bf16[576,4096]{1,0:T(8,128)(2,1)}, u32[]{:S(2)}, u32[]{:S(2)}) collective-permute-start(bf16[576,4096]{1,0:T(8,128)(2,1)} %pre.1), channel_id=1, source_target_pairs={{0,8},{8,0},{1,9},{9,1},{2,10},{10,2},{3,11},{11,3},{4,12},{12,4},... | collective-permute-start | bytes 14155784 | tf_op jit(solution)/shard_map/ppermute | solution.py:250
  1.4 20.4 %collective-permute-start.4 = (bf16[576,1024]{1,0:T(8,128)(2,1)}, bf16[576,1024]{1,0:T(8,128)(2,1)}, u32[]{:S(2)}, u32[]{:S(2)}) collective-permute-start(bf16[576,1024]{1,0:T(8,128)(2,1)} %cot.1), channel_id=1, source_target_pairs={{0,8},{8,0},{1,9},{9,1},{2,10},{10,2},{3,11},{11,3},{4,12},{12,4},... | collective-permute-start | bytes 3538952 | tf_op jit(solution)/shard_map/ppermute | solution.py:250
  3.3 17.9 %collective-permute-start = (bf16[256,1024]{1,0:T(8,128)(2,1)}, bf16[256,1024]{1,0:T(8,128)(2,1)}, u32[]{:S(2)}, u32[]{:S(2)}) collective-permute-start(bf16[256,1024]{1,0:T(8,128)(2,1)} %constant_dynamic-slice_fusion.refs_8_), channel_id=1, source_target_pairs={{0,6},{2,0},{4,2},{6,4},{1,7},{3,1},{5,3},{7,5},{8,14},{10,8},{12,... | collective-permute-start | bytes 1572872 | tf_op jit(solution)/shard_map/ppermute | solution.py:256
  6.2 15.0 %collective-permute-start.1 = (bf16[256,1024]{1,0:T(8,128)(2,1)}, bf16[256,1024]{1,0:T(8,128)(2,1)}, u32[]{:S(2)}, u32[]{:S(2)}) collective-permute-start(bf16[256,1024]{1,0:T(8,128)(2,1)} %constant_dynamic-slice_fusion.refs_8_), channel_id=1, source_target_pairs={{0,2},{2,4},{4,6},{6,0},{1,3},{3,5},{5,7},{7,1},{8,10},{10,12},{12... | collective-permute-start | bytes 1572872 | tf_op jit(solution)/shard_map/ppermute | solution.py:256
  6.2 15.6 %collective-permute-start.2 = (bf16[256,1024]{1,0:T(8,128)(2,1)}, bf16[256,1024]{1,0:T(8,128)(2,1)}, u32[]{:S(2)}, u32[]{:S(2)}) collective-permute-start(bf16[256,1024]{1,0:T(8,128)(2,1)} %constant_dynamic-slice_fusion.refs_8_), channel_id=1, source_target_pairs={{0,65},{1,64},{64,1},{65,0},{2,67},{3,66},{66,3},{67,2},{4,69},{5,... | collective-permute-start | bytes 1572872 | tf_op jit(solution)/shard_map/ppermute | solution.py:253
  14.2 9.0 %copy-start.1 = (bf16[576,1024]{1,0:T(8,128)(2,1)S(1)}, bf16[576,1024]{1,0:T(8,128)(2,1)}, u32[]{:S(2)}) copy-start(bf16[576,1024]{1,0:T(8,128)(2,1)} %refs_2_.7) | copy-start | bytes 3538948
  21.8 14.6 %collective-permute-start.7 = (bf16[2048,1024]{1,0:T(8,128)(2,1)}, bf16[2048,1024]{1,0:T(8,128)(2,1)}, u32[]{:S(2)}, u32[]{:S(2)}) collective-permute-start(bf16[2048,1024]{1,0:T(8,128)(2,1)} %get-tuple-element.56), channel_id=1, source_target_pairs={{0,8},{8,0},{1,9},{9,1},{2,10},{10,2},{3,11},{11,3},{4,12},{12,4},... | collective-permute-start | bytes 12582920 | tf_op jit(solution)/shard_map/ppermute | solution.py:250
  23.2 13.2 %collective-permute-start.8 = (bf16[576,1024]{1,0:T(8,128)(2,1)S(1)}, bf16[576,1024]{1,0:T(8,128)(2,1)}, u32[]{:S(2)}, u32[]{:S(2)}) collective-permute-start(bf16[576,1024]{1,0:T(8,128)(2,1)S(1)} %copy-done.1), channel_id=1, source_target_pairs={{0,8},{8,0},{1,9},{9,1},{2,10},{10,2},{3,11},{11,3},{4,12},{12,4},... | collective-permute-start | bytes 3538952 | tf_op jit(solution)/shard_map/ppermute | solution.py:250
  25.2 8.5 %collective-permute-start.5 = (bf16[128,1024]{1,0:T(8,128)(2,1)}, bf16[128,1024]{1,0:T(8,128)(2,1)S(1)}, u32[]{:S(2)}, u32[]{:S(2)}) collective-permute-start(bf16[128,1024]{1,0:T(8,128)(2,1)} %get-tuple-element.54), channel_id=1, source_target_pairs={{0,6},{2,0},{4,2},{6,4},{1,7},{3,1},{5,3},{7,5},{8,14},{10,8},{12,... | collective-permute-start | bytes 786440 | tf_op jit(solution)/shard_map/ppermute | solution.py:256
  27.8 8.6 %collective-permute-start.6 = (bf16[128,1024]{1,0:T(8,128)(2,1)}, bf16[128,1024]{1,0:T(8,128)(2,1)S(1)}, u32[]{:S(2)}, u32[]{:S(2)}) collective-permute-start(bf16[128,1024]{1,0:T(8,128)(2,1)} %get-tuple-element.55), channel_id=1, source_target_pairs={{0,2},{2,4},{4,6},{6,0},{1,3},{3,5},{5,7},{7,1},{8,10},{10,12},{12... | collective-permute-start | bytes 786440 | tf_op jit(solution)/shard_map/ppermute | solution.py:256
  33.7 8.7 %copy-start.7 = (bf16[128,1024]{1,0:T(8,128)(2,1)}, bf16[128,1024]{1,0:T(8,128)(2,1)S(1)}, u32[]{:S(2)}) copy-start(bf16[128,1024]{1,0:T(8,128)(2,1)S(1)} %collective-permute-done.5.refs_11_) | copy-start | bytes 786436
  36.4 0.7 copy-start.8
  37.1 18.3 %collective-permute-start.10 = (bf16[256,1024]{1,0:T(8,128)(2,1)}, bf16[256,1024]{1,0:T(8,128)(2,1)S(1)}, u32[]{:S(2)}, u32[]{:S(2)}) collective-permute-start(bf16[256,1024]{1,0:T(8,128)(2,1)} %collective-permute-done.2.refs_8_), channel_id=1, source_target_pairs={{0,2},{2,4},{4,6},{6,0},{1,3},{3,5},{5,7},{7,1},{8,10},{10,12},{12... | collective-permute-start | bytes 1572872 | tf_op jit(solution)/shard_map/ppermute | solution.py:256
  37.1 18.3 %collective-permute-start.9 = (bf16[256,1024]{1,0:T(8,128)(2,1)}, bf16[256,1024]{1,0:T(8,128)(2,1)S(1)}, u32[]{:S(2)}, u32[]{:S(2)}) collective-permute-start(bf16[256,1024]{1,0:T(8,128)(2,1)} %collective-permute-done.2.refs_8_), channel_id=1, source_target_pairs={{0,6},{2,0},{4,2},{6,4},{1,7},{3,1},{5,3},{7,5},{8,14},{10,8},{12,... | collective-permute-start | bytes 1572872 | tf_op jit(solution)/shard_map/ppermute | solution.py:256
  39.8 15.6 %collective-permute-start.11 = (bf16[128,1024]{1,0:T(8,128)(2,1)S(1)}, bf16[128,1024]{1,0:T(8,128)(2,1)S(1)}, u32[]{:S(2)}, u32[]{:S(2)}) collective-permute-start(bf16[128,1024]{1,0:T(8,128)(2,1)S(1)} %collective-permute-done.5.refs_11_), channel_id=1, source_target_pairs={{0,65},{1,64},{64,1},{65,0},{2,67},{3,66},{66,3},{67,2},{4,69},{5,... | collective-permute-start | bytes 786440 | tf_op jit(solution)/shard_map/ppermute | solution.py:253
  42.4 13.0 %collective-permute-start.12 = (bf16[128,1024]{1,0:T(8,128)(2,1)}, bf16[128,1024]{1,0:T(8,128)(2,1)S(1)}, u32[]{:S(2)}, u32[]{:S(2)}) collective-permute-start(bf16[128,1024]{1,0:T(8,128)(2,1)} %copy-done.8), channel_id=1, source_target_pairs={{0,65},{1,64},{64,1},{65,0},{2,67},{3,66},{66,3},{67,2},{4,69},{5,... | collective-permute-start | bytes 786440 | tf_op jit(solution)/shard_map/ppermute | solution.py:253
  55.4 5.0 %copy-start.5 = (bf16[128,1024]{1,0:T(8,128)(2,1)}, bf16[128,1024]{1,0:T(8,128)(2,1)S(1)}, u32[]{:S(2)}) copy-start(bf16[128,1024]{1,0:T(8,128)(2,1)S(1)} %collective-permute-done.11.refs_8_) | copy-start | bytes 786436
  55.4 4.9 %copy-start.6 = (bf16[128,1024]{1,0:T(8,128)(2,1)}, bf16[128,1024]{1,0:T(8,128)(2,1)S(1)}, u32[]{:S(2)}) copy-start(bf16[128,1024]{1,0:T(8,128)(2,1)S(1)} %collective-permute-done.12.refs_9_) | copy-start | bytes 786436
  55.4 10.5 %copy-start.3 = (bf16[256,1024]{1,0:T(8,128)(2,1)}, bf16[256,1024]{1,0:T(8,128)(2,1)S(1)}, u32[]{:S(2)}) copy-start(bf16[256,1024]{1,0:T(8,128)(2,1)S(1)} %collective-permute-done.10.refs_9_) | copy-start | bytes 1572868
  55.4 4.9 %copy-start.4 = (bf16[256,1024]{1,0:T(8,128)(2,1)}, bf16[256,1024]{1,0:T(8,128)(2,1)S(1)}, u32[]{:S(2)}) copy-start(bf16[256,1024]{1,0:T(8,128)(2,1)S(1)} %collective-permute-done.9.refs_8_) | copy-start | bytes 1572868
  55.4 19.5 %collective-permute-start.13 = (bf16[4,2,256,128]{3,2,1,0:T(8,128)(2,1)}, bf16[4,2,256,128]{3,2,1,0:T(8,128)(2,1)}, u32[]{:S(2)}, u32[]{:S(2)}) collective-permute-start(bf16[4,2,256,128]{3,2,1,0:T(8,128)(2,1)} %get-tuple-element.78), channel_id=1, source_target_pairs={{0,16},{16,32},{32,48},{48,0},{1,17},{17,33},{33,49},{49,1},{2,18}... | collective-permute-start | bytes 1572872 | tf_op jit(solution)/shard_map/ppermute | solution.py:256
  56.7 23.3 %collective-permute-start.14 = (bf16[4,2,256,128]{3,2,1,0:T(8,128)(2,1)}, bf16[4,2,256,128]{3,2,1,0:T(8,128)(2,1)}, u32[]{:S(2)}, u32[]{:S(2)}) collective-permute-start(bf16[4,2,256,128]{3,2,1,0:T(8,128)(2,1)} %get-tuple-element.79), channel_id=1, source_target_pairs={{0,32},{16,48},{32,0},{48,16},{1,33},{17,49},{33,1},{49,17},{2,34}... | collective-permute-start | bytes 1572872 | tf_op jit(solution)/shard_map/ppermute | solution.py:256
  59.2 22.5 %collective-permute-start.15 = (bf16[4,2,256,128]{3,2,1,0:T(8,128)(2,1)}, bf16[4,2,256,128]{3,2,1,0:T(8,128)(2,1)}, u32[]{:S(2)}, u32[]{:S(2)}) collective-permute-start(bf16[4,2,256,128]{3,2,1,0:T(8,128)(2,1)} %get-tuple-element.80), channel_id=1, source_target_pairs={{0,48},{16,0},{32,16},{48,32},{1,49},{17,1},{33,17},{49,33},{2,50}... | collective-permute-start | bytes 1572872 | tf_op jit(solution)/shard_map/ppermute | solution.py:256
  65.9 15.7 %copy-start.2 = (bf16[4,2,256,128]{3,2,1,0:T(8,128)(2,1)S(1)}, bf16[4,2,256,128]{3,2,1,0:T(8,128)(2,1)}, u32[]{:S(2)}) copy-start(bf16[4,2,256,128]{3,2,1,0:T(8,128)(2,1)} %get-tuple-element.77) | copy-start | bytes 1572868
  65.9 27.2 %collective-permute-start.17 = (bf16[8,256,128]{2,1,0:T(8,128)(2,1)}, bf16[8,256,128]{2,1,0:T(8,128)(2,1)S(1)}, u32[]{:S(2)}, u32[]{:S(2)}) collective-permute-start(bf16[8,256,128]{2,1,0:T(8,128)(2,1)} %shard_map.80), channel_id=1, source_target_pairs={{0,4},{2,6},{4,0},{6,2},{1,5},{3,7},{5,1},{7,3},{8,12},{10,14},{12... | collective-permute-start | bytes 1572872 | tf_op jit(solution)/shard_map/ppermute | solution.py:256
  74.2 19.0 %collective-permute-start.16 = (bf16[8,256,128]{2,1,0:T(8,128)(2,1)}, bf16[8,256,128]{2,1,0:T(8,128)(2,1)}, u32[]{:S(2)}, u32[]{:S(2)}) collective-permute-start(bf16[8,256,128]{2,1,0:T(8,128)(2,1)} %get-tuple-element.83), channel_id=1, source_target_pairs={{0,2},{2,4},{4,6},{6,0},{1,3},{3,5},{5,7},{7,1},{8,10},{10,12},{12... | collective-permute-start | bytes 1572872 | tf_op jit(solution)/shard_map/ppermute | solution.py:256
  74.9 18.3 %collective-permute-start.18 = (bf16[8,256,128]{2,1,0:T(8,128)(2,1)}, bf16[8,256,128]{2,1,0:T(8,128)(2,1)}, u32[]{:S(2)}, u32[]{:S(2)}) collective-permute-start(bf16[8,256,128]{2,1,0:T(8,128)(2,1)} %get-tuple-element.86), channel_id=1, source_target_pairs={{0,6},{2,0},{4,2},{6,4},{1,7},{3,1},{5,3},{7,5},{8,14},{10,8},{12,... | collective-permute-start | bytes 1572872 | tf_op jit(solution)/shard_map/ppermute | solution.py:256
  84.1 13.4 %all-to-all-start = ((bf16[8,256,128]{2,1,0:T(8,128)(2,1)}), bf16[8,256,128]{2,1,0:T(8,128)(2,1)S(1)}, u32[]{:S(2)}, u32[]{:S(2)}) async-start(bf16[8,256,128]{2,1,0:T(8,128)(2,1)} %bitcast.5), calls=%async_computation | async-start | bytes 1048576 | tf_op jit(solution)/shard_map/all_to_all | solution.py:284
  97.5 12.6 %all-to-all-start.1 = ((bf16[8,256,128]{2,1,0:T(8,128)(2,1)}), bf16[8,256,128]{2,1,0:T(8,128)(2,1)S(1)}, u32[]{:S(2)}, u32[]{:S(2)}) async-start(bf16[8,256,128]{2,1,0:T(8,128)(2,1)} %add_convert_fusion), calls=%async_computation.1 | async-start | bytes 1048576 | tf_op jit(solution)/shard_map/all_to_all | solution.py:284
  110.2 5.4 %collective-permute-start.19 = (bf16[2,256,128]{2,1,0:T(8,128)(2,1)S(1)}, bf16[2,256,128]{2,1,0:T(8,128)(2,1)S(1)}, u32[]{:S(2)}, u32[]{:S(2)}) collective-permute-start(bf16[2,256,128]{2,1,0:T(8,128)(2,1)S(1)} %pad_maximum_fusion.1), channel_id=1, source_target_pairs={{0,1},{1,0},{2,3},{3,2},{4,5},{5,4},{6,7},{7,6},{8,9},{9,8},{10,11... | collective-permute-start | bytes 393224 | tf_op jit(solution)/shard_map/ppermute | solution.py:295
  115.6 3.9 %collective-permute-start.20 = (bf16[2,256,128]{2,1,0:T(8,128)(2,1)S(1)}, bf16[2,256,128]{2,1,0:T(8,128)(2,1)S(1)}, u32[]{:S(2)}, u32[]{:S(2)}) collective-permute-start(bf16[2,256,128]{2,1,0:T(8,128)(2,1)S(1)} %add_convert_fusion.2), channel_id=1, source_target_pairs={{0,6},{2,0},{4,2},{6,4},{1,7},{3,1},{5,3},{7,5},{8,14},{10,8},{12,... | collective-permute-start | bytes 393224 | tf_op jit(solution)/shard_map/ppermute | solution.py:256
  117.5 6.4 %collective-permute-start.21 = (bf16[2,256,128]{2,1,0:T(8,128)(2,1)S(1)}, bf16[2,256,128]{2,1,0:T(8,128)(2,1)S(1)}, u32[]{:S(2)}, u32[]{:S(2)}) collective-permute-start(bf16[2,256,128]{2,1,0:T(8,128)(2,1)S(1)} %add_convert_fusion.2), channel_id=1, source_target_pairs={{0,2},{2,4},{4,6},{6,0},{1,3},{3,5},{5,7},{7,1},{8,10},{10,12},{12... | collective-permute-start | bytes 393224 | tf_op jit(solution)/shard_map/ppermute | solution.py:256
  117.5 6.4 %collective-permute-start.22 = (bf16[2,256,128]{2,1,0:T(8,128)(2,1)S(1)}, bf16[2,256,128]{2,1,0:T(8,128)(2,1)S(1)}, u32[]{:S(2)}, u32[]{:S(2)}) collective-permute-start(bf16[2,256,128]{2,1,0:T(8,128)(2,1)S(1)} %add_convert_fusion.2), channel_id=1, source_target_pairs={{0,4},{2,6},{4,0},{6,2},{1,5},{3,7},{5,1},{7,3},{8,12},{10,14},{12... | collective-permute-start | bytes 393224 | tf_op jit(solution)/shard_map/ppermute | solution.py:256
  126.4 6.0 %collective-permute-start.23 = (f32[256,128]{1,0:T(8,128)S(1)}, f32[256,128]{1,0:T(8,128)S(1)}, u32[]{:S(2)}, u32[]{:S(2)}) collective-permute-start(f32[256,128]{1,0:T(8,128)S(1)} %dynamic-slice_bitcast_fusion), channel_id=1, source_target_pairs={{0,8},{8,0},{1,9},{9,1},{2,10},{10,2},{3,11},{11,3},{4,12},{12,4},... | collective-permute-start | bytes 393224 | tf_op jit(solution)/shard_map/ppermute | solution.py:250
  144.7 3.7 %collective-permute-start.24 = (bf16[256,1024]{0,1:T(8,128)(2,1)S(1)}, bf16[256,1024]{0,1:T(8,128)(2,1)S(1)}, u32[]{:S(2)}, u32[]{:S(2)}) collective-permute-start(bf16[256,1024]{0,1:T(8,128)(2,1)S(1)} %bitcast.23), channel_id=1, source_target_pairs={{0,8},{8,0},{1,9},{9,1},{2,10},{10,2},{3,11},{11,3},{4,12},{12,4},... | collective-permute-start | bytes 1572872 | tf_op jit(solution)/shard_map/ppermute | solution.py:250

commit v4 on v3

--- a/solution.py
+++ b/solution.py
@@ -111,10 +111,10 @@
 def term_kernel(by_columns, part, here, *refs):
     n = len(part)
     cot, cot_o, inp, inp_o, slope, slope_o, ef, ef_o = refs[:8]
-    n_out = 4 if by_columns else n
+    n_out = 1 if by_columns else n
     ws, outs = refs[8 : -8 - n_out], refs[-8 - n_out : -8]
     w_v, cot_v, inp_v, slope_v, ef_v, out_v, sem, out_sem = refs[-8:]
-    core, x, y, zh = (here[k] for k in range(4))
+    core, _, y, zh = (here[k] for k in range(4))
     blocks = [lax.rem(y + dy, 4) * 2 + (1 - zh if dz else zh) for dy, dz in part]
 
     def rows(ref, block):
@@ -160,10 +160,7 @@
                 reads["inp" + suffix].wait()
             reads["ef" + suffix, i].wait()
         for j in range(4):
-            if by_columns:
-                cols = pl.ds(pl.multiple_of(lax.rem(x + j, 4) * 256, 256), 256)
-            else:
-                cols = slice(j * 256, (j + 1) * 256)
+            cols = slice(j * 256, (j + 1) * 256)
             total = ef_v[i, 0, :, cols].astype(F32) + ef_v[i, 1, :, cols].astype(F32)
             for k in range(2):
                 total += jnp.dot(hidden[k], inp_v[k, :, cols], preferred_element_type=F32)
@@ -173,7 +170,7 @@
             if by_columns:
                 writes.append(
                     pltpu.make_async_copy(
-                        out_v.at[i, pl.ds(2 * j, 2)], outs[j].at[lax.rem(y + part[i][0], 4)], out_sem.at[len(writes)]
+                        out_v.at[i, pl.ds(2 * j, 2)], outs[0].at[j, pl.ds(0, 2), i], out_sem.at[len(writes)]
                     )
                 )
                 writes[-1].start()
@@ -187,7 +184,7 @@
 def terms(by_columns, part, here, cot, cot_o, inp, inp_o, slope, slope_o, ef, ef_o, ws):
     n = len(part)
     if by_columns:
-        out_shape = [jax.ShapeDtypeStruct((n, 2, 256, 128), BF)] * 4
+        out_shape = [jax.ShapeDtypeStruct((4, 2, n, 256, 128), BF)]
     else:
         out_shape = [jax.ShapeDtypeStruct((8, 256, 128), BF)] * n
     return pl.pallas_call(
@@ -243,7 +240,7 @@
 
 
 def shards(inputs, cotangent, pre_gelu, w_down, error_feedback, a_inverse, g_inverse):
-    c, x, y, zh = (lax.axis_index(a) for a in ("c", "x", "y", "zh"))
+    c, x, y, zh, zl = (lax.axis_index(a) for a in ("c", "x", "y", "zh", "zl"))
     here = jnp.stack([c, x, y, zh]).astype(jnp.int32)
 
     def swap(a):
@@ -280,18 +277,22 @@
     def added(parts):
         return sum(p.astype(F32) for p in parts).astype(BF)
 
+    def half(a, which):
+        return lax.dynamic_index_in_dim(a, which, 0, keepdims=False)
+
     def exchanged(a, axes):
         return lax.all_to_all(a.reshape(8, 256, 128), axes, 0, 0, tiled=True)
 
-    near = product(True, ((0, 0), (1, 0), (3, 0), (2, 0)), [w_own, w_up, w_low, upper, lower])
+    (near,) = product(True, ((0, 0), (1, 0), (3, 0), (2, 0)), [w_own, w_up, w_low, upper, lower])
     near, third = lax.optimization_barrier((near, third))
-    near = added([near[0]] + [ring(near[j], "x", j) for j in (1, 2, 3)])
+    near = added(lax.all_to_all(near, "x", 0, 0, tiled=True))
+    near = added([half(near, zl), lax.ppermute(half(near, 1 - zl), "zl", [(0, 1), (1, 0)])])
+    near = added([near[0], ring(near[1], "y", 1), ring(near[2], "y", -1), ring(near[3], "y", 2)])
     (far,) = product(False, ((2, 1),), third[2:])
     up, low = product(False, ((1, 1), (3, 1)), [third[0], third[1]])
     (own,) = product(False, ((0, 1),), [w_z])
     others = added([own, ring(up, "y", 1), ring(far, "y", 2), ring(low, "y", -1)])
-    near, others = lax.optimization_barrier((exchanged(near, ("y", "zl")), others))
-    near, others = added(near), added(exchanged(others, ("x", "zl")))
+    others = added(exchanged(others, ("x", "zl")))
     theirs = lax.ppermute(jnp.stack([others, near]), "zh", [(0, 1), (1, 0)])
     grad = added([jnp.stack([near, others]), theirs])
     grads = [grad, ring(grad, "y", -1), ring(grad, "y", 1), ring(grad, "y", 2)]

time: 152 us -> 151 us (level)
  waiting for transfers between devices: 28.7 us -> 25.2 us
  blocking collectives: 12 us -> 13.6 us
    all_to_all x2 -> x1, waiting for transfers between devices: 9.68 us -> 3.32 us  [exchanged(): return lax.all_to_all(a.reshape(8, 256, 128), axes, 0, 0, tiled=True)]
    all_to_all x0 -> x1, starting transfers between devices: none -> 4.45 us  [shards(): near = added(lax.all_to_all(near, 'x', 0, 0, tiled=True))]
    all_to_all x2 -> x1, starting transfers between devices: 8.17 us -> 4.05 us  [exchanged(): return lax.all_to_all(a.reshape(8, 256, 128), axes, 0, 0, tiled=True)]
    ppermute x15, starting transfers between devices: 19.8 us -> 16.1 us  [ring(): return lax.ppermute(a, axis, [(i, (i + step) % 4) for i in range(4)])]
    ppermute x15, waiting for transfers between devices: 12.1 us -> 14.8 us  [ring(): return lax.ppermute(a, axis, [(i, (i + step) % 4) for i in range(4)])]
    ppermute x1, starting transfers between devices: 1.65 us -> 3.59 us  [shards(): theirs = lax.ppermute(jnp.stack([others, near]), 'zh', [(0, 1), (1, 0)])]
    another operation x0 -> x2, other arithmetic: none -> 1.83 us
    all_to_all x1, blocking collectives: 12 us -> 13.6 us  [shards(): lax.all_to_all(jnp.broadcast_to(left[None], (8, 256, 128)), ('x', 'zl'),...]
  transfers between devices with their start and end apart: 27 -> 28, of which waited for: 11 -> 12; matrix products, arithmetic and copies ran while one was open for 5% -> 5% of each run, Pallas kernels for 33% -> 33%
where the time goes in v4:
time: 151 us; the launch traced here: 150 us
  Pallas kernels  50.2 us (33%)
  starting transfers between devices  46.1 us (31%)
  waiting for transfers between devices  25.2 us (17%)
  blocking collectives  13.6 us (9%)
  other arithmetic  6.09 us (4%)
  matrix products  4.89 us (3%)
  local copies, waits for them, and re-layouts  3.96 us (3%)
    pallas_call x4, Pallas kernels, terms(): pl.pallas_call(functools.partial(term_kernel, by_columns, part), in_specs...  31.9 us
    ppermute x15, starting transfers between devices, ring(): return lax.ppermute(a, axis, [(i, (i + step) % 4) for i in range(4)])  16.1 us
    ppermute x15, waiting for transfers between devices, ring(): return lax.ppermute(a, axis, [(i, (i + step) % 4) for i in range(4)])  14.8 us
    all_to_all x1, blocking collectives, shards(): lax.all_to_all(jnp.broadcast_to(left[None], (8, 256, 128)), ('x', 'zl'),...  13.6 us
    pallas_call x2, Pallas kernels, prepare(): pl.pallas_call(prepare_kernel, in_specs=[pl.BlockSpec(memory_space=pltpu....  12.8 us
    ppermute x6, starting transfers between devices, swap(): return lax.ppermute(a, 'c', [(0, 1), (1, 0)])  11.4 us
    ppermute x3, starting transfers between devices, across_z(): return lax.ppermute(a, ('zl', 'zh'), [(i, 3 - i) for i in range(4)])  6.45 us
    all_to_all x1, starting transfers between devices, shards(): near = added(lax.all_to_all(near, 'x', 0, 0, tiled=True))  4.45 us
  transfers between devices with their start and end apart: 28, of which 12 were waited for; matrix products, arithmetic and copies ran while one was open for 5% of the time, Pallas kernels for 33%

profile of v4, /device:TPU:1, one launch (start us, length us, event | category | flops | bytes accessed | tf_op | source)
XLA Modules:
  0.0 150.3 jit_solution(5859267399389911580)
XLA Ops:
  0.0 1.4 collective-permute-start.3
  1.4 0.0 collective-permute-start.4
  1.4 1.9 %constant_dynamic-slice_fusion.refs_8_ = bf16[256,1024]{1,0:T(8,128)(2,1)} fusion(bf16[512,1024]{1,0:T(8,128)(2,1)} %param.10, s32[]{:T(128)S(6)} %select_n.26), kind=kLoop, calls=%fused_computation.29 | loop fusion | bytes 1048580 | tf_op jit(solution)/shard_map/dynamic_slice | solution.py:255
  3.3 2.9 %collective-permute-start = (bf16[256,1024]{1,0:T(8,128)(2,1)}, bf16[256,1024]{1,0:T(8,128)(2,1)}, u32[]{:S(2)}, u32[]{:S(2)}) collective-permute-start(bf16[256,1024]{1,0:T(8,128)(2,1)} %constant_dynamic-slice_fusion.refs_8_), channel_id=1, source_target_pairs={{0,6},{2,0},{4,2},{6,4},{1,7},{3,1},{5,3},{7,5},{8,14},{10,8},{12,... | collective-permute-start | bytes 1572872 | tf_op jit(solution)/shard_map/ppermute | solution.py:253
  6.2 3.8 %collective-permute-start.2 = (bf16[256,1024]{1,0:T(8,128)(2,1)}, bf16[256,1024]{1,0:T(8,128)(2,1)}, u32[]{:S(2)}, u32[]{:S(2)}) collective-permute-start(bf16[256,1024]{1,0:T(8,128)(2,1)} %constant_dynamic-slice_fusion.refs_8_), channel_id=1, source_target_pairs={{0,65},{1,64},{64,1},{65,0},{2,67},{3,66},{66,3},{67,2},{4,69},{5,... | collective-permute-start | bytes 1572872 | tf_op jit(solution)/shard_map/ppermute | solution.py:250
  10.0 0.6 pad_add_fusion.here
  10.5 3.6 %shard_map.74 = bf16[512,2048]{1,0:T(8,128)(2,1)} custom-call(s32[4]{0:T(128)} %pad_add_fusion.here, bf16[512,4096]{1,0:T(8,128)(2,1)} %g.1), custom_call_target="tpu_custom_call" | custom-call | bytes 4194304 | tf_op jit(solution)/shard_map/pallas_call | solution.py:232
  14.1 0.0 copy-start.1
  14.2 6.9 %shard_map.73 = (bf16[2048,576]{1,0:T(8,128)(2,1)}, bf16[1024,576]{1,0:T(8,128)(2,1)}, bf16[2048,1024]{1,0:T(8,128)(2,1)}) custom-call(s32[4]{0:T(128)} %pad_add_fusion.here, bf16[576,4096]{1,0:T(8,128)(2,1)} %pre.1, bf16[576,1024]{1,0:T(8,128)(2,1)} %cot.1, bf16[4096,1024]{1,0:T(8,128)(2,1)} %refs_6_.7), custom_call_target="tpu_custom_call" | custom-call | flops 70778880 | bytes 5242880 | tf_op jit(solution)/shard_map/pallas_call | solution.py:73
  21.1 0.0 collective-permute-done.upper.refs_9_
  21.1 0.0 collective-permute-done.1.lower.refs_10_
  21.1 0.7 collective-permute-done.2.refs_8_
  21.8 1.4 collective-permute-start.7
  23.2 0.1 collective-permute-start.8
  23.3 1.8 %shard_map.75 = (bf16[128,1024]{1,0:T(8,128)(2,1)}, bf16[128,1024]{1,0:T(8,128)(2,1)}) custom-call(bf16[256,1024]{1,0:T(8,128)(2,1)} %collective-permute-done.upper.refs_9_, bf16[256,1024]{1,0:T(8,128)(2,1)} %collective-permute-done.1.lower.refs_10_), custom_call_target="tpu_custom_call" | custom-call | tf_op jit(solution)/shard_map/pallas_call | solution.py:102
  25.2 2.6 %collective-permute-start.5 = (bf16[128,1024]{1,0:T(8,128)(2,1)}, bf16[128,1024]{1,0:T(8,128)(2,1)S(1)}, u32[]{:S(2)}, u32[]{:S(2)}) collective-permute-start(bf16[128,1024]{1,0:T(8,128)(2,1)} %get-tuple-element.45), channel_id=1, source_target_pairs={{0,6},{2,0},{4,2},{6,4},{1,7},{3,1},{5,3},{7,5},{8,14},{10,8},{12,... | collective-permute-start | bytes 786440 | tf_op jit(solution)/shard_map/ppermute | solution.py:253
  27.8 5.9 %shard_map.76 = (bf16[2048,576]{1,0:T(8,128)(2,1)}, bf16[1024,576]{1,0:T(8,128)(2,1)}) custom-call(s32[4]{0:T(128)} %pad_add_fusion.here, bf16[576,4096]{1,0:T(8,128)(2,1)} %collective-permute-done.3.pre, bf16[576,1024]{1,0:T(8,128)(2,1)} %collective-permute-done.4.cot), custom_call_target="tpu_custom_call" | custom-call | flops 70778880 | bytes 5242880 | tf_op jit(solution)/shard_map/pallas_call | solution.py:73
  33.7 2.7 %collective-permute-done.6.refs_12_ = bf16[128,1024]{1,0:T(8,128)(2,1)S(1)} collective-permute-done((bf16[128,1024]{1,0:T(8,128)(2,1)}, bf16[128,1024]{1,0:T(8,128)(2,1)S(1)}, u32[]{:S(2)}, u32[]{:S(2)}) %collective-permute-start.6) | collective-permute-done | bytes 262176 | tf_op jit(solution)/shard_map/ppermute | solution.py:253
  36.4 0.1 collective-permute-start.10
  36.5 2.7 %collective-permute-start.9 = (bf16[256,1024]{1,0:T(8,128)(2,1)}, bf16[256,1024]{1,0:T(8,128)(2,1)S(1)}, u32[]{:S(2)}, u32[]{:S(2)}) collective-permute-start(bf16[256,1024]{1,0:T(8,128)(2,1)} %collective-permute-done.2.refs_8_), channel_id=1, source_target_pairs={{0,6},{2,0},{4,2},{6,4},{1,7},{3,1},{5,3},{7,5},{8,14},{10,8},{12,... | collective-permute-start | bytes 1572872 | tf_op jit(solution)/shard_map/ppermute | solution.py:253
  39.1 2.6 %collective-permute-start.11 = (bf16[128,1024]{1,0:T(8,128)(2,1)S(1)}, bf16[128,1024]{1,0:T(8,128)(2,1)S(1)}, u32[]{:S(2)}, u32[]{:S(2)}) collective-permute-start(bf16[128,1024]{1,0:T(8,128)(2,1)S(1)} %collective-permute-done.5.refs_11_), channel_id=1, source_target_pairs={{0,65},{1,64},{64,1},{65,0},{2,67},{3,66},{66,3},{67,2},{4,69},{5,... | collective-permute-start | bytes 786440 | tf_op jit(solution)/shard_map/ppermute | solution.py:250
  41.8 0.1 collective-permute-start.12
  41.8 12.8 %shard_map.77 = bf16[4,2,4,256,128]{4,3,2,1,0:T(8,128)(2,1)} custom-call(s32[4]{0:T(128)} %pad_add_fusion.here, bf16[1024,576]{1,0:T(8,128)(2,1)} %get-tuple-element.42.refs_0_, bf16[1024,576]{1,0:T(8,128)(2,1)} %get-tuple-element.54.refs_1_, bf16[576,1024]{1,0:T(8,128)(2,1)} %refs_2_.7, bf16[576,1024]{1,0:T(8,128)(2,1)} %collective-permute-done.8.refs_3_, ...), custom_call_target="tpu_custom_call" | custom-call | flops 19327352832 | bytes 12582912 | tf_op jit(solution)/shard_map/pallas_call | solution.py:190
  54.7 0.7 copy-done.6
  55.5 0.0 copy-done.5
  55.5 0.8 copy-done.3
  56.3 0.2 copy-done.4
  56.4 4.4 %all-to-all-start = ((bf16[4,2,4,256,128]{4,3,2,1,0:T(8,128)(2,1)}), bf16[4,2,4,256,128]{4,3,2,1,0:T(8,128)(2,1)}, u32[]{:S(2)}, u32[]{:S(2)}) async-start(bf16[4,2,4,256,128]{4,3,2,1,0:T(8,128)(2,1)} %shard_map.77), calls=%async_computation | async-start | bytes 4194304 | tf_op jit(solution)/shard_map/all_to_all | solution.py:288
  60.9 5.6 %shard_map.80 = bf16[8,256,128]{2,1,0:T(8,128)(2,1)} custom-call(s32[4]{0:T(128)} %pad_add_fusion.here, bf16[1024,576]{1,0:T(8,128)(2,1)} %get-tuple-element.42.refs_0_, bf16[1024,576]{1,0:T(8,128)(2,1)} %get-tuple-element.54.refs_1_, bf16[576,1024]{1,0:T(8,128)(2,1)} %refs_2_.7, bf16[576,1024]{1,0:T(8,128)(2,1)} %collective-permute-done.8.refs_3_, ...), custom_call_target="tpu_custom_call" | custom-call | flops 1207959552 | bytes 3145728 | tf_op jit(solution)/shard_map/pallas_call | solution.py:190
  66.5 0.3 collective-permute-start.18
  66.8 8.0 %shard_map.79 = (bf16[8,256,128]{2,1,0:T(8,128)(2,1)}, bf16[8,256,128]{2,1,0:T(8,128)(2,1)}) custom-call(s32[4]{0:T(128)} %pad_add_fusion.here, bf16[1024,576]{1,0:T(8,128)(2,1)} %get-tuple-element.42.refs_0_, bf16[1024,576]{1,0:T(8,128)(2,1)} %get-tuple-element.54.refs_1_, bf16[576,1024]{1,0:T(8,128)(2,1)} %refs_2_.7, ...), custom_call_target="tpu_custom_call" | custom-call | flops 2415919104 | bytes 6291456 | tf_op jit(solution)/shard_map/pallas_call | solution.py:190
  74.8 0.8 collective-permute-start.17
  75.6 1.9 %collective-permute-start.19 = (bf16[8,256,128]{2,1,0:T(8,128)(2,1)}, bf16[8,256,128]{2,1,0:T(8,128)(2,1)}, u32[]{:S(2)}, u32[]{:S(2)}) collective-permute-start(bf16[8,256,128]{2,1,0:T(8,128)(2,1)} %get-tuple-element.70), channel_id=1, source_target_pairs={{0,6},{2,0},{4,2},{6,4},{1,7},{3,1},{5,3},{7,5},{8,14},{10,8},{12,... | collective-permute-start | bytes 1572872 | tf_op jit(solution)/shard_map/ppermute | solution.py:253
  77.5 5.6 %shard_map.78 = bf16[8,256,128]{2,1,0:T(8,128)(2,1)} custom-call(s32[4]{0:T(128)} %pad_add_fusion.here, bf16[1024,576]{1,0:T(8,128)(2,1)} %get-tuple-element.42.refs_0_, bf16[1024,576]{1,0:T(8,128)(2,1)} %get-tuple-element.54.refs_1_, bf16[576,1024]{1,0:T(8,128)(2,1)} %refs_2_.7, bf16[576,1024]{1,0:T(8,128)(2,1)} %collective-permute-done.8.refs_3_, ...), custom_call_target="tpu_custom_call" | custom-call | flops 1207959552 | bytes 3145728 | tf_op jit(solution)/shard_map/pallas_call | solution.py:190
  83.1 1.5 %all-to-all-done = bf16[4,2,4,256,128]{4,3,2,1,0:T(8,128)(2,1)} async-done(((bf16[4,2,4,256,128]{4,3,2,1,0:T(8,128)(2,1)}), bf16[4,2,4,256,128]{4,3,2,1,0:T(8,128)(2,1)}, u32[]{:S(2)}, u32[]{:S(2)}) %all-to-all-start) | async-done | bytes 2097184 | tf_op jit(solution)/shard_map/all_to_all | solution.py:288
  84.6 1.8 %add_convert_fusion.1 = bf16[1,2,4,256,128]{4,3,2,1,0:T(8,128)(2,1)S(1)} fusion(bf16[4,2,4,256,128]{4,3,2,1,0:T(8,128)(2,1)} %all-to-all-done), kind=kLoop, calls=%fused_computation.8 | loop fusion | flops 2097152 | bytes 2621440 | tf_op jit(solution)/shard_map/convert.2
  86.5 0.1 collective-permute-start.13
  86.6 5.7 %collective-permute-done.17 = bf16[8,256,128]{2,1,0:T(8,128)(2,1)} collective-permute-done((bf16[8,256,128]{2,1,0:T(8,128)(2,1)}, bf16[8,256,128]{2,1,0:T(8,128)(2,1)}, u32[]{:S(2)}, u32[]{:S(2)}) %collective-permute-start.17) | collective-permute-done | bytes 524320 | tf_op jit(solution)/shard_map/ppermute | solution.py:253
  92.3 2.4 %add_convert_fusion = bf16[8,256,128]{2,1,0:T(8,128)(2,1)} fusion(bf16[8,256,128]{2,1,0:T(8,128)(2,1)} %collective-permute-done.19, bf16[8,256,128]{2,1,0:T(8,128)(2,1)} %collective-permute-done.18, bf16[8,256,128]{2,1,0:T(8,128)(2,1)} %collective-permute-done.17, bf16[8,256,128]{2,1,0:T(8,128)(2,1)S(1)} %copy-done.2), kind=kLoop, calls=%fused_computation.7 | loop fusion | flops 2097152 | bytes 2621440 | tf_op jit(solution)/shard_map/convert_element_type | solution.py:278
  94.7 4.0 %all-to-all-start.1 = ((bf16[8,256,128]{2,1,0:T(8,128)(2,1)}), bf16[8,256,128]{2,1,0:T(8,128)(2,1)S(1)}, u32[]{:S(2)}, u32[]{:S(2)}) async-start(bf16[8,256,128]{2,1,0:T(8,128)(2,1)} %add_convert_fusion), calls=%async_computation.1 | async-start | bytes 1048576 | tf_op jit(solution)/shard_map/all_to_all | solution.py:284
  98.8 1.0 fusion.7
  99.9 0.1 collective-permute-start.14
  99.9 2.7 %collective-permute-start.15 = (bf16[256,128]{1,0:T(8,128)(2,1)S(1)}, bf16[256,128]{1,0:T(8,128)(2,1)S(1)}, u32[]{:S(2)}, u32[]{:S(2)}) collective-permute-start(bf16[256,128]{1,0:T(8,128)(2,1)S(1)} %get-tuple-element.73), channel_id=1, source_target_pairs={{0,6},{2,0},{4,2},{6,4},{1,7},{3,1},{5,3},{7,5},{8,14},{10,8},{12,... | collective-permute-start | bytes 196616 | tf_op jit(solution)/shard_map/ppermute | solution.py:253
  102.6 3.3 %all-to-all-done.1 = bf16[8,256,128]{2,1,0:T(8,128)(2,1)S(1)} async-done(((bf16[8,256,128]{2,1,0:T(8,128)(2,1)}), bf16[8,256,128]{2,1,0:T(8,128)(2,1)S(1)}, u32[]{:S(2)}, u32[]{:S(2)}) %all-to-all-start.1) | async-done | bytes 524320 | tf_op jit(solution)/shard_map/all_to_all | solution.py:284
  105.9 0.1 add_convert_fusion.3
  106.0 1.5 collective-permute-done.16
  107.6 3.6 %collective-permute-start.20 = (bf16[2,256,128]{2,1,0:T(8,128)(2,1)S(1)}, bf16[2,256,128]{2,1,0:T(8,128)(2,1)S(1)}, u32[]{:S(2)}, u32[]{:S(2)}) collective-permute-start(bf16[2,256,128]{2,1,0:T(8,128)(2,1)S(1)} %pad_maximum_fusion.1), channel_id=1, source_target_pairs={{0,1},{1,0},{2,3},{3,2},{4,5},{5,4},{6,7},{7,6},{8,9},{9,8},{10,11... | collective-permute-start | bytes 393224 | tf_op jit(solution)/shard_map/ppermute | solution.py:296
  111.2 2.4 %collective-permute-done.20 = bf16[2,256,128]{2,1,0:T(8,128)(2,1)S(1)} collective-permute-done((bf16[2,256,128]{2,1,0:T(8,128)(2,1)S(1)}, bf16[2,256,128]{2,1,0:T(8,128)(2,1)S(1)}, u32[]{:S(2)}, u32[]{:S(2)}) %collective-permute-start.20) | collective-permute-done | bytes 131104 | tf_op jit(solution)/shard_map/ppermute | solution.py:296
  113.6 0.4 collective-permute-start.21
  114.0 1.1 collective-permute-start.22
  115.1 0.5 collective-permute-start.23
  115.6 2.1 %collective-permute-done.21 = bf16[2,256,128]{2,1,0:T(8,128)(2,1)S(1)} collective-permute-done((bf16[2,256,128]{2,1,0:T(8,128)(2,1)S(1)}, bf16[2,256,128]{2,1,0:T(8,128)(2,1)S(1)}, u32[]{:S(2)}, u32[]{:S(2)}) %collective-permute-start.21) | collective-permute-done | bytes 131104 | tf_op jit(solution)/shard_map/ppermute | solution.py:253
  117.7 1.3 collective-permute-done.22
  119.0 1.4 collective-permute-done.23
  120.4 0.1 pad_maximum_fusion
  120.5 2.3 %fusion.14 = f32[2,256,128]{2,1,0:T(8,128)S(1)} fusion(bf16[2,256,2048]{2,1,0:T(8,128)(2,1)} %bitcast.38, bf16[2048,128,1]{1,0,2:T(8,128)(2,1)S(1)} %bitcast.39), kind=kOutput, calls=%fused_computation.32 | convolution fusion | flops 268435456 | bytes 2883584 | tf_op jit(solution)/shard_map/dot_general | solution.py:299
  122.8 6.4 %collective-permute-start.24 = (f32[256,128]{1,0:T(8,128)S(1)}, f32[256,128]{1,0:T(8,128)S(1)}, u32[]{:S(2)}, u32[]{:S(2)}) collective-permute-start(f32[256,128]{1,0:T(8,128)S(1)} %dynamic-slice_bitcast_fusion.1), channel_id=1, source_target_pairs={{0,8},{8,0},{1,9},{9,1},{2,10},{10,2},{3,11},{11,3},{4,12},{12,4},... | collective-permute-start | bytes 393224 | tf_op jit(solution)/shard_map/ppermute | solution.py:247
  129.2 1.0 collective-permute-done.24
  130.2 0.1 broadcast_in_dim.2
  130.3 13.6 %all_to_all.15 = bf16[8,256,128]{2,1,0:T(8,128)(2,1)S(1)} all-to-all(bf16[8,256,128]{2,1,0:T(8,128)(2,1)S(1)} %broadcast_in_dim.2), channel_id=1, replica_groups=mesh['zl'=2,'x'=4,'c'=2,'y'=4,'zh'=2] {'x','zl'}, dimensions={0} | all-to-all | bytes 1048576 | tf_op jit(solution)/shard_map/all_to_all | solution.py:304
  143.8 0.2 copy.8
  144.1 2.1 %collective-permute-start.25 = (bf16[256,1024]{0,1:T(8,128)(2,1)S(1)}, bf16[256,1024]{0,1:T(8,128)(2,1)S(1)}, u32[]{:S(2)}, u32[]{:S(2)}) collective-permute-start(bf16[256,1024]{0,1:T(8,128)(2,1)S(1)} %bitcast.40), channel_id=1, source_target_pairs={{0,8},{8,0},{1,9},{9,1},{2,10},{10,2},{3,11},{11,3},{4,12},{12,4},... | collective-permute-start | bytes 1572872 | tf_op jit(solution)/shard_map/ppermute | solution.py:247
  146.2 1.5 %collective-permute-done.25 = bf16[256,1024]{0,1:T(8,128)(2,1)S(1)} collective-permute-done((bf16[256,1024]{0,1:T(8,128)(2,1)S(1)}, bf16[256,1024]{0,1:T(8,128)(2,1)S(1)}, u32[]{:S(2)}, u32[]{:S(2)}) %collective-permute-start.25) | collective-permute-done | bytes 524320 | tf_op jit(solution)/shard_map/ppermute | solution.py:247
  147.7 2.6 %fusion = f32[512,1024]{1,0:T(8,128)} fusion(bf16[1024,1024]{1,0:T(8,128)(2,1)S(1)} %copy-done, bf16[256,1024]{0,1:T(8,128)(2,1)S(1)} %collective-permute-done.25, bf16[256,1024]{0,1:T(8,128)(2,1)S(1)} %bitcast.41, pred[]{:T(512)S(6)} %eq.3), kind=kOutput, calls=%fused_computation.1 | convolution fusion | flops 1078460416 | bytes 5242881 | tf_op jit(solution)/shard_map/dot_general | solution.py:309
  (37 shorter events, 0.2 us)
Async XLA Ops:
  0.0 147.7 %copy-start = (bf16[1024,1024]{1,0:T(8,128)(2,1)S(1)}, bf16[1024,1024]{1,0:T(8,128)(2,1)}, u32[]{:S(2)}) copy-start(bf16[1024,1024]{1,0:T(8,128)(2,1)} %param.12) | copy-start | bytes 6291460
  0.0 21.8 %collective-permute-start.3 = (bf16[576,4096]{1,0:T(8,128)(2,1)}, bf16[576,4096]{1,0:T(8,128)(2,1)}, u32[]{:S(2)}, u32[]{:S(2)}) collective-permute-start(bf16[576,4096]{1,0:T(8,128)(2,1)} %pre.1), channel_id=1, source_target_pairs={{0,8},{8,0},{1,9},{9,1},{2,10},{10,2},{3,11},{11,3},{4,12},{12,4},... | collective-permute-start | bytes 14155784 | tf_op jit(solution)/shard_map/ppermute | solution.py:247
  1.4 20.4 %collective-permute-start.4 = (bf16[576,1024]{1,0:T(8,128)(2,1)}, bf16[576,1024]{1,0:T(8,128)(2,1)}, u32[]{:S(2)}, u32[]{:S(2)}) collective-permute-start(bf16[576,1024]{1,0:T(8,128)(2,1)} %cot.1), channel_id=1, source_target_pairs={{0,8},{8,0},{1,9},{9,1},{2,10},{10,2},{3,11},{11,3},{4,12},{12,4},... | collective-permute-start | bytes 3538952 | tf_op jit(solution)/shard_map/ppermute | solution.py:247
  3.3 17.8 %collective-permute-start = (bf16[256,1024]{1,0:T(8,128)(2,1)}, bf16[256,1024]{1,0:T(8,128)(2,1)}, u32[]{:S(2)}, u32[]{:S(2)}) collective-permute-start(bf16[256,1024]{1,0:T(8,128)(2,1)} %constant_dynamic-slice_fusion.refs_8_), channel_id=1, source_target_pairs={{0,6},{2,0},{4,2},{6,4},{1,7},{3,1},{5,3},{7,5},{8,14},{10,8},{12,... | collective-permute-start | bytes 1572872 | tf_op jit(solution)/shard_map/ppermute | solution.py:253
  6.2 14.9 %collective-permute-start.1 = (bf16[256,1024]{1,0:T(8,128)(2,1)}, bf16[256,1024]{1,0:T(8,128)(2,1)}, u32[]{:S(2)}, u32[]{:S(2)}) collective-permute-start(bf16[256,1024]{1,0:T(8,128)(2,1)} %constant_dynamic-slice_fusion.refs_8_), channel_id=1, source_target_pairs={{0,2},{2,4},{4,6},{6,0},{1,3},{3,5},{5,7},{7,1},{8,10},{10,12},{12... | collective-permute-start | bytes 1572872 | tf_op jit(solution)/shard_map/ppermute | solution.py:253
  6.2 15.6 %collective-permute-start.2 = (bf16[256,1024]{1,0:T(8,128)(2,1)}, bf16[256,1024]{1,0:T(8,128)(2,1)}, u32[]{:S(2)}, u32[]{:S(2)}) collective-permute-start(bf16[256,1024]{1,0:T(8,128)(2,1)} %constant_dynamic-slice_fusion.refs_8_), channel_id=1, source_target_pairs={{0,65},{1,64},{64,1},{65,0},{2,67},{3,66},{66,3},{67,2},{4,69},{5,... | collective-permute-start | bytes 1572872 | tf_op jit(solution)/shard_map/ppermute | solution.py:250
  14.1 9.1 %copy-start.1 = (bf16[576,1024]{1,0:T(8,128)(2,1)S(1)}, bf16[576,1024]{1,0:T(8,128)(2,1)}, u32[]{:S(2)}) copy-start(bf16[576,1024]{1,0:T(8,128)(2,1)} %refs_2_.7) | copy-start | bytes 3538948
  21.8 14.6 %collective-permute-start.7 = (bf16[2048,1024]{1,0:T(8,128)(2,1)}, bf16[2048,1024]{1,0:T(8,128)(2,1)}, u32[]{:S(2)}, u32[]{:S(2)}) collective-permute-start(bf16[2048,1024]{1,0:T(8,128)(2,1)} %get-tuple-element.47), channel_id=1, source_target_pairs={{0,8},{8,0},{1,9},{9,1},{2,10},{10,2},{3,11},{11,3},{4,12},{12,4},... | collective-permute-start | bytes 12582920 | tf_op jit(solution)/shard_map/ppermute | solution.py:247
  23.2 13.2 %collective-permute-start.8 = (bf16[576,1024]{1,0:T(8,128)(2,1)S(1)}, bf16[576,1024]{1,0:T(8,128)(2,1)}, u32[]{:S(2)}, u32[]{:S(2)}) collective-permute-start(bf16[576,1024]{1,0:T(8,128)(2,1)S(1)} %copy-done.1), channel_id=1, source_target_pairs={{0,8},{8,0},{1,9},{9,1},{2,10},{10,2},{3,11},{11,3},{4,12},{12,4},... | collective-permute-start | bytes 3538952 | tf_op jit(solution)/shard_map/ppermute | solution.py:247
  25.2 8.5 %collective-permute-start.5 = (bf16[128,1024]{1,0:T(8,128)(2,1)}, bf16[128,1024]{1,0:T(8,128)(2,1)S(1)}, u32[]{:S(2)}, u32[]{:S(2)}) collective-permute-start(bf16[128,1024]{1,0:T(8,128)(2,1)} %get-tuple-element.45), channel_id=1, source_target_pairs={{0,6},{2,0},{4,2},{6,4},{1,7},{3,1},{5,3},{7,5},{8,14},{10,8},{12,... | collective-permute-start | bytes 786440 | tf_op jit(solution)/shard_map/ppermute | solution.py:253
  27.8 8.6 %collective-permute-start.6 = (bf16[128,1024]{1,0:T(8,128)(2,1)}, bf16[128,1024]{1,0:T(8,128)(2,1)S(1)}, u32[]{:S(2)}, u32[]{:S(2)}) collective-permute-start(bf16[128,1024]{1,0:T(8,128)(2,1)} %get-tuple-element.46), channel_id=1, source_target_pairs={{0,2},{2,4},{4,6},{6,0},{1,3},{3,5},{5,7},{7,1},{8,10},{10,12},{12... | collective-permute-start | bytes 786440 | tf_op jit(solution)/shard_map/ppermute | solution.py:253
  33.7 8.1 %copy-start.7 = (bf16[128,1024]{1,0:T(8,128)(2,1)}, bf16[128,1024]{1,0:T(8,128)(2,1)S(1)}, u32[]{:S(2)}) copy-start(bf16[128,1024]{1,0:T(8,128)(2,1)S(1)} %collective-permute-done.5.refs_11_) | copy-start | bytes 786436
  36.4 2.8 %copy-start.8 = (bf16[128,1024]{1,0:T(8,128)(2,1)}, bf16[128,1024]{1,0:T(8,128)(2,1)S(1)}, u32[]{:S(2)}) copy-start(bf16[128,1024]{1,0:T(8,128)(2,1)S(1)} %collective-permute-done.6.refs_12_) | copy-start | bytes 786436
  36.4 18.3 %collective-permute-start.10 = (bf16[256,1024]{1,0:T(8,128)(2,1)}, bf16[256,1024]{1,0:T(8,128)(2,1)S(1)}, u32[]{:S(2)}, u32[]{:S(2)}) collective-permute-start(bf16[256,1024]{1,0:T(8,128)(2,1)} %collective-permute-done.2.refs_8_), channel_id=1, source_target_pairs={{0,2},{2,4},{4,6},{6,0},{1,3},{3,5},{5,7},{7,1},{8,10},{10,12},{12... | collective-permute-start | bytes 1572872 | tf_op jit(solution)/shard_map/ppermute | solution.py:253
  36.5 19.0 %collective-permute-start.9 = (bf16[256,1024]{1,0:T(8,128)(2,1)}, bf16[256,1024]{1,0:T(8,128)(2,1)S(1)}, u32[]{:S(2)}, u32[]{:S(2)}) collective-permute-start(bf16[256,1024]{1,0:T(8,128)(2,1)} %collective-permute-done.2.refs_8_), channel_id=1, source_target_pairs={{0,6},{2,0},{4,2},{6,4},{1,7},{3,1},{5,3},{7,5},{8,14},{10,8},{12,... | collective-permute-start | bytes 1572872 | tf_op jit(solution)/shard_map/ppermute | solution.py:253
  39.1 15.5 %collective-permute-start.11 = (bf16[128,1024]{1,0:T(8,128)(2,1)S(1)}, bf16[128,1024]{1,0:T(8,128)(2,1)S(1)}, u32[]{:S(2)}, u32[]{:S(2)}) collective-permute-start(bf16[128,1024]{1,0:T(8,128)(2,1)S(1)} %collective-permute-done.5.refs_11_), channel_id=1, source_target_pairs={{0,65},{1,64},{64,1},{65,0},{2,67},{3,66},{66,3},{67,2},{4,69},{5,... | collective-permute-start | bytes 786440 | tf_op jit(solution)/shard_map/ppermute | solution.py:250
  41.8 12.9 %collective-permute-start.12 = (bf16[128,1024]{1,0:T(8,128)(2,1)}, bf16[128,1024]{1,0:T(8,128)(2,1)S(1)}, u32[]{:S(2)}, u32[]{:S(2)}) collective-permute-start(bf16[128,1024]{1,0:T(8,128)(2,1)} %copy-done.8), channel_id=1, source_target_pairs={{0,65},{1,64},{64,1},{65,0},{2,67},{3,66},{66,3},{67,2},{4,69},{5,... | collective-permute-start | bytes 786440 | tf_op jit(solution)/shard_map/ppermute | solution.py:250
  54.7 0.8 copy-start.5
  54.7 0.8 copy-start.6
  55.5 0.8 copy-start.3
  55.5 1.0 copy-start.4
  56.4 28.2 %all-to-all-start = ((bf16[4,2,4,256,128]{4,3,2,1,0:T(8,128)(2,1)}), bf16[4,2,4,256,128]{4,3,2,1,0:T(8,128)(2,1)}, u32[]{:S(2)}, u32[]{:S(2)}) async-start(bf16[4,2,4,256,128]{4,3,2,1,0:T(8,128)(2,1)} %shard_map.77), calls=%async_computation | async-start | bytes 4194304 | tf_op jit(solution)/shard_map/all_to_all | solution.py:288
  66.5 20.1 %collective-permute-start.18 = (bf16[8,256,128]{2,1,0:T(8,128)(2,1)}, bf16[8,256,128]{2,1,0:T(8,128)(2,1)}, u32[]{:S(2)}, u32[]{:S(2)}) collective-permute-start(bf16[8,256,128]{2,1,0:T(8,128)(2,1)} %shard_map.80), channel_id=1, source_target_pairs={{0,4},{2,6},{4,0},{6,2},{1,5},{3,7},{5,1},{7,3},{8,12},{10,14},{12... | collective-permute-start | bytes 1572872 | tf_op jit(solution)/shard_map/ppermute | solution.py:253
  74.8 17.6 %collective-permute-start.17 = (bf16[8,256,128]{2,1,0:T(8,128)(2,1)}, bf16[8,256,128]{2,1,0:T(8,128)(2,1)}, u32[]{:S(2)}, u32[]{:S(2)}) collective-permute-start(bf16[8,256,128]{2,1,0:T(8,128)(2,1)} %get-tuple-element.67), channel_id=1, source_target_pairs={{0,2},{2,4},{4,6},{6,0},{1,3},{3,5},{5,7},{7,1},{8,10},{10,12},{12... | collective-permute-start | bytes 1572872 | tf_op jit(solution)/shard_map/ppermute | solution.py:253
  75.6 16.7 %collective-permute-start.19 = (bf16[8,256,128]{2,1,0:T(8,128)(2,1)}, bf16[8,256,128]{2,1,0:T(8,128)(2,1)}, u32[]{:S(2)}, u32[]{:S(2)}) collective-permute-start(bf16[8,256,128]{2,1,0:T(8,128)(2,1)} %get-tuple-element.70), channel_id=1, source_target_pairs={{0,6},{2,0},{4,2},{6,4},{1,7},{3,1},{5,3},{7,5},{8,14},{10,8},{12,... | collective-permute-start | bytes 1572872 | tf_op jit(solution)/shard_map/ppermute | solution.py:253
  83.1 9.2 %copy-start.2 = (bf16[8,256,128]{2,1,0:T(8,128)(2,1)S(1)}, bf16[8,256,128]{2,1,0:T(8,128)(2,1)}, u32[]{:S(2)}) copy-start(bf16[8,256,128]{2,1,0:T(8,128)(2,1)} %shard_map.78) | copy-start | bytes 1572868
  86.5 12.3 %collective-permute-start.13 = (bf16[4,256,128]{2,1,0:T(8,128)(2,1)S(1)}, bf16[4,256,128]{2,1,0:T(8,128)(2,1)}, u32[]{:S(2)}, u32[]{:S(2)}) collective-permute-start(bf16[4,256,128]{2,1,0:T(8,128)(2,1)S(1)} %dynamic-slice_bitcast_fusion), channel_id=1, source_target_pairs={{0,64},{64,0},{1,65},{65,1},{2,66},{66,2},{3,67},{67,3},{4,68},{68... | collective-permute-start | bytes 786440 | tf_op jit(solution)/shard_map/ppermute | solution.py:289
  94.7 11.2 %all-to-all-start.1 = ((bf16[8,256,128]{2,1,0:T(8,128)(2,1)}), bf16[8,256,128]{2,1,0:T(8,128)(2,1)S(1)}, u32[]{:S(2)}, u32[]{:S(2)}) async-start(bf16[8,256,128]{2,1,0:T(8,128)(2,1)} %add_convert_fusion), calls=%async_computation.1 | async-start | bytes 1048576 | tf_op jit(solution)/shard_map/all_to_all | solution.py:284
  99.9 6.2 %collective-permute-start.14 = (bf16[256,128]{1,0:T(8,128)(2,1)S(1)}, bf16[256,128]{1,0:T(8,128)(2,1)S(1)}, u32[]{:S(2)}, u32[]{:S(2)}) collective-permute-start(bf16[256,128]{1,0:T(8,128)(2,1)S(1)} %get-tuple-element.71), channel_id=1, source_target_pairs={{0,2},{2,4},{4,6},{6,0},{1,3},{3,5},{5,7},{7,1},{8,10},{10,12},{12... | collective-permute-start | bytes 196616 | tf_op jit(solution)/shard_map/ppermute | solution.py:253
  99.9 6.1 %collective-permute-start.15 = (bf16[256,128]{1,0:T(8,128)(2,1)S(1)}, bf16[256,128]{1,0:T(8,128)(2,1)S(1)}, u32[]{:S(2)}, u32[]{:S(2)}) collective-permute-start(bf16[256,128]{1,0:T(8,128)(2,1)S(1)} %get-tuple-element.73), channel_id=1, source_target_pairs={{0,6},{2,0},{4,2},{6,4},{1,7},{3,1},{5,3},{7,5},{8,14},{10,8},{12,... | collective-permute-start | bytes 196616 | tf_op jit(solution)/shard_map/ppermute | solution.py:253
  102.6 4.9 %collective-permute-start.16 = (bf16[256,128]{1,0:T(8,128)(2,1)S(1)}, bf16[256,128]{1,0:T(8,128)(2,1)S(1)}, u32[]{:S(2)}, u32[]{:S(2)}) collective-permute-start(bf16[256,128]{1,0:T(8,128)(2,1)S(1)} %get-tuple-element.72), channel_id=1, source_target_pairs={{0,4},{2,6},{4,0},{6,2},{1,5},{3,7},{5,1},{7,3},{8,12},{10,14},{12... | collective-permute-start | bytes 196616 | tf_op jit(solution)/shard_map/ppermute | solution.py:253
  107.6 6.0 %collective-permute-start.20 = (bf16[2,256,128]{2,1,0:T(8,128)(2,1)S(1)}, bf16[2,256,128]{2,1,0:T(8,128)(2,1)S(1)}, u32[]{:S(2)}, u32[]{:S(2)}) collective-permute-start(bf16[2,256,128]{2,1,0:T(8,128)(2,1)S(1)} %pad_maximum_fusion.1), channel_id=1, source_target_pairs={{0,1},{1,0},{2,3},{3,2},{4,5},{5,4},{6,7},{7,6},{8,9},{9,8},{10,11... | collective-permute-start | bytes 393224 | tf_op jit(solution)/shard_map/ppermute | solution.py:296
  113.6 4.1 %collective-permute-start.21 = (bf16[2,256,128]{2,1,0:T(8,128)(2,1)S(1)}, bf16[2,256,128]{2,1,0:T(8,128)(2,1)S(1)}, u32[]{:S(2)}, u32[]{:S(2)}) collective-permute-start(bf16[2,256,128]{2,1,0:T(8,128)(2,1)S(1)} %add_convert_fusion.2), channel_id=1, source_target_pairs={{0,6},{2,0},{4,2},{6,4},{1,7},{3,1},{5,3},{7,5},{8,14},{10,8},{12,... | collective-permute-start | bytes 393224 | tf_op jit(solution)/shard_map/ppermute | solution.py:253
  114.0 5.0 %collective-permute-start.22 = (bf16[2,256,128]{2,1,0:T(8,128)(2,1)S(1)}, bf16[2,256,128]{2,1,0:T(8,128)(2,1)S(1)}, u32[]{:S(2)}, u32[]{:S(2)}) collective-permute-start(bf16[2,256,128]{2,1,0:T(8,128)(2,1)S(1)} %add_convert_fusion.2), channel_id=1, source_target_pairs={{0,2},{2,4},{4,6},{6,0},{1,3},{3,5},{5,7},{7,1},{8,10},{10,12},{12... | collective-permute-start | bytes 393224 | tf_op jit(solution)/shard_map/ppermute | solution.py:253
  115.1 5.3 %collective-permute-start.23 = (bf16[2,256,128]{2,1,0:T(8,128)(2,1)S(1)}, bf16[2,256,128]{2,1,0:T(8,128)(2,1)S(1)}, u32[]{:S(2)}, u32[]{:S(2)}) collective-permute-start(bf16[2,256,128]{2,1,0:T(8,128)(2,1)S(1)} %add_convert_fusion.2), channel_id=1, source_target_pairs={{0,4},{2,6},{4,0},{6,2},{1,5},{3,7},{5,1},{7,3},{8,12},{10,14},{12... | collective-permute-start | bytes 393224 | tf_op jit(solution)/shard_map/ppermute | solution.py:253
  122.8 7.3 %collective-permute-start.24 = (f32[256,128]{1,0:T(8,128)S(1)}, f32[256,128]{1,0:T(8,128)S(1)}, u32[]{:S(2)}, u32[]{:S(2)}) collective-permute-start(f32[256,128]{1,0:T(8,128)S(1)} %dynamic-slice_bitcast_fusion.1), channel_id=1, source_target_pairs={{0,8},{8,0},{1,9},{9,1},{2,10},{10,2},{3,11},{11,3},{4,12},{12,4},... | collective-permute-start | bytes 393224 | tf_op jit(solution)/shard_map/ppermute | solution.py:247
  144.1 3.7 %collective-permute-start.25 = (bf16[256,1024]{0,1:T(8,128)(2,1)S(1)}, bf16[256,1024]{0,1:T(8,128)(2,1)S(1)}, u32[]{:S(2)}, u32[]{:S(2)}) collective-permute-start(bf16[256,1024]{0,1:T(8,128)(2,1)S(1)} %bitcast.40), channel_id=1, source_target_pairs={{0,8},{8,0},{1,9},{9,1},{2,10},{10,2},{3,11},{11,3},{4,12},{12,4},... | collective-permute-start | bytes 1572872 | tf_op jit(solution)/shard_map/ppermute | solution.py:247

commit v5 on v4

--- a/solution.py
+++ b/solution.py
@@ -239,9 +239,36 @@
     )(here, g)
 
 
+def rows_kernel(here, a, out, sem):
+    x, zl = here[1], here[4]
+    copies = []
+    for i, dx in enumerate((0, 1, 3, 2)):
+        for k in range(2):
+            block = lax.rem(x + dx, 4) * 2 + (1 - zl if k else zl)
+            rows = pl.ds(pl.multiple_of(block * 128, 128), 128)
+            n = 2 * i + k
+            copies.append(
+                pltpu.make_async_copy(a.at[rows], out.at[pl.ds(n * 128, 128)], sem.at[n])
+            )
+            copies[-1].start()
+    for copy in copies:
+        copy.wait()
+
+
+def own_rows(here, a):
+    return pl.pallas_call(
+        rows_kernel,
+        in_specs=[pl.BlockSpec(memory_space=pltpu.SMEM), pl.BlockSpec(memory_space=pl.ANY)],
+        out_specs=pl.BlockSpec(memory_space=pltpu.VMEM),
+        out_shape=jax.ShapeDtypeStruct((1024, 1024), BF),
+        scratch_shapes=[pltpu.SemaphoreType.DMA((8,))],
+        cost_estimate=pl.CostEstimate(flops=0, bytes_accessed=4 * 2**20, transcendentals=0),
+    )(here, a)
+
+
 def shards(inputs, cotangent, pre_gelu, w_down, error_feedback, a_inverse, g_inverse):
     c, x, y, zh, zl = (lax.axis_index(a) for a in ("c", "x", "y", "zh", "zl"))
-    here = jnp.stack([c, x, y, zh]).astype(jnp.int32)
+    here = jnp.stack([c, x, y, zh, zl]).astype(jnp.int32)
 
     def swap(a):
         return lax.ppermute(a, "c", [(0, 1), (1, 0)])
@@ -291,7 +318,10 @@
     (far,) = product(False, ((2, 1),), third[2:])
     up, low = product(False, ((1, 1), (3, 1)), [third[0], third[1]])
     (own,) = product(False, ((0, 1),), [w_z])
+    own, a_rows = lax.optimization_barrier((own, a_inverse))
+    a_rows = own_rows(here, a_rows)
     others = added([own, ring(up, "y", 1), ring(far, "y", 2), ring(low, "y", -1)])
+    others, a_rows = lax.optimization_barrier((others, a_rows))
     others = added(exchanged(others, ("x", "zl")))
     theirs = lax.ppermute(jnp.stack([others, near]), "zh", [(0, 1), (1, 0)])
     grad = added([jnp.stack([near, others]), theirs])
@@ -301,12 +331,12 @@
     ).reshape(2, 256, 128)
     mine, other = (lax.dynamic_index_in_dim(part, k, 0, keepdims=False) for k in (c, 1 - c))
     left = (mine + swap(other)).astype(BF)
-    mine = lax.all_to_all(
-        jnp.broadcast_to(left[None], (8, 256, 128)), ("x", "zl"), 0, 0, tiled=True
-    ).transpose(1, 0, 2).reshape(256, 1024)
+    pair = jnp.stack([left, lax.ppermute(left, "zl", [(0, 1), (1, 0)])])
+    mine = jnp.concatenate([pair, ring(pair, "x", -1), ring(pair, "x", 1), ring(pair, "x", 2)])
+    mine = mine.transpose(1, 0, 2).reshape(256, 1024)
     other = swap(mine)
     both = jnp.where(c == 0, jnp.concatenate([mine, other]), jnp.concatenate([other, mine]))
-    return jnp.dot(both, a_inverse, preferred_element_type=F32)
+    return jnp.dot(both, a_rows, preferred_element_type=F32)
 
 
 def solution(mesh):

time: 151 us -> 152 us (level)
  blocking collectives: 13.6 us -> 0 us
  starting transfers between devices: 46.1 us -> 53.3 us
  waiting for transfers between devices: 25.2 us -> 29.7 us
  Pallas kernels: 50.2 us -> 53.8 us
  other arithmetic: 6.09 us -> 4.15 us
    all_to_all x1 -> x0, blocking collectives: 13.6 us -> none  [shards(): lax.all_to_all(jnp.broadcast_to(left[None], (8, 256, 128)), ('x', 'zl'),...]
    ppermute x15 -> x18, starting transfers between devices: 16.1 us -> 21.3 us  [ring(): return lax.ppermute(a, axis, [(i, (i + step) % 4) for i in range(4)])]
    ppermute x15 -> x18, waiting for transfers between devices: 14.8 us -> 19.4 us  [ring(): return lax.ppermute(a, axis, [(i, (i + step) % 4) for i in range(4)])]
    pallas_call x0 -> x1, Pallas kernels: none -> 3.58 us  [own_rows(): pl.pallas_call(rows_kernel, in_specs=[pl.BlockSpec(memory_space=pltpu.SME...]
    another operation x2, other arithmetic: 2.38 us -> 0.29 us
    unnamed x18 -> x29, local copies, waits for them, and re-layouts: 1.75 us -> 3.44 us
    ppermute x0 -> x1, waiting for transfers between devices: none -> 1.66 us  [shards(): pair = jnp.stack([left, lax.ppermute(left, 'zl', [(0, 1), (1, 0)])])]
    dot_general x1, matrix products: 2.59 us -> 4.19 us  [shards(): return jnp.dot(both, a_rows, preferred_element_type=F32)]
  transfers between devices with their start and end apart: 28 -> 32, of which waited for: 12 -> 14; matrix products, arithmetic and copies ran while one was open for 5% -> 4% of each run, Pallas kernels for 33% -> 36%
where the time goes in v5:
time: 152 us; the launch traced here: 151 us
  Pallas kernels  53.8 us (35%)
  starting transfers between devices  53.3 us (35%)
  waiting for transfers between devices  29.7 us (20%)
  matrix products  5.01 us (3%)
  local copies, waits for them, and re-layouts  4.97 us (3%)
  other arithmetic  4.15 us (3%)
    pallas_call x4, Pallas kernels, terms(): pl.pallas_call(functools.partial(term_kernel, by_columns, part), in_specs...  32 us
    ppermute x18, starting transfers between devices, ring(): return lax.ppermute(a, axis, [(i, (i + step) % 4) for i in range(4)])  21.3 us
    ppermute x18, waiting for transfers between devices, ring(): return lax.ppermute(a, axis, [(i, (i + step) % 4) for i in range(4)])  19.4 us
    pallas_call x2, Pallas kernels, prepare(): pl.pallas_call(prepare_kernel, in_specs=[pl.BlockSpec(memory_space=pltpu....  12.8 us
    ppermute x6, starting transfers between devices, swap(): return lax.ppermute(a, 'c', [(0, 1), (1, 0)])  12.3 us
    ppermute x3, starting transfers between devices, across_z(): return lax.ppermute(a, ('zl', 'zh'), [(i, 3 - i) for i in range(4)])  6.45 us
    dot_general x1, matrix products, shards(): return jnp.dot(both, a_rows, preferred_element_type=F32)  4.19 us
    all_to_all x1, starting transfers between devices, exchanged(): return lax.all_to_all(a.reshape(8, 256, 128), axes, 0, 0, tiled=True)  4.1 us
  transfers between devices with their start and end apart: 32, of which 14 were waited for; matrix products, arithmetic and copies ran while one was open for 4% of the time, Pallas kernels for 36%

profile of v5, /device:TPU:1, one launch (start us, length us, event | category | flops | bytes accessed | tf_op | source)
XLA Modules:
  0.0 151.3 jit_solution(16856232438762531026)
XLA Ops:
  0.0 1.4 collective-permute-start.3
  1.4 0.9 constant_dynamic-slice_fusion.refs_8_
  2.3 3.4 %collective-permute-start = (bf16[256,1024]{1,0:T(8,128)(2,1)}, bf16[256,1024]{1,0:T(8,128)(2,1)S(1)}, u32[]{:S(2)}, u32[]{:S(2)}) collective-permute-start(bf16[256,1024]{1,0:T(8,128)(2,1)} %constant_dynamic-slice_fusion.refs_8_), channel_id=1, source_target_pairs={{0,6},{2,0},{4,2},{6,4},{1,7},{3,1},{5,3},{7,5},{8,14},{10,8},{12,... | collective-permute-start | bytes 1572872 | tf_op jit(solution)/shard_map/ppermute | solution.py:280
  5.6 3.8 %collective-permute-start.2 = (bf16[256,1024]{1,0:T(8,128)(2,1)}, bf16[256,1024]{1,0:T(8,128)(2,1)S(1)}, u32[]{:S(2)}, u32[]{:S(2)}) collective-permute-start(bf16[256,1024]{1,0:T(8,128)(2,1)} %constant_dynamic-slice_fusion.refs_8_), channel_id=1, source_target_pairs={{0,65},{1,64},{64,1},{65,0},{2,67},{3,66},{66,3},{67,2},{4,69},{5,... | collective-permute-start | bytes 1572872 | tf_op jit(solution)/shard_map/ppermute | solution.py:277
  9.4 0.6 stack.44.here
  10.0 3.6 %shard_map.74 = bf16[512,2048]{1,0:T(8,128)(2,1)} custom-call(s32[5]{0:T(128)} %stack.44.here, bf16[512,4096]{1,0:T(8,128)(2,1)} %g.1), custom_call_target="tpu_custom_call" | custom-call | bytes 4194304 | tf_op jit(solution)/shard_map/pallas_call | solution.py:232
  13.6 0.0 copy-start.2
  13.6 6.9 %shard_map.73 = (bf16[2048,576]{1,0:T(8,128)(2,1)}, bf16[1024,576]{1,0:T(8,128)(2,1)}, bf16[2048,1024]{1,0:T(8,128)(2,1)}) custom-call(s32[5]{0:T(128)} %stack.44.here, bf16[576,4096]{1,0:T(8,128)(2,1)} %pre.1, bf16[576,1024]{1,0:T(8,128)(2,1)} %cot.1, bf16[4096,1024]{1,0:T(8,128)(2,1)} %refs_6_.7), custom_call_target="tpu_custom_call" | custom-call | flops 70778880 | bytes 5242880 | tf_op jit(solution)/shard_map/pallas_call | solution.py:73
  20.6 0.5 collective-permute-done.2.refs_8_
  21.1 1.1 copy-done.6
  22.2 1.4 collective-permute-start.7
  23.6 0.0 collective-permute-start.8
  23.6 1.9 %shard_map.75 = (bf16[128,1024]{1,0:T(8,128)(2,1)}, bf16[128,1024]{1,0:T(8,128)(2,1)}) custom-call(bf16[256,1024]{1,0:T(8,128)(2,1)} %copy-done.9, bf16[256,1024]{1,0:T(8,128)(2,1)} %collective-permute-done.1.lower.refs_10_), custom_call_target="tpu_custom_call" | custom-call | tf_op jit(solution)/shard_map/pallas_call | solution.py:102
  25.5 2.6 %collective-permute-start.5 = (bf16[128,1024]{1,0:T(8,128)(2,1)}, bf16[128,1024]{1,0:T(8,128)(2,1)}, u32[]{:S(2)}, u32[]{:S(2)}) collective-permute-start(bf16[128,1024]{1,0:T(8,128)(2,1)} %get-tuple-element.49), channel_id=1, source_target_pairs={{0,6},{2,0},{4,2},{6,4},{1,7},{3,1},{5,3},{7,5},{8,14},{10,8},{12,... | collective-permute-start | bytes 786440 | tf_op jit(solution)/shard_map/ppermute | solution.py:280
  28.2 5.9 %shard_map.76 = (bf16[2048,576]{1,0:T(8,128)(2,1)}, bf16[1024,576]{1,0:T(8,128)(2,1)}) custom-call(s32[5]{0:T(128)} %stack.44.here, bf16[576,4096]{1,0:T(8,128)(2,1)} %collective-permute-done.3.pre, bf16[576,1024]{1,0:T(8,128)(2,1)} %copy-done.6), custom_call_target="tpu_custom_call" | custom-call | flops 70778880 | bytes 5242880 | tf_op jit(solution)/shard_map/pallas_call | solution.py:73
  34.1 2.6 %collective-permute-done.6.refs_12_ = bf16[128,1024]{1,0:T(8,128)(2,1)S(1)} collective-permute-done((bf16[128,1024]{1,0:T(8,128)(2,1)}, bf16[128,1024]{1,0:T(8,128)(2,1)S(1)}, u32[]{:S(2)}, u32[]{:S(2)}) %collective-permute-start.6) | collective-permute-done | bytes 262176 | tf_op jit(solution)/shard_map/ppermute | solution.py:280
  36.6 0.7 copy-done.12
  37.4 2.7 %collective-permute-start.9 = (bf16[256,1024]{1,0:T(8,128)(2,1)S(1)}, bf16[256,1024]{1,0:T(8,128)(2,1)}, u32[]{:S(2)}, u32[]{:S(2)}) collective-permute-start(bf16[256,1024]{1,0:T(8,128)(2,1)S(1)} %collective-permute-done.2.refs_8_), channel_id=1, source_target_pairs={{0,6},{2,0},{4,2},{6,4},{1,7},{3,1},{5,3},{7,5},{8,14},{10,8},{12,... | collective-permute-start | bytes 1572872 | tf_op jit(solution)/shard_map/ppermute | solution.py:280
  40.0 2.6 %collective-permute-start.11 = (bf16[128,1024]{1,0:T(8,128)(2,1)}, bf16[128,1024]{1,0:T(8,128)(2,1)S(1)}, u32[]{:S(2)}, u32[]{:S(2)}) collective-permute-start(bf16[128,1024]{1,0:T(8,128)(2,1)} %collective-permute-done.5.refs_11_), channel_id=1, source_target_pairs={{0,65},{1,64},{64,1},{65,0},{2,67},{3,66},{66,3},{67,2},{4,69},{5,... | collective-permute-start | bytes 786440 | tf_op jit(solution)/shard_map/ppermute | solution.py:277
  42.7 0.1 collective-permute-start.12
  42.7 12.8 %shard_map.77 = bf16[4,2,4,256,128]{4,3,2,1,0:T(8,128)(2,1)} custom-call(s32[5]{0:T(128)} %stack.44.here, bf16[1024,576]{1,0:T(8,128)(2,1)} %get-tuple-element.46.refs_0_, bf16[1024,576]{1,0:T(8,128)(2,1)} %get-tuple-element.58.refs_1_, bf16[576,1024]{1,0:T(8,128)(2,1)} %refs_2_.7, bf16[576,1024]{1,0:T(8,128)(2,1)} %copy-done.3, ...), custom_call_target="tpu_custom_call" | custom-call | flops 19327352832 | bytes 12582912 | tf_op jit(solution)/shard_map/pallas_call | solution.py:190
  55.6 0.6 copy-done.10
  56.2 0.1 copy-done.11
  56.4 0.8 copy-done.8
  57.2 4.0 %all-to-all-start = ((bf16[4,2,4,256,128]{4,3,2,1,0:T(8,128)(2,1)}), bf16[4,2,4,256,128]{4,3,2,1,0:T(8,128)(2,1)S(1)}, u32[]{:S(2)}, u32[]{:S(2)}) async-start(bf16[4,2,4,256,128]{4,3,2,1,0:T(8,128)(2,1)} %shard_map.77), calls=%async_computation | async-start | bytes 4194304 | tf_op jit(solution)/shard_map/all_to_all | solution.py:315
  61.2 5.6 %shard_map.80 = bf16[8,256,128]{2,1,0:T(8,128)(2,1)} custom-call(s32[5]{0:T(128)} %stack.44.here, bf16[1024,576]{1,0:T(8,128)(2,1)} %get-tuple-element.46.refs_0_, bf16[1024,576]{1,0:T(8,128)(2,1)} %get-tuple-element.58.refs_1_, bf16[576,1024]{1,0:T(8,128)(2,1)} %refs_2_.7, bf16[576,1024]{1,0:T(8,128)(2,1)} %copy-done.3, ...), custom_call_target="tpu_custom_call" | custom-call | flops 1207959552 | bytes 3145728 | tf_op jit(solution)/shard_map/pallas_call | solution.py:190
  66.8 0.3 collective-permute-start.18
  67.1 8.0 %shard_map.79 = (bf16[8,256,128]{2,1,0:T(8,128)(2,1)}, bf16[8,256,128]{2,1,0:T(8,128)(2,1)}) custom-call(s32[5]{0:T(128)} %stack.44.here, bf16[1024,576]{1,0:T(8,128)(2,1)} %get-tuple-element.46.refs_0_, bf16[1024,576]{1,0:T(8,128)(2,1)} %get-tuple-element.58.refs_1_, bf16[576,1024]{1,0:T(8,128)(2,1)} %refs_2_.7, bf16[576,1024]{1,0:T(8,128)(2,1)} %copy-done.3, ...), custom_call_target="tpu_custom_call" | custom-call | flops 2415919104 | bytes 6291456 | tf_op jit(solution)/shard_map/pallas_call | solution.py:190
  75.1 0.6 collective-permute-start.17
  75.8 2.1 %collective-permute-start.19 = (bf16[8,256,128]{2,1,0:T(8,128)(2,1)}, bf16[8,256,128]{2,1,0:T(8,128)(2,1)}, u32[]{:S(2)}, u32[]{:S(2)}) collective-permute-start(bf16[8,256,128]{2,1,0:T(8,128)(2,1)} %get-tuple-element.75), channel_id=1, source_target_pairs={{0,6},{2,0},{4,2},{6,4},{1,7},{3,1},{5,3},{7,5},{8,14},{10,8},{12,... | collective-permute-start | bytes 1572872 | tf_op jit(solution)/shard_map/ppermute | solution.py:280
  77.9 5.6 %shard_map.78 = bf16[8,256,128]{2,1,0:T(8,128)(2,1)} custom-call(s32[5]{0:T(128)} %stack.44.here, bf16[1024,576]{1,0:T(8,128)(2,1)} %get-tuple-element.46.refs_0_, bf16[1024,576]{1,0:T(8,128)(2,1)} %get-tuple-element.58.refs_1_, bf16[576,1024]{1,0:T(8,128)(2,1)} %refs_2_.7, bf16[576,1024]{1,0:T(8,128)(2,1)} %copy-done.3, ...), custom_call_target="tpu_custom_call" | custom-call | flops 1207959552 | bytes 3145728 | tf_op jit(solution)/shard_map/pallas_call | solution.py:190
  83.4 3.6 %shard_map.81 = bf16[1024,1024]{1,0:T(8,128)(2,1)} custom-call(s32[5]{0:T(128)} %stack.44.here, bf16[1024,1024]{1,0:T(8,128)(2,1)} %a), custom_call_target="tpu_custom_call" | custom-call | bytes 4194304 | tf_op jit(solution)/shard_map/pallas_call | solution.py:259
  87.1 0.3 add_convert_fusion.1
  87.4 0.1 collective-permute-start.13
  87.5 5.0 %collective-permute-done.17 = bf16[8,256,128]{2,1,0:T(8,128)(2,1)} collective-permute-done((bf16[8,256,128]{2,1,0:T(8,128)(2,1)}, bf16[8,256,128]{2,1,0:T(8,128)(2,1)}, u32[]{:S(2)}, u32[]{:S(2)}) %collective-permute-start.17) | collective-permute-done | bytes 524320 | tf_op jit(solution)/shard_map/ppermute | solution.py:280
  92.5 2.4 %add_convert_fusion = bf16[8,256,128]{2,1,0:T(8,128)(2,1)} fusion(bf16[8,256,128]{2,1,0:T(8,128)(2,1)} %collective-permute-done.19, bf16[8,256,128]{2,1,0:T(8,128)(2,1)} %collective-permute-done.18, bf16[8,256,128]{2,1,0:T(8,128)(2,1)} %collective-permute-done.17, bf16[8,256,128]{2,1,0:T(8,128)(2,1)S(1)} %copy-done.5), kind=kLoop, calls=%fused_computation.7 | loop fusion | flops 2097152 | bytes 2621440 | tf_op jit(solution)/shard_map/convert_element_type | solution.py:305
  94.9 4.1 %all-to-all-start.1 = ((bf16[8,256,128]{2,1,0:T(8,128)(2,1)}), bf16[8,256,128]{2,1,0:T(8,128)(2,1)S(1)}, u32[]{:S(2)}, u32[]{:S(2)}) async-start(bf16[8,256,128]{2,1,0:T(8,128)(2,1)} %add_convert_fusion), calls=%async_computation.1 | async-start | bytes 1048576 | tf_op jit(solution)/shard_map/all_to_all | solution.py:311
  99.0 1.2 fusion.7
  100.2 0.1 collective-permute-start.14
  100.3 2.7 %collective-permute-start.15 = (bf16[256,128]{1,0:T(8,128)(2,1)S(1)}, bf16[256,128]{1,0:T(8,128)(2,1)S(1)}, u32[]{:S(2)}, u32[]{:S(2)}) collective-permute-start(bf16[256,128]{1,0:T(8,128)(2,1)S(1)} %get-tuple-element.83), channel_id=1, source_target_pairs={{0,6},{2,0},{4,2},{6,4},{1,7},{3,1},{5,3},{7,5},{8,14},{10,8},{12,... | collective-permute-start | bytes 196616 | tf_op jit(solution)/shard_map/ppermute | solution.py:280
  103.0 3.2 %all-to-all-done.1 = bf16[8,256,128]{2,1,0:T(8,128)(2,1)S(1)} async-done(((bf16[8,256,128]{2,1,0:T(8,128)(2,1)}), bf16[8,256,128]{2,1,0:T(8,128)(2,1)S(1)}, u32[]{:S(2)}, u32[]{:S(2)}) %all-to-all-start.1) | async-done | bytes 524320 | tf_op jit(solution)/shard_map/all_to_all | solution.py:311
  106.1 0.1 add_convert_fusion.3
  106.2 1.6 %collective-permute-done.16 = bf16[256,128]{1,0:T(8,128)(2,1)S(1)} collective-permute-done((bf16[256,128]{1,0:T(8,128)(2,1)S(1)}, bf16[256,128]{1,0:T(8,128)(2,1)S(1)}, u32[]{:S(2)}, u32[]{:S(2)}) %collective-permute-start.16) | collective-permute-done | bytes 65568 | tf_op jit(solution)/shard_map/ppermute | solution.py:280
  107.9 3.6 %collective-permute-start.20 = (bf16[2,256,128]{2,1,0:T(8,128)(2,1)S(1)}, bf16[2,256,128]{2,1,0:T(8,128)(2,1)S(1)}, u32[]{:S(2)}, u32[]{:S(2)}) collective-permute-start(bf16[2,256,128]{2,1,0:T(8,128)(2,1)S(1)} %pad_maximum_fusion.1), channel_id=1, source_target_pairs={{0,1},{1,0},{2,3},{3,2},{4,5},{5,4},{6,7},{7,6},{8,9},{9,8},{10,11... | collective-permute-start | bytes 393224 | tf_op jit(solution)/shard_map/ppermute | solution.py:326
  111.5 2.4 %collective-permute-done.20 = bf16[2,256,128]{2,1,0:T(8,128)(2,1)S(1)} collective-permute-done((bf16[2,256,128]{2,1,0:T(8,128)(2,1)S(1)}, bf16[2,256,128]{2,1,0:T(8,128)(2,1)S(1)}, u32[]{:S(2)}, u32[]{:S(2)}) %collective-permute-start.20) | collective-permute-done | bytes 131104 | tf_op jit(solution)/shard_map/ppermute | solution.py:326
  113.9 0.4 collective-permute-start.21
  114.4 1.1 collective-permute-start.22
  115.5 0.5 collective-permute-start.23
  116.0 2.2 %collective-permute-done.21 = bf16[2,256,128]{2,1,0:T(8,128)(2,1)S(1)} collective-permute-done((bf16[2,256,128]{2,1,0:T(8,128)(2,1)S(1)}, bf16[2,256,128]{2,1,0:T(8,128)(2,1)S(1)}, u32[]{:S(2)}, u32[]{:S(2)}) %collective-permute-start.21) | collective-permute-done | bytes 131104 | tf_op jit(solution)/shard_map/ppermute | solution.py:280
  118.1 1.3 collective-permute-done.22
  119.4 1.4 collective-permute-done.23
  120.8 0.1 pad_maximum_fusion
  120.9 0.8 fusion.15
  121.7 6.5 %collective-permute-start.24 = (f32[256,128]{0,1:T(8,128)S(1)}, f32[256,128]{0,1:T(8,128)S(1)}, u32[]{:S(2)}, u32[]{:S(2)}) collective-permute-start(f32[256,128]{0,1:T(8,128)S(1)} %dynamic-slice_bitcast_fusion.1), channel_id=1, source_target_pairs={{0,8},{8,0},{1,9},{9,1},{2,10},{10,2},{3,11},{11,3},{4,12},{12,4},... | collective-permute-start | bytes 393224 | tf_op jit(solution)/shard_map/ppermute | solution.py:274
  128.3 1.0 collective-permute-done.24
  129.3 1.5 %collective-permute-start.25 = (bf16[256,128]{0,1:T(8,128)(2,1)S(1)}, bf16[256,128]{0,1:T(8,128)(2,1)S(1)}, u32[]{:S(2)}, u32[]{:S(2)}) collective-permute-start(bf16[256,128]{0,1:T(8,128)(2,1)S(1)} %get-tuple-element.80), channel_id=1, source_target_pairs={{0,64},{64,0},{1,65},{65,1},{2,66},{66,2},{3,67},{67,3},{4,68},{68... | collective-permute-start | bytes 196616 | tf_op jit(solution)/shard_map/ppermute | solution.py:334
  130.8 1.7 %collective-permute-done.25 = bf16[256,128]{0,1:T(8,128)(2,1)S(1)} collective-permute-done((bf16[256,128]{0,1:T(8,128)(2,1)S(1)}, bf16[256,128]{0,1:T(8,128)(2,1)S(1)}, u32[]{:S(2)}, u32[]{:S(2)}) %collective-permute-start.25) | collective-permute-done | bytes 65568 | tf_op jit(solution)/shard_map/ppermute | solution.py:334
  132.5 3.0 %collective-permute-start.26 = (bf16[2,256,128]{1,2,0:T(8,128)(2,1)S(1)}, bf16[2,256,128]{1,2,0:T(8,128)(2,1)S(1)}, u32[]{:S(2)}, u32[]{:S(2)}) collective-permute-start(bf16[2,256,128]{1,2,0:T(8,128)(2,1)S(1)} %pad_maximum_fusion.2), channel_id=1, source_target_pairs={{0,48},{16,0},{32,16},{48,32},{1,49},{17,1},{33,17},{49,33},{2,50}... | collective-permute-start | bytes 393224 | tf_op jit(solution)/shard_map/ppermute | solution.py:280
  135.5 1.8 %collective-permute-start.28 = (bf16[2,256,128]{1,2,0:T(8,128)(2,1)S(1)}, bf16[2,256,128]{1,2,0:T(8,128)(2,1)S(1)}, u32[]{:S(2)}, u32[]{:S(2)}) collective-permute-start(bf16[2,256,128]{1,2,0:T(8,128)(2,1)S(1)} %pad_maximum_fusion.2), channel_id=1, source_target_pairs={{0,32},{16,48},{32,0},{48,16},{1,33},{17,49},{33,1},{49,17},{2,34}... | collective-permute-start | bytes 393224 | tf_op jit(solution)/shard_map/ppermute | solution.py:280
  137.3 0.2 collective-permute-done.26
  137.5 5.2 %collective-permute-done.27 = bf16[2,256,128]{1,2,0:T(8,128)(2,1)S(1)} collective-permute-done((bf16[2,256,128]{1,2,0:T(8,128)(2,1)S(1)}, bf16[2,256,128]{1,2,0:T(8,128)(2,1)S(1)}, u32[]{:S(2)}, u32[]{:S(2)}) %collective-permute-start.27) | collective-permute-done | bytes 131104 | tf_op jit(solution)/shard_map/ppermute | solution.py:280
  142.7 2.9 %collective-permute-start.29 = (bf16[256,1024]{0,1:T(8,128)(2,1)S(1)}, bf16[256,1024]{0,1:T(8,128)(2,1)S(1)}, u32[]{:S(2)}, u32[]{:S(2)}) collective-permute-start(bf16[256,1024]{0,1:T(8,128)(2,1)S(1)} %bitcast.48), channel_id=1, source_target_pairs={{0,8},{8,0},{1,9},{9,1},{2,10},{10,2},{3,11},{11,3},{4,12},{12,4},... | collective-permute-start | bytes 1572872 | tf_op jit(solution)/shard_map/ppermute | solution.py:274
  145.6 1.5 %collective-permute-done.29 = bf16[256,1024]{0,1:T(8,128)(2,1)S(1)} collective-permute-done((bf16[256,1024]{0,1:T(8,128)(2,1)S(1)}, bf16[256,1024]{0,1:T(8,128)(2,1)S(1)}, u32[]{:S(2)}, u32[]{:S(2)}) %collective-permute-start.29) | collective-permute-done | bytes 524320 | tf_op jit(solution)/shard_map/ppermute | solution.py:274
  147.1 4.2 %fusion = f32[512,1024]{1,0:T(8,128)} fusion(bf16[1024,1024]{1,0:T(8,128)(2,1)} %shard_map.81, bf16[256,1024]{0,1:T(8,128)(2,1)S(1)} %collective-permute-done.29, bf16[256,1024]{0,1:T(8,128)(2,1)S(1)} %bitcast.49, pred[]{:T(512)S(6)} %eq.3), kind=kOutput, calls=%fused_computation.1 | convolution fusion | flops 1078460416 | bytes 5242881 | tf_op jit(solution)/shard_map/dot_general | solution.py:339
  (56 shorter events, 0.3 us)
Async XLA Ops:
  0.0 1.4 copy-start
  0.0 21.1 %collective-permute-start.3 = (bf16[576,4096]{1,0:T(8,128)(2,1)}, bf16[576,4096]{1,0:T(8,128)(2,1)}, u32[]{:S(2)}, u32[]{:S(2)}) collective-permute-start(bf16[576,4096]{1,0:T(8,128)(2,1)} %pre.1), channel_id=1, source_target_pairs={{0,8},{8,0},{1,9},{9,1},{2,10},{10,2},{3,11},{11,3},{4,12},{12,4},... | collective-permute-start | bytes 14155784 | tf_op jit(solution)/shard_map/ppermute | solution.py:274
  1.4 19.7 %collective-permute-start.4 = (bf16[576,1024]{1,0:T(8,128)(2,1)}, bf16[576,1024]{1,0:T(8,128)(2,1)S(1)}, u32[]{:S(2)}, u32[]{:S(2)}) collective-permute-start(bf16[576,1024]{1,0:T(8,128)(2,1)} %cot.1), channel_id=1, source_target_pairs={{0,8},{8,0},{1,9},{9,1},{2,10},{10,2},{3,11},{11,3},{4,12},{12,4},... | collective-permute-start | bytes 3538952 | tf_op jit(solution)/shard_map/ppermute | solution.py:274
  2.3 18.3 %collective-permute-start = (bf16[256,1024]{1,0:T(8,128)(2,1)}, bf16[256,1024]{1,0:T(8,128)(2,1)S(1)}, u32[]{:S(2)}, u32[]{:S(2)}) collective-permute-start(bf16[256,1024]{1,0:T(8,128)(2,1)} %constant_dynamic-slice_fusion.refs_8_), channel_id=1, source_target_pairs={{0,6},{2,0},{4,2},{6,4},{1,7},{3,1},{5,3},{7,5},{8,14},{10,8},{12,... | collective-permute-start | bytes 1572872 | tf_op jit(solution)/shard_map/ppermute | solution.py:280
  5.6 14.9 %collective-permute-start.1 = (bf16[256,1024]{1,0:T(8,128)(2,1)}, bf16[256,1024]{1,0:T(8,128)(2,1)}, u32[]{:S(2)}, u32[]{:S(2)}) collective-permute-start(bf16[256,1024]{1,0:T(8,128)(2,1)} %constant_dynamic-slice_fusion.refs_8_), channel_id=1, source_target_pairs={{0,2},{2,4},{4,6},{6,0},{1,3},{3,5},{5,7},{7,1},{8,10},{10,12},{12... | collective-permute-start | bytes 1572872 | tf_op jit(solution)/shard_map/ppermute | solution.py:280
  5.6 15.5 %collective-permute-start.2 = (bf16[256,1024]{1,0:T(8,128)(2,1)}, bf16[256,1024]{1,0:T(8,128)(2,1)S(1)}, u32[]{:S(2)}, u32[]{:S(2)}) collective-permute-start(bf16[256,1024]{1,0:T(8,128)(2,1)} %constant_dynamic-slice_fusion.refs_8_), channel_id=1, source_target_pairs={{0,65},{1,64},{64,1},{65,0},{2,67},{3,66},{66,3},{67,2},{4,69},{5,... | collective-permute-start | bytes 1572872 | tf_op jit(solution)/shard_map/ppermute | solution.py:277
  13.6 10.0 %copy-start.2 = (bf16[576,1024]{1,0:T(8,128)(2,1)S(1)}, bf16[576,1024]{1,0:T(8,128)(2,1)}, u32[]{:S(2)}) copy-start(bf16[576,1024]{1,0:T(8,128)(2,1)} %refs_2_.7) | copy-start | bytes 3538948
  20.6 3.1 %copy-start.9 = (bf16[256,1024]{1,0:T(8,128)(2,1)}, bf16[256,1024]{1,0:T(8,128)(2,1)S(1)}, u32[]{:S(2)}) copy-start(bf16[256,1024]{1,0:T(8,128)(2,1)S(1)} %collective-permute-done.upper.refs_9_) | copy-start | bytes 1572868
  21.1 34.4 %copy-start.7 = (bf16[256,1024]{1,0:T(8,128)(2,1)}, bf16[256,1024]{1,0:T(8,128)(2,1)S(1)}, u32[]{:S(2)}) copy-start(bf16[256,1024]{1,0:T(8,128)(2,1)S(1)} %collective-permute-done.2.refs_8_) | copy-start | bytes 1572868
  21.1 1.1 copy-start.6
  22.2 14.4 %collective-permute-start.7 = (bf16[2048,1024]{1,0:T(8,128)(2,1)}, bf16[2048,1024]{1,0:T(8,128)(2,1)}, u32[]{:S(2)}, u32[]{:S(2)}) collective-permute-start(bf16[2048,1024]{1,0:T(8,128)(2,1)} %get-tuple-element.51), channel_id=1, source_target_pairs={{0,8},{8,0},{1,9},{9,1},{2,10},{10,2},{3,11},{11,3},{4,12},{12,4},... | collective-permute-start | bytes 12582920 | tf_op jit(solution)/shard_map/ppermute | solution.py:274
  23.6 13.0 %collective-permute-start.8 = (bf16[576,1024]{1,0:T(8,128)(2,1)S(1)}, bf16[576,1024]{1,0:T(8,128)(2,1)S(1)}, u32[]{:S(2)}, u32[]{:S(2)}) collective-permute-start(bf16[576,1024]{1,0:T(8,128)(2,1)S(1)} %copy-done.2), channel_id=1, source_target_pairs={{0,8},{8,0},{1,9},{9,1},{2,10},{10,2},{3,11},{11,3},{4,12},{12,4},... | collective-permute-start | bytes 3538952 | tf_op jit(solution)/shard_map/ppermute | solution.py:274
  25.5 8.5 %collective-permute-start.5 = (bf16[128,1024]{1,0:T(8,128)(2,1)}, bf16[128,1024]{1,0:T(8,128)(2,1)}, u32[]{:S(2)}, u32[]{:S(2)}) collective-permute-start(bf16[128,1024]{1,0:T(8,128)(2,1)} %get-tuple-element.49), channel_id=1, source_target_pairs={{0,6},{2,0},{4,2},{6,4},{1,7},{3,1},{5,3},{7,5},{8,14},{10,8},{12,... | collective-permute-start | bytes 786440 | tf_op jit(solution)/shard_map/ppermute | solution.py:280
  28.2 8.5 %collective-permute-start.6 = (bf16[128,1024]{1,0:T(8,128)(2,1)}, bf16[128,1024]{1,0:T(8,128)(2,1)S(1)}, u32[]{:S(2)}, u32[]{:S(2)}) collective-permute-start(bf16[128,1024]{1,0:T(8,128)(2,1)} %get-tuple-element.50), channel_id=1, source_target_pairs={{0,2},{2,4},{4,6},{6,0},{1,3},{3,5},{5,7},{7,1},{8,10},{10,12},{12... | collective-permute-start | bytes 786440 | tf_op jit(solution)/shard_map/ppermute | solution.py:280
  36.6 0.7 copy-start.12
  36.6 6.1 %copy-start.3 = (bf16[576,1024]{1,0:T(8,128)(2,1)}, bf16[576,1024]{1,0:T(8,128)(2,1)S(1)}, u32[]{:S(2)}) copy-start(bf16[576,1024]{1,0:T(8,128)(2,1)S(1)} %collective-permute-done.8.refs_3_) | copy-start | bytes 3538948
  37.4 18.2 %collective-permute-start.10 = (bf16[256,1024]{1,0:T(8,128)(2,1)S(1)}, bf16[256,1024]{1,0:T(8,128)(2,1)S(1)}, u32[]{:S(2)}, u32[]{:S(2)}) collective-permute-start(bf16[256,1024]{1,0:T(8,128)(2,1)S(1)} %collective-permute-done.2.refs_8_), channel_id=1, source_target_pairs={{0,2},{2,4},{4,6},{6,0},{1,3},{3,5},{5,7},{7,1},{8,10},{10,12},{12... | collective-permute-start | bytes 1572872 | tf_op jit(solution)/shard_map/ppermute | solution.py:280
  37.4 19.0 %collective-permute-start.9 = (bf16[256,1024]{1,0:T(8,128)(2,1)S(1)}, bf16[256,1024]{1,0:T(8,128)(2,1)}, u32[]{:S(2)}, u32[]{:S(2)}) collective-permute-start(bf16[256,1024]{1,0:T(8,128)(2,1)S(1)} %collective-permute-done.2.refs_8_), channel_id=1, source_target_pairs={{0,6},{2,0},{4,2},{6,4},{1,7},{3,1},{5,3},{7,5},{8,14},{10,8},{12,... | collective-permute-start | bytes 1572872 | tf_op jit(solution)/shard_map/ppermute | solution.py:280
  40.0 15.5 %collective-permute-start.11 = (bf16[128,1024]{1,0:T(8,128)(2,1)}, bf16[128,1024]{1,0:T(8,128)(2,1)S(1)}, u32[]{:S(2)}, u32[]{:S(2)}) collective-permute-start(bf16[128,1024]{1,0:T(8,128)(2,1)} %collective-permute-done.5.refs_11_), channel_id=1, source_target_pairs={{0,65},{1,64},{64,1},{65,0},{2,67},{3,66},{66,3},{67,2},{4,69},{5,... | collective-permute-start | bytes 786440 | tf_op jit(solution)/shard_map/ppermute | solution.py:277
  42.7 12.9 %collective-permute-start.12 = (bf16[128,1024]{1,0:T(8,128)(2,1)}, bf16[128,1024]{1,0:T(8,128)(2,1)S(1)}, u32[]{:S(2)}, u32[]{:S(2)}) collective-permute-start(bf16[128,1024]{1,0:T(8,128)(2,1)} %copy-done.12), channel_id=1, source_target_pairs={{0,65},{1,64},{64,1},{65,0},{2,67},{3,66},{66,3},{67,2},{4,69},{5,... | collective-permute-start | bytes 786440 | tf_op jit(solution)/shard_map/ppermute | solution.py:277
  55.6 0.7 copy-start.10
  55.6 0.8 copy-start.11
  56.4 0.8 copy-start.8
  57.2 29.9 %all-to-all-start = ((bf16[4,2,4,256,128]{4,3,2,1,0:T(8,128)(2,1)}), bf16[4,2,4,256,128]{4,3,2,1,0:T(8,128)(2,1)S(1)}, u32[]{:S(2)}, u32[]{:S(2)}) async-start(bf16[4,2,4,256,128]{4,3,2,1,0:T(8,128)(2,1)} %shard_map.77), calls=%async_computation | async-start | bytes 4194304 | tf_op jit(solution)/shard_map/all_to_all | solution.py:315
  66.8 20.7 %collective-permute-start.18 = (bf16[8,256,128]{2,1,0:T(8,128)(2,1)}, bf16[8,256,128]{2,1,0:T(8,128)(2,1)}, u32[]{:S(2)}, u32[]{:S(2)}) collective-permute-start(bf16[8,256,128]{2,1,0:T(8,128)(2,1)} %shard_map.80), channel_id=1, source_target_pairs={{0,4},{2,6},{4,0},{6,2},{1,5},{3,7},{5,1},{7,3},{8,12},{10,14},{12... | collective-permute-start | bytes 1572872 | tf_op jit(solution)/shard_map/ppermute | solution.py:280
  75.1 17.3 %collective-permute-start.17 = (bf16[8,256,128]{2,1,0:T(8,128)(2,1)}, bf16[8,256,128]{2,1,0:T(8,128)(2,1)}, u32[]{:S(2)}, u32[]{:S(2)}) collective-permute-start(bf16[8,256,128]{2,1,0:T(8,128)(2,1)} %get-tuple-element.72), channel_id=1, source_target_pairs={{0,2},{2,4},{4,6},{6,0},{1,3},{3,5},{5,7},{7,1},{8,10},{10,12},{12... | collective-permute-start | bytes 1572872 | tf_op jit(solution)/shard_map/ppermute | solution.py:280
  75.8 16.7 %collective-permute-start.19 = (bf16[8,256,128]{2,1,0:T(8,128)(2,1)}, bf16[8,256,128]{2,1,0:T(8,128)(2,1)}, u32[]{:S(2)}, u32[]{:S(2)}) collective-permute-start(bf16[8,256,128]{2,1,0:T(8,128)(2,1)} %get-tuple-element.75), channel_id=1, source_target_pairs={{0,6},{2,0},{4,2},{6,4},{1,7},{3,1},{5,3},{7,5},{8,14},{10,8},{12,... | collective-permute-start | bytes 1572872 | tf_op jit(solution)/shard_map/ppermute | solution.py:280
  87.0 5.4 %copy-start.5 = (bf16[8,256,128]{2,1,0:T(8,128)(2,1)S(1)}, bf16[8,256,128]{2,1,0:T(8,128)(2,1)}, u32[]{:S(2)}) copy-start(bf16[8,256,128]{2,1,0:T(8,128)(2,1)} %shard_map.78) | copy-start | bytes 1572868
  87.4 11.6 %collective-permute-start.13 = (bf16[4,256,128]{2,1,0:T(8,128)(2,1)S(1)}, bf16[4,256,128]{2,1,0:T(8,128)(2,1)}, u32[]{:S(2)}, u32[]{:S(2)}) collective-permute-start(bf16[4,256,128]{2,1,0:T(8,128)(2,1)S(1)} %dynamic-slice_bitcast_fusion), channel_id=1, source_target_pairs={{0,64},{64,0},{1,65},{65,1},{2,66},{66,2},{3,67},{67,3},{4,68},{68... | collective-permute-start | bytes 786440 | tf_op jit(solution)/shard_map/ppermute | solution.py:316
  94.9 11.2 %all-to-all-start.1 = ((bf16[8,256,128]{2,1,0:T(8,128)(2,1)}), bf16[8,256,128]{2,1,0:T(8,128)(2,1)S(1)}, u32[]{:S(2)}, u32[]{:S(2)}) async-start(bf16[8,256,128]{2,1,0:T(8,128)(2,1)} %add_convert_fusion), calls=%async_computation.1 | async-start | bytes 1048576 | tf_op jit(solution)/shard_map/all_to_all | solution.py:311
  99.0 21.9 %copy-start.4 = (bf16[512,2048]{1,0:T(8,128)(2,1)S(1)}, bf16[512,2048]{1,0:T(8,128)(2,1)}, u32[]{:S(2)}) copy-start(bf16[512,2048]{1,0:T(8,128)(2,1)} %shard_map.74) | copy-start | bytes 6291460
  100.2 6.0 %collective-permute-start.14 = (bf16[256,128]{1,0:T(8,128)(2,1)S(1)}, bf16[256,128]{1,0:T(8,128)(2,1)S(1)}, u32[]{:S(2)}, u32[]{:S(2)}) collective-permute-start(bf16[256,128]{1,0:T(8,128)(2,1)S(1)} %get-tuple-element.81), channel_id=1, source_target_pairs={{0,2},{2,4},{4,6},{6,0},{1,3},{3,5},{5,7},{7,1},{8,10},{10,12},{12... | collective-permute-start | bytes 196616 | tf_op jit(solution)/shard_map/ppermute | solution.py:280
  100.3 5.9 %collective-permute-start.15 = (bf16[256,128]{1,0:T(8,128)(2,1)S(1)}, bf16[256,128]{1,0:T(8,128)(2,1)S(1)}, u32[]{:S(2)}, u32[]{:S(2)}) collective-permute-start(bf16[256,128]{1,0:T(8,128)(2,1)S(1)} %get-tuple-element.83), channel_id=1, source_target_pairs={{0,6},{2,0},{4,2},{6,4},{1,7},{3,1},{5,3},{7,5},{8,14},{10,8},{12,... | collective-permute-start | bytes 196616 | tf_op jit(solution)/shard_map/ppermute | solution.py:280
  103.0 4.9 %collective-permute-start.16 = (bf16[256,128]{1,0:T(8,128)(2,1)S(1)}, bf16[256,128]{1,0:T(8,128)(2,1)S(1)}, u32[]{:S(2)}, u32[]{:S(2)}) collective-permute-start(bf16[256,128]{1,0:T(8,128)(2,1)S(1)} %get-tuple-element.82), channel_id=1, source_target_pairs={{0,4},{2,6},{4,0},{6,2},{1,5},{3,7},{5,1},{7,3},{8,12},{10,14},{12... | collective-permute-start | bytes 196616 | tf_op jit(solution)/shard_map/ppermute | solution.py:280
  107.9 6.0 %collective-permute-start.20 = (bf16[2,256,128]{2,1,0:T(8,128)(2,1)S(1)}, bf16[2,256,128]{2,1,0:T(8,128)(2,1)S(1)}, u32[]{:S(2)}, u32[]{:S(2)}) collective-permute-start(bf16[2,256,128]{2,1,0:T(8,128)(2,1)S(1)} %pad_maximum_fusion.1), channel_id=1, source_target_pairs={{0,1},{1,0},{2,3},{3,2},{4,5},{5,4},{6,7},{7,6},{8,9},{9,8},{10,11... | collective-permute-start | bytes 393224 | tf_op jit(solution)/shard_map/ppermute | solution.py:326
  113.9 4.2 %collective-permute-start.21 = (bf16[2,256,128]{2,1,0:T(8,128)(2,1)S(1)}, bf16[2,256,128]{2,1,0:T(8,128)(2,1)S(1)}, u32[]{:S(2)}, u32[]{:S(2)}) collective-permute-start(bf16[2,256,128]{2,1,0:T(8,128)(2,1)S(1)} %add_convert_fusion.2), channel_id=1, source_target_pairs={{0,6},{2,0},{4,2},{6,4},{1,7},{3,1},{5,3},{7,5},{8,14},{10,8},{12,... | collective-permute-start | bytes 393224 | tf_op jit(solution)/shard_map/ppermute | solution.py:280
  114.4 5.0 %collective-permute-start.22 = (bf16[2,256,128]{2,1,0:T(8,128)(2,1)S(1)}, bf16[2,256,128]{2,1,0:T(8,128)(2,1)S(1)}, u32[]{:S(2)}, u32[]{:S(2)}) collective-permute-start(bf16[2,256,128]{2,1,0:T(8,128)(2,1)S(1)} %add_convert_fusion.2), channel_id=1, source_target_pairs={{0,2},{2,4},{4,6},{6,0},{1,3},{3,5},{5,7},{7,1},{8,10},{10,12},{12... | collective-permute-start | bytes 393224 | tf_op jit(solution)/shard_map/ppermute | solution.py:280
  115.5 5.3 %collective-permute-start.23 = (bf16[2,256,128]{2,1,0:T(8,128)(2,1)S(1)}, bf16[2,256,128]{2,1,0:T(8,128)(2,1)S(1)}, u32[]{:S(2)}, u32[]{:S(2)}) collective-permute-start(bf16[2,256,128]{2,1,0:T(8,128)(2,1)S(1)} %add_convert_fusion.2), channel_id=1, source_target_pairs={{0,4},{2,6},{4,0},{6,2},{1,5},{3,7},{5,1},{7,3},{8,12},{10,14},{12... | collective-permute-start | bytes 393224 | tf_op jit(solution)/shard_map/ppermute | solution.py:280
  121.7 7.5 %collective-permute-start.24 = (f32[256,128]{0,1:T(8,128)S(1)}, f32[256,128]{0,1:T(8,128)S(1)}, u32[]{:S(2)}, u32[]{:S(2)}) collective-permute-start(f32[256,128]{0,1:T(8,128)S(1)} %dynamic-slice_bitcast_fusion.1), channel_id=1, source_target_pairs={{0,8},{8,0},{1,9},{9,1},{2,10},{10,2},{3,11},{11,3},{4,12},{12,4},... | collective-permute-start | bytes 393224 | tf_op jit(solution)/shard_map/ppermute | solution.py:274
  129.3 3.2 %collective-permute-start.25 = (bf16[256,128]{0,1:T(8,128)(2,1)S(1)}, bf16[256,128]{0,1:T(8,128)(2,1)S(1)}, u32[]{:S(2)}, u32[]{:S(2)}) collective-permute-start(bf16[256,128]{0,1:T(8,128)(2,1)S(1)} %get-tuple-element.80), channel_id=1, source_target_pairs={{0,64},{64,0},{1,65},{65,1},{2,66},{66,2},{3,67},{67,3},{4,68},{68... | collective-permute-start | bytes 196616 | tf_op jit(solution)/shard_map/ppermute | solution.py:334
  132.5 5.0 %collective-permute-start.26 = (bf16[2,256,128]{1,2,0:T(8,128)(2,1)S(1)}, bf16[2,256,128]{1,2,0:T(8,128)(2,1)S(1)}, u32[]{:S(2)}, u32[]{:S(2)}) collective-permute-start(bf16[2,256,128]{1,2,0:T(8,128)(2,1)S(1)} %pad_maximum_fusion.2), channel_id=1, source_target_pairs={{0,48},{16,0},{32,16},{48,32},{1,49},{17,1},{33,17},{49,33},{2,50}... | collective-permute-start | bytes 393224 | tf_op jit(solution)/shard_map/ppermute | solution.py:280
  135.5 7.2 %collective-permute-start.27 = (bf16[2,256,128]{1,2,0:T(8,128)(2,1)S(1)}, bf16[2,256,128]{1,2,0:T(8,128)(2,1)S(1)}, u32[]{:S(2)}, u32[]{:S(2)}) collective-permute-start(bf16[2,256,128]{1,2,0:T(8,128)(2,1)S(1)} %pad_maximum_fusion.2), channel_id=1, source_target_pairs={{0,16},{16,32},{32,48},{48,0},{1,17},{17,33},{33,49},{49,1},{2,18}... | collective-permute-start | bytes 393224 | tf_op jit(solution)/shard_map/ppermute | solution.py:280
  135.5 7.2 %collective-permute-start.28 = (bf16[2,256,128]{1,2,0:T(8,128)(2,1)S(1)}, bf16[2,256,128]{1,2,0:T(8,128)(2,1)S(1)}, u32[]{:S(2)}, u32[]{:S(2)}) collective-permute-start(bf16[2,256,128]{1,2,0:T(8,128)(2,1)S(1)} %pad_maximum_fusion.2), channel_id=1, source_target_pairs={{0,32},{16,48},{32,0},{48,16},{1,33},{17,49},{33,1},{49,17},{2,34}... | collective-permute-start | bytes 393224 | tf_op jit(solution)/shard_map/ppermute | solution.py:280
  142.7 4.4 %collective-permute-start.29 = (bf16[256,1024]{0,1:T(8,128)(2,1)S(1)}, bf16[256,1024]{0,1:T(8,128)(2,1)S(1)}, u32[]{:S(2)}, u32[]{:S(2)}) collective-permute-start(bf16[256,1024]{0,1:T(8,128)(2,1)S(1)} %bitcast.48), channel_id=1, source_target_pairs={{0,8},{8,0},{1,9},{9,1},{2,10},{10,2},{3,11},{11,3},{4,12},{12,4},... | collective-permute-start | bytes 1572872 | tf_op jit(solution)/shard_map/ppermute | solution.py:274
  145.6 5.7 %copy-start.1 = (bf16[512,1024]{1,0:T(8,128)(2,1)S(1)}, bf16[512,1024]{1,0:T(8,128)(2,1)}, u32[]{:S(2)}) copy-start(bf16[512,1024]{1,0:T(8,128)(2,1)} %param.10) | copy-start | bytes 3145732

commit v6 on v4

--- a/solution.py
+++ b/solution.py
@@ -296,9 +296,11 @@
     theirs = lax.ppermute(jnp.stack([others, near]), "zh", [(0, 1), (1, 0)])
     grad = added([jnp.stack([near, others]), theirs])
     grads = [grad, ring(grad, "y", -1), ring(grad, "y", 1), ring(grad, "y", 2)]
-    part = jnp.dot(
-        g_half, jnp.concatenate(grads).reshape(2048, 128), preferred_element_type=F32
-    ).reshape(2, 256, 128)
+    part = jnp.dot(g_half[:, :512], grad.reshape(512, 128), preferred_element_type=F32)
+    part += jnp.dot(
+        g_half[:, 512:], jnp.concatenate(grads[1:]).reshape(1536, 128), preferred_element_type=F32
+    )
+    part = part.reshape(2, 256, 128)
     mine, other = (lax.dynamic_index_in_dim(part, k, 0, keepdims=False) for k in (c, 1 - c))
     left = (mine + swap(other)).astype(BF)
     mine = lax.all_to_all(

time: 151 us -> 152 us (level)
    dot_general x1 -> x2, matrix products: 2.3 us -> 3.31 us  [the longest x1 1.97 us: shards(): jnp.dot(g_half[:, 512:], jnp.concatenate(grads[1:]).reshape(1536, 128), p...]
where the time goes in v6:
time: 152 us; the launch traced here: 151 us
  Pallas kernels  50.2 us (33%)
  starting transfers between devices  46.1 us (30%)
  waiting for transfers between devices  25.1 us (17%)
  blocking collectives  13.6 us (9%)
  other arithmetic  6.14 us (4%)
  matrix products  5.91 us (4%)
  local copies, waits for them, and re-layouts  4.01 us (3%)
    pallas_call x4, Pallas kernels, terms(): pl.pallas_call(functools.partial(term_kernel, by_columns, part), in_specs...  32 us
    ppermute x15, starting transfers between devices, ring(): return lax.ppermute(a, axis, [(i, (i + step) % 4) for i in range(4)])  16.1 us
    ppermute x15, waiting for transfers between devices, ring(): return lax.ppermute(a, axis, [(i, (i + step) % 4) for i in range(4)])  14.8 us
    all_to_all x1, blocking collectives, shards(): lax.all_to_all(jnp.broadcast_to(left[None], (8, 256, 128)), ('x', 'zl'),...  13.6 us
    pallas_call x2, Pallas kernels, prepare(): pl.pallas_call(prepare_kernel, in_specs=[pl.BlockSpec(memory_space=pltpu....  12.8 us
    ppermute x6, starting transfers between devices, swap(): return lax.ppermute(a, 'c', [(0, 1), (1, 0)])  11.4 us
    ppermute x3, starting transfers between devices, across_z(): return lax.ppermute(a, ('zl', 'zh'), [(i, 3 - i) for i in range(4)])  6.45 us
    all_to_all x1, starting transfers between devices, shards(): near = added(lax.all_to_all(near, 'x', 0, 0, tiled=True))  4.46 us
  transfers between devices with their start and end apart: 28, of which 12 were waited for; matrix products, arithmetic and copies ran while one was open for 5% of the time, Pallas kernels for 33%

profile of v6, /device:TPU:1, one launch (start us, length us, event | category | flops | bytes accessed | tf_op | source)
XLA Modules:
  0.0 151.4 jit_solution(16971367740153902384)
XLA Ops:
  0.0 1.4 collective-permute-start.3
  1.4 0.0 collective-permute-start.4
  1.4 1.9 %constant_dynamic-slice_fusion.refs_8_ = bf16[256,1024]{1,0:T(8,128)(2,1)} fusion(bf16[512,1024]{1,0:T(8,128)(2,1)} %param.10, s32[]{:T(128)S(6)} %select_n.26), kind=kLoop, calls=%fused_computation.33 | loop fusion | bytes 1048580 | tf_op jit(solution)/shard_map/dynamic_slice | solution.py:255
  3.3 2.9 %collective-permute-start = (bf16[256,1024]{1,0:T(8,128)(2,1)}, bf16[256,1024]{1,0:T(8,128)(2,1)}, u32[]{:S(2)}, u32[]{:S(2)}) collective-permute-start(bf16[256,1024]{1,0:T(8,128)(2,1)} %constant_dynamic-slice_fusion.refs_8_), channel_id=1, source_target_pairs={{0,6},{2,0},{4,2},{6,4},{1,7},{3,1},{5,3},{7,5},{8,14},{10,8},{12,... | collective-permute-start | bytes 1572872 | tf_op jit(solution)/shard_map/ppermute | solution.py:253
  6.2 0.0 collective-permute-start.1
  6.2 3.8 %collective-permute-start.2 = (bf16[256,1024]{1,0:T(8,128)(2,1)}, bf16[256,1024]{1,0:T(8,128)(2,1)}, u32[]{:S(2)}, u32[]{:S(2)}) collective-permute-start(bf16[256,1024]{1,0:T(8,128)(2,1)} %constant_dynamic-slice_fusion.refs_8_), channel_id=1, source_target_pairs={{0,65},{1,64},{64,1},{65,0},{2,67},{3,66},{66,3},{67,2},{4,69},{5,... | collective-permute-start | bytes 1572872 | tf_op jit(solution)/shard_map/ppermute | solution.py:250
  10.0 0.7 pad_add_fusion.here
  10.6 3.6 %shard_map.74 = bf16[512,2048]{1,0:T(8,128)(2,1)} custom-call(s32[4]{0:T(128)} %pad_add_fusion.here, bf16[512,4096]{1,0:T(8,128)(2,1)} %g.1), custom_call_target="tpu_custom_call" | custom-call | bytes 4194304 | tf_op jit(solution)/shard_map/pallas_call | solution.py:232
  14.2 0.0 copy-start.1
  14.2 6.9 %shard_map.73 = (bf16[2048,576]{1,0:T(8,128)(2,1)}, bf16[1024,576]{1,0:T(8,128)(2,1)}, bf16[2048,1024]{1,0:T(8,128)(2,1)}) custom-call(s32[4]{0:T(128)} %pad_add_fusion.here, bf16[576,4096]{1,0:T(8,128)(2,1)} %pre.1, bf16[576,1024]{1,0:T(8,128)(2,1)} %cot.1, bf16[4096,1024]{1,0:T(8,128)(2,1)} %refs_6_.7), custom_call_target="tpu_custom_call" | custom-call | flops 70778880 | bytes 5242880 | tf_op jit(solution)/shard_map/pallas_call | solution.py:73
  21.2 0.0 collective-permute-done.upper.refs_9_
  21.2 0.6 collective-permute-done.2.refs_8_
  21.8 1.4 collective-permute-start.7
  23.2 0.1 collective-permute-start.8
  23.3 1.8 %shard_map.75 = (bf16[128,1024]{1,0:T(8,128)(2,1)}, bf16[128,1024]{1,0:T(8,128)(2,1)}) custom-call(bf16[256,1024]{1,0:T(8,128)(2,1)} %collective-permute-done.upper.refs_9_, bf16[256,1024]{1,0:T(8,128)(2,1)} %collective-permute-done.1.lower.refs_10_), custom_call_target="tpu_custom_call" | custom-call | tf_op jit(solution)/shard_map/pallas_call | solution.py:102
  25.1 2.6 %collective-permute-start.5 = (bf16[128,1024]{1,0:T(8,128)(2,1)}, bf16[128,1024]{1,0:T(8,128)(2,1)S(1)}, u32[]{:S(2)}, u32[]{:S(2)}) collective-permute-start(bf16[128,1024]{1,0:T(8,128)(2,1)} %get-tuple-element.45), channel_id=1, source_target_pairs={{0,6},{2,0},{4,2},{6,4},{1,7},{3,1},{5,3},{7,5},{8,14},{10,8},{12,... | collective-permute-start | bytes 786440 | tf_op jit(solution)/shard_map/ppermute | solution.py:253
  27.8 5.9 %shard_map.76 = (bf16[2048,576]{1,0:T(8,128)(2,1)}, bf16[1024,576]{1,0:T(8,128)(2,1)}) custom-call(s32[4]{0:T(128)} %pad_add_fusion.here, bf16[576,4096]{1,0:T(8,128)(2,1)} %collective-permute-done.3.pre, bf16[576,1024]{1,0:T(8,128)(2,1)} %collective-permute-done.4.cot), custom_call_target="tpu_custom_call" | custom-call | flops 70778880 | bytes 5242880 | tf_op jit(solution)/shard_map/pallas_call | solution.py:73
  33.7 2.6 %collective-permute-done.6.refs_12_ = bf16[128,1024]{1,0:T(8,128)(2,1)S(1)} collective-permute-done((bf16[128,1024]{1,0:T(8,128)(2,1)}, bf16[128,1024]{1,0:T(8,128)(2,1)S(1)}, u32[]{:S(2)}, u32[]{:S(2)}) %collective-permute-start.6) | collective-permute-done | bytes 262176 | tf_op jit(solution)/shard_map/ppermute | solution.py:253
  36.4 0.1 collective-permute-start.10
  36.5 2.7 %collective-permute-start.9 = (bf16[256,1024]{1,0:T(8,128)(2,1)}, bf16[256,1024]{1,0:T(8,128)(2,1)S(1)}, u32[]{:S(2)}, u32[]{:S(2)}) collective-permute-start(bf16[256,1024]{1,0:T(8,128)(2,1)} %collective-permute-done.2.refs_8_), channel_id=1, source_target_pairs={{0,6},{2,0},{4,2},{6,4},{1,7},{3,1},{5,3},{7,5},{8,14},{10,8},{12,... | collective-permute-start | bytes 1572872 | tf_op jit(solution)/shard_map/ppermute | solution.py:253
  39.1 2.6 %collective-permute-start.11 = (bf16[128,1024]{1,0:T(8,128)(2,1)S(1)}, bf16[128,1024]{1,0:T(8,128)(2,1)S(1)}, u32[]{:S(2)}, u32[]{:S(2)}) collective-permute-start(bf16[128,1024]{1,0:T(8,128)(2,1)S(1)} %collective-permute-done.5.refs_11_), channel_id=1, source_target_pairs={{0,65},{1,64},{64,1},{65,0},{2,67},{3,66},{66,3},{67,2},{4,69},{5,... | collective-permute-start | bytes 786440 | tf_op jit(solution)/shard_map/ppermute | solution.py:250
  41.8 0.1 collective-permute-start.12
  41.8 12.8 %shard_map.77 = bf16[4,2,4,256,128]{4,3,2,1,0:T(8,128)(2,1)} custom-call(s32[4]{0:T(128)} %pad_add_fusion.here, bf16[1024,576]{1,0:T(8,128)(2,1)} %get-tuple-element.42.refs_0_, bf16[1024,576]{1,0:T(8,128)(2,1)} %get-tuple-element.54.refs_1_, bf16[576,1024]{1,0:T(8,128)(2,1)} %refs_2_.7, bf16[576,1024]{1,0:T(8,128)(2,1)} %collective-permute-done.8.refs_3_, ...), custom_call_target="tpu_custom_call" | custom-call | flops 19327352832 | bytes 12582912 | tf_op jit(solution)/shard_map/pallas_call | solution.py:190
  54.7 0.8 copy-done.6
  55.4 0.0 copy-done.5
  55.5 0.8 copy-done.3
  56.2 0.2 copy-done.4
  56.4 4.5 %all-to-all-start = ((bf16[4,2,4,256,128]{4,3,2,1,0:T(8,128)(2,1)}), bf16[4,2,4,256,128]{4,3,2,1,0:T(8,128)(2,1)}, u32[]{:S(2)}, u32[]{:S(2)}) async-start(bf16[4,2,4,256,128]{4,3,2,1,0:T(8,128)(2,1)} %shard_map.77), calls=%async_computation | async-start | bytes 4194304 | tf_op jit(solution)/shard_map/all_to_all | solution.py:288
  60.9 5.6 %shard_map.80 = bf16[8,256,128]{2,1,0:T(8,128)(2,1)} custom-call(s32[4]{0:T(128)} %pad_add_fusion.here, bf16[1024,576]{1,0:T(8,128)(2,1)} %get-tuple-element.42.refs_0_, bf16[1024,576]{1,0:T(8,128)(2,1)} %get-tuple-element.54.refs_1_, bf16[576,1024]{1,0:T(8,128)(2,1)} %refs_2_.7, bf16[576,1024]{1,0:T(8,128)(2,1)} %collective-permute-done.8.refs_3_, ...), custom_call_target="tpu_custom_call" | custom-call | flops 1207959552 | bytes 3145728 | tf_op jit(solution)/shard_map/pallas_call | solution.py:190
  66.5 0.3 collective-permute-start.18
  66.9 8.0 %shard_map.79 = (bf16[8,256,128]{2,1,0:T(8,128)(2,1)}, bf16[8,256,128]{2,1,0:T(8,128)(2,1)}) custom-call(s32[4]{0:T(128)} %pad_add_fusion.here, bf16[1024,576]{1,0:T(8,128)(2,1)} %get-tuple-element.42.refs_0_, bf16[1024,576]{1,0:T(8,128)(2,1)} %get-tuple-element.54.refs_1_, bf16[576,1024]{1,0:T(8,128)(2,1)} %refs_2_.7, ...), custom_call_target="tpu_custom_call" | custom-call | flops 2415919104 | bytes 6291456 | tf_op jit(solution)/shard_map/pallas_call | solution.py:190
  74.8 0.8 collective-permute-start.17
  75.7 1.9 %collective-permute-start.19 = (bf16[8,256,128]{2,1,0:T(8,128)(2,1)}, bf16[8,256,128]{2,1,0:T(8,128)(2,1)}, u32[]{:S(2)}, u32[]{:S(2)}) collective-permute-start(bf16[8,256,128]{2,1,0:T(8,128)(2,1)} %get-tuple-element.70), channel_id=1, source_target_pairs={{0,6},{2,0},{4,2},{6,4},{1,7},{3,1},{5,3},{7,5},{8,14},{10,8},{12,... | collective-permute-start | bytes 1572872 | tf_op jit(solution)/shard_map/ppermute | solution.py:253
  77.6 5.6 %shard_map.78 = bf16[8,256,128]{2,1,0:T(8,128)(2,1)} custom-call(s32[4]{0:T(128)} %pad_add_fusion.here, bf16[1024,576]{1,0:T(8,128)(2,1)} %get-tuple-element.42.refs_0_, bf16[1024,576]{1,0:T(8,128)(2,1)} %get-tuple-element.54.refs_1_, bf16[576,1024]{1,0:T(8,128)(2,1)} %refs_2_.7, bf16[576,1024]{1,0:T(8,128)(2,1)} %collective-permute-done.8.refs_3_, ...), custom_call_target="tpu_custom_call" | custom-call | flops 1207959552 | bytes 3145728 | tf_op jit(solution)/shard_map/pallas_call | solution.py:190
  83.2 1.5 all-to-all-done
  84.7 1.8 %add_convert_fusion.1 = bf16[1,2,4,256,128]{4,3,2,1,0:T(8,128)(2,1)S(1)} fusion(bf16[4,2,4,256,128]{4,3,2,1,0:T(8,128)(2,1)} %all-to-all-done), kind=kLoop, calls=%fused_computation.11 | loop fusion | flops 2097152 | bytes 2621440 | tf_op jit(solution)/shard_map/convert.2
  86.5 0.1 collective-permute-start.13
  86.6 5.8 %collective-permute-done.17 = bf16[8,256,128]{2,1,0:T(8,128)(2,1)} collective-permute-done((bf16[8,256,128]{2,1,0:T(8,128)(2,1)}, bf16[8,256,128]{2,1,0:T(8,128)(2,1)}, u32[]{:S(2)}, u32[]{:S(2)}) %collective-permute-start.17) | collective-permute-done | bytes 524320 | tf_op jit(solution)/shard_map/ppermute | solution.py:253
  92.4 2.4 %add_convert_fusion = bf16[8,256,128]{2,1,0:T(8,128)(2,1)} fusion(bf16[8,256,128]{2,1,0:T(8,128)(2,1)} %collective-permute-done.19, bf16[8,256,128]{2,1,0:T(8,128)(2,1)} %collective-permute-done.18, bf16[8,256,128]{2,1,0:T(8,128)(2,1)} %collective-permute-done.17, bf16[8,256,128]{2,1,0:T(8,128)(2,1)S(1)} %copy-done.2), kind=kLoop, calls=%fused_computation.10 | loop fusion | flops 2097152 | bytes 2621440 | tf_op jit(solution)/shard_map/convert_element_type | solution.py:278
  94.8 4.1 %all-to-all-start.1 = ((bf16[8,256,128]{2,1,0:T(8,128)(2,1)}), bf16[8,256,128]{2,1,0:T(8,128)(2,1)S(1)}, u32[]{:S(2)}, u32[]{:S(2)}) async-start(bf16[8,256,128]{2,1,0:T(8,128)(2,1)} %add_convert_fusion), calls=%async_computation.1 | async-start | bytes 1048576 | tf_op jit(solution)/shard_map/all_to_all | solution.py:284
  98.9 1.0 fusion.9
  99.9 0.1 collective-permute-start.14
  100.0 2.7 %collective-permute-start.15 = (bf16[256,128]{1,0:T(8,128)(2,1)S(1)}, bf16[256,128]{1,0:T(8,128)(2,1)S(1)}, u32[]{:S(2)}, u32[]{:S(2)}) collective-permute-start(bf16[256,128]{1,0:T(8,128)(2,1)S(1)} %get-tuple-element.73), channel_id=1, source_target_pairs={{0,6},{2,0},{4,2},{6,4},{1,7},{3,1},{5,3},{7,5},{8,14},{10,8},{12,... | collective-permute-start | bytes 196616 | tf_op jit(solution)/shard_map/ppermute | solution.py:253
  102.7 3.3 %all-to-all-done.1 = bf16[8,256,128]{2,1,0:T(8,128)(2,1)S(1)} async-done(((bf16[8,256,128]{2,1,0:T(8,128)(2,1)}), bf16[8,256,128]{2,1,0:T(8,128)(2,1)S(1)}, u32[]{:S(2)}, u32[]{:S(2)}) %all-to-all-start.1) | async-done | bytes 524320 | tf_op jit(solution)/shard_map/all_to_all | solution.py:284
  106.0 0.1 add_convert_fusion.3
  106.1 1.5 collective-permute-done.16
  107.7 3.6 %collective-permute-start.20 = (bf16[2,256,128]{2,1,0:T(8,128)(2,1)S(1)}, bf16[2,256,128]{2,1,0:T(8,128)(2,1)S(1)}, u32[]{:S(2)}, u32[]{:S(2)}) collective-permute-start(bf16[2,256,128]{2,1,0:T(8,128)(2,1)S(1)} %pad_maximum_fusion.1), channel_id=1, source_target_pairs={{0,1},{1,0},{2,3},{3,2},{4,5},{5,4},{6,7},{7,6},{8,9},{9,8},{10,11... | collective-permute-start | bytes 393224 | tf_op jit(solution)/shard_map/ppermute | solution.py:296
  111.3 2.4 %collective-permute-done.20 = bf16[2,256,128]{2,1,0:T(8,128)(2,1)S(1)} collective-permute-done((bf16[2,256,128]{2,1,0:T(8,128)(2,1)S(1)}, bf16[2,256,128]{2,1,0:T(8,128)(2,1)S(1)}, u32[]{:S(2)}, u32[]{:S(2)}) %collective-permute-start.20) | collective-permute-done | bytes 131104 | tf_op jit(solution)/shard_map/ppermute | solution.py:296
  113.7 0.4 collective-permute-start.21
  114.1 1.1 collective-permute-start.22
  115.2 0.5 collective-permute-start.23
  115.7 2.1 %collective-permute-done.21 = bf16[2,256,128]{2,1,0:T(8,128)(2,1)S(1)} collective-permute-done((bf16[2,256,128]{2,1,0:T(8,128)(2,1)S(1)}, bf16[2,256,128]{2,1,0:T(8,128)(2,1)S(1)}, u32[]{:S(2)}, u32[]{:S(2)}) %collective-permute-start.21) | collective-permute-done | bytes 131104 | tf_op jit(solution)/shard_map/ppermute | solution.py:253
  117.8 1.3 collective-permute-done.22
  119.1 1.4 collective-permute-done.23
  120.6 2.0 %fusion = f32[512,128]{1,0:T(8,128)S(1)} fusion(bf16[1536,128]{1,0:T(8,128)(2,1)S(1)} %bitcast.42, bf16[512,2048]{1,0:T(8,128)(2,1)} %shard_map.74), kind=kOutput, calls=%fused_computation | convolution fusion | flops 201326592 | bytes 2228224 | tf_op jit(solution)/shard_map/dot_general | solution.py:300
  122.5 1.3 convolution_add_fusion
  123.9 6.4 %collective-permute-start.24 = (f32[256,128]{1,0:T(8,128)S(1)}, f32[256,128]{1,0:T(8,128)S(1)}, u32[]{:S(2)}, u32[]{:S(2)}) collective-permute-start(f32[256,128]{1,0:T(8,128)S(1)} %dynamic-slice_bitcast_fusion.1), channel_id=1, source_target_pairs={{0,8},{8,0},{1,9},{9,1},{2,10},{10,2},{3,11},{11,3},{4,12},{12,4},... | collective-permute-start | bytes 393224 | tf_op jit(solution)/shard_map/ppermute | solution.py:247
  130.3 1.0 collective-permute-done.24
  131.3 0.1 broadcast_in_dim.2
  131.4 13.6 %all_to_all.15 = bf16[8,256,128]{2,1,0:T(8,128)(2,1)S(1)} all-to-all(bf16[8,256,128]{2,1,0:T(8,128)(2,1)S(1)} %broadcast_in_dim.2), channel_id=1, replica_groups=mesh['zl'=2,'x'=4,'c'=2,'y'=4,'zh'=2] {'x','zl'}, dimensions={0} | all-to-all | bytes 1048576 | tf_op jit(solution)/shard_map/all_to_all | solution.py:306
  144.9 0.2 copy.8
  145.1 2.1 %collective-permute-start.25 = (bf16[256,1024]{0,1:T(8,128)(2,1)S(1)}, bf16[256,1024]{0,1:T(8,128)(2,1)S(1)}, u32[]{:S(2)}, u32[]{:S(2)}) collective-permute-start(bf16[256,1024]{0,1:T(8,128)(2,1)S(1)} %bitcast.40), channel_id=1, source_target_pairs={{0,8},{8,0},{1,9},{9,1},{2,10},{10,2},{3,11},{11,3},{4,12},{12,4},... | collective-permute-start | bytes 1572872 | tf_op jit(solution)/shard_map/ppermute | solution.py:247
  147.3 1.5 %collective-permute-done.25 = bf16[256,1024]{0,1:T(8,128)(2,1)S(1)} collective-permute-done((bf16[256,1024]{0,1:T(8,128)(2,1)S(1)}, bf16[256,1024]{0,1:T(8,128)(2,1)S(1)}, u32[]{:S(2)}, u32[]{:S(2)}) %collective-permute-start.25) | collective-permute-done | bytes 524320 | tf_op jit(solution)/shard_map/ppermute | solution.py:247
  148.8 2.6 %fusion.2 = f32[512,1024]{1,0:T(8,128)} fusion(bf16[1024,1024]{1,0:T(8,128)(2,1)S(1)} %copy-done, bf16[256,1024]{0,1:T(8,128)(2,1)S(1)} %collective-permute-done.25, bf16[256,1024]{0,1:T(8,128)(2,1)S(1)} %bitcast.41, pred[]{:T(512)S(6)} %eq.3), kind=kOutput, calls=%fused_computation.4 | convolution fusion | flops 1078460416 | bytes 5242881 | tf_op jit(solution)/shard_map/dot_general | solution.py:311
  (38 shorter events, 0.3 us)
Async XLA Ops:
  0.0 148.8 %copy-start = (bf16[1024,1024]{1,0:T(8,128)(2,1)S(1)}, bf16[1024,1024]{1,0:T(8,128)(2,1)}, u32[]{:S(2)}) copy-start(bf16[1024,1024]{1,0:T(8,128)(2,1)} %param.12) | copy-start | bytes 6291460
  0.0 21.8 %collective-permute-start.3 = (bf16[576,4096]{1,0:T(8,128)(2,1)}, bf16[576,4096]{1,0:T(8,128)(2,1)}, u32[]{:S(2)}, u32[]{:S(2)}) collective-permute-start(bf16[576,4096]{1,0:T(8,128)(2,1)} %pre.1), channel_id=1, source_target_pairs={{0,8},{8,0},{1,9},{9,1},{2,10},{10,2},{3,11},{11,3},{4,12},{12,4},... | collective-permute-start | bytes 14155784 | tf_op jit(solution)/shard_map/ppermute | solution.py:247
  1.4 20.4 %collective-permute-start.4 = (bf16[576,1024]{1,0:T(8,128)(2,1)}, bf16[576,1024]{1,0:T(8,128)(2,1)}, u32[]{:S(2)}, u32[]{:S(2)}) collective-permute-start(bf16[576,1024]{1,0:T(8,128)(2,1)} %cot.1), channel_id=1, source_target_pairs={{0,8},{8,0},{1,9},{9,1},{2,10},{10,2},{3,11},{11,3},{4,12},{12,4},... | collective-permute-start | bytes 3538952 | tf_op jit(solution)/shard_map/ppermute | solution.py:247
  3.3 17.9 %collective-permute-start = (bf16[256,1024]{1,0:T(8,128)(2,1)}, bf16[256,1024]{1,0:T(8,128)(2,1)}, u32[]{:S(2)}, u32[]{:S(2)}) collective-permute-start(bf16[256,1024]{1,0:T(8,128)(2,1)} %constant_dynamic-slice_fusion.refs_8_), channel_id=1, source_target_pairs={{0,6},{2,0},{4,2},{6,4},{1,7},{3,1},{5,3},{7,5},{8,14},{10,8},{12,... | collective-permute-start | bytes 1572872 | tf_op jit(solution)/shard_map/ppermute | solution.py:253
  6.2 15.0 %collective-permute-start.1 = (bf16[256,1024]{1,0:T(8,128)(2,1)}, bf16[256,1024]{1,0:T(8,128)(2,1)}, u32[]{:S(2)}, u32[]{:S(2)}) collective-permute-start(bf16[256,1024]{1,0:T(8,128)(2,1)} %constant_dynamic-slice_fusion.refs_8_), channel_id=1, source_target_pairs={{0,2},{2,4},{4,6},{6,0},{1,3},{3,5},{5,7},{7,1},{8,10},{10,12},{12... | collective-permute-start | bytes 1572872 | tf_op jit(solution)/shard_map/ppermute | solution.py:253
  6.2 15.6 %collective-permute-start.2 = (bf16[256,1024]{1,0:T(8,128)(2,1)}, bf16[256,1024]{1,0:T(8,128)(2,1)}, u32[]{:S(2)}, u32[]{:S(2)}) collective-permute-start(bf16[256,1024]{1,0:T(8,128)(2,1)} %constant_dynamic-slice_fusion.refs_8_), channel_id=1, source_target_pairs={{0,65},{1,64},{64,1},{65,0},{2,67},{3,66},{66,3},{67,2},{4,69},{5,... | collective-permute-start | bytes 1572872 | tf_op jit(solution)/shard_map/ppermute | solution.py:250
  14.2 9.0 %copy-start.1 = (bf16[576,1024]{1,0:T(8,128)(2,1)S(1)}, bf16[576,1024]{1,0:T(8,128)(2,1)}, u32[]{:S(2)}) copy-start(bf16[576,1024]{1,0:T(8,128)(2,1)} %refs_2_.7) | copy-start | bytes 3538948
  21.8 14.5 %collective-permute-start.7 = (bf16[2048,1024]{1,0:T(8,128)(2,1)}, bf16[2048,1024]{1,0:T(8,128)(2,1)}, u32[]{:S(2)}, u32[]{:S(2)}) collective-permute-start(bf16[2048,1024]{1,0:T(8,128)(2,1)} %get-tuple-element.47), channel_id=1, source_target_pairs={{0,8},{8,0},{1,9},{9,1},{2,10},{10,2},{3,11},{11,3},{4,12},{12,4},... | collective-permute-start | bytes 12582920 | tf_op jit(solution)/shard_map/ppermute | solution.py:247
  23.2 13.1 %collective-permute-start.8 = (bf16[576,1024]{1,0:T(8,128)(2,1)S(1)}, bf16[576,1024]{1,0:T(8,128)(2,1)}, u32[]{:S(2)}, u32[]{:S(2)}) collective-permute-start(bf16[576,1024]{1,0:T(8,128)(2,1)S(1)} %copy-done.1), channel_id=1, source_target_pairs={{0,8},{8,0},{1,9},{9,1},{2,10},{10,2},{3,11},{11,3},{4,12},{12,4},... | collective-permute-start | bytes 3538952 | tf_op jit(solution)/shard_map/ppermute | solution.py:247
  25.1 8.6 %collective-permute-start.5 = (bf16[128,1024]{1,0:T(8,128)(2,1)}, bf16[128,1024]{1,0:T(8,128)(2,1)S(1)}, u32[]{:S(2)}, u32[]{:S(2)}) collective-permute-start(bf16[128,1024]{1,0:T(8,128)(2,1)} %get-tuple-element.45), channel_id=1, source_target_pairs={{0,6},{2,0},{4,2},{6,4},{1,7},{3,1},{5,3},{7,5},{8,14},{10,8},{12,... | collective-permute-start | bytes 786440 | tf_op jit(solution)/shard_map/ppermute | solution.py:253
  27.8 8.6 %collective-permute-start.6 = (bf16[128,1024]{1,0:T(8,128)(2,1)}, bf16[128,1024]{1,0:T(8,128)(2,1)S(1)}, u32[]{:S(2)}, u32[]{:S(2)}) collective-permute-start(bf16[128,1024]{1,0:T(8,128)(2,1)} %get-tuple-element.46), channel_id=1, source_target_pairs={{0,2},{2,4},{4,6},{6,0},{1,3},{3,5},{5,7},{7,1},{8,10},{10,12},{12... | collective-permute-start | bytes 786440 | tf_op jit(solution)/shard_map/ppermute | solution.py:253
  33.7 8.1 %copy-start.7 = (bf16[128,1024]{1,0:T(8,128)(2,1)}, bf16[128,1024]{1,0:T(8,128)(2,1)S(1)}, u32[]{:S(2)}) copy-start(bf16[128,1024]{1,0:T(8,128)(2,1)S(1)} %collective-permute-done.5.refs_11_) | copy-start | bytes 786436
  36.4 2.8 %copy-start.8 = (bf16[128,1024]{1,0:T(8,128)(2,1)}, bf16[128,1024]{1,0:T(8,128)(2,1)S(1)}, u32[]{:S(2)}) copy-start(bf16[128,1024]{1,0:T(8,128)(2,1)S(1)} %collective-permute-done.6.refs_12_) | copy-start | bytes 786436
  36.4 18.3 %collective-permute-start.10 = (bf16[256,1024]{1,0:T(8,128)(2,1)}, bf16[256,1024]{1,0:T(8,128)(2,1)S(1)}, u32[]{:S(2)}, u32[]{:S(2)}) collective-permute-start(bf16[256,1024]{1,0:T(8,128)(2,1)} %collective-permute-done.2.refs_8_), channel_id=1, source_target_pairs={{0,2},{2,4},{4,6},{6,0},{1,3},{3,5},{5,7},{7,1},{8,10},{10,12},{12... | collective-permute-start | bytes 1572872 | tf_op jit(solution)/shard_map/ppermute | solution.py:253
  36.5 19.0 %collective-permute-start.9 = (bf16[256,1024]{1,0:T(8,128)(2,1)}, bf16[256,1024]{1,0:T(8,128)(2,1)S(1)}, u32[]{:S(2)}, u32[]{:S(2)}) collective-permute-start(bf16[256,1024]{1,0:T(8,128)(2,1)} %collective-permute-done.2.refs_8_), channel_id=1, source_target_pairs={{0,6},{2,0},{4,2},{6,4},{1,7},{3,1},{5,3},{7,5},{8,14},{10,8},{12,... | collective-permute-start | bytes 1572872 | tf_op jit(solution)/shard_map/ppermute | solution.py:253
  39.1 15.5 %collective-permute-start.11 = (bf16[128,1024]{1,0:T(8,128)(2,1)S(1)}, bf16[128,1024]{1,0:T(8,128)(2,1)S(1)}, u32[]{:S(2)}, u32[]{:S(2)}) collective-permute-start(bf16[128,1024]{1,0:T(8,128)(2,1)S(1)} %collective-permute-done.5.refs_11_), channel_id=1, source_target_pairs={{0,65},{1,64},{64,1},{65,0},{2,67},{3,66},{66,3},{67,2},{4,69},{5,... | collective-permute-start | bytes 786440 | tf_op jit(solution)/shard_map/ppermute | solution.py:250
  41.8 12.9 %collective-permute-start.12 = (bf16[128,1024]{1,0:T(8,128)(2,1)}, bf16[128,1024]{1,0:T(8,128)(2,1)S(1)}, u32[]{:S(2)}, u32[]{:S(2)}) collective-permute-start(bf16[128,1024]{1,0:T(8,128)(2,1)} %copy-done.8), channel_id=1, source_target_pairs={{0,65},{1,64},{64,1},{65,0},{2,67},{3,66},{66,3},{67,2},{4,69},{5,... | collective-permute-start | bytes 786440 | tf_op jit(solution)/shard_map/ppermute | solution.py:250
  54.6 0.8 copy-start.5
  54.7 0.8 copy-start.6
  55.4 0.8 copy-start.3
  55.4 1.0 copy-start.4
  56.4 28.2 %all-to-all-start = ((bf16[4,2,4,256,128]{4,3,2,1,0:T(8,128)(2,1)}), bf16[4,2,4,256,128]{4,3,2,1,0:T(8,128)(2,1)}, u32[]{:S(2)}, u32[]{:S(2)}) async-start(bf16[4,2,4,256,128]{4,3,2,1,0:T(8,128)(2,1)} %shard_map.77), calls=%async_computation | async-start | bytes 4194304 | tf_op jit(solution)/shard_map/all_to_all | solution.py:288
  66.5 20.0 %collective-permute-start.18 = (bf16[8,256,128]{2,1,0:T(8,128)(2,1)}, bf16[8,256,128]{2,1,0:T(8,128)(2,1)}, u32[]{:S(2)}, u32[]{:S(2)}) collective-permute-start(bf16[8,256,128]{2,1,0:T(8,128)(2,1)} %shard_map.80), channel_id=1, source_target_pairs={{0,4},{2,6},{4,0},{6,2},{1,5},{3,7},{5,1},{7,3},{8,12},{10,14},{12... | collective-permute-start | bytes 1572872 | tf_op jit(solution)/shard_map/ppermute | solution.py:253
  74.8 17.5 %collective-permute-start.17 = (bf16[8,256,128]{2,1,0:T(8,128)(2,1)}, bf16[8,256,128]{2,1,0:T(8,128)(2,1)}, u32[]{:S(2)}, u32[]{:S(2)}) collective-permute-start(bf16[8,256,128]{2,1,0:T(8,128)(2,1)} %get-tuple-element.67), channel_id=1, source_target_pairs={{0,2},{2,4},{4,6},{6,0},{1,3},{3,5},{5,7},{7,1},{8,10},{10,12},{12... | collective-permute-start | bytes 1572872 | tf_op jit(solution)/shard_map/ppermute | solution.py:253
  75.7 16.7 %collective-permute-start.19 = (bf16[8,256,128]{2,1,0:T(8,128)(2,1)}, bf16[8,256,128]{2,1,0:T(8,128)(2,1)}, u32[]{:S(2)}, u32[]{:S(2)}) collective-permute-start(bf16[8,256,128]{2,1,0:T(8,128)(2,1)} %get-tuple-element.70), channel_id=1, source_target_pairs={{0,6},{2,0},{4,2},{6,4},{1,7},{3,1},{5,3},{7,5},{8,14},{10,8},{12,... | collective-permute-start | bytes 1572872 | tf_op jit(solution)/shard_map/ppermute | solution.py:253
  83.2 9.2 %copy-start.2 = (bf16[8,256,128]{2,1,0:T(8,128)(2,1)S(1)}, bf16[8,256,128]{2,1,0:T(8,128)(2,1)}, u32[]{:S(2)}) copy-start(bf16[8,256,128]{2,1,0:T(8,128)(2,1)} %shard_map.78) | copy-start | bytes 1572868
  86.5 12.4 %collective-permute-start.13 = (bf16[4,256,128]{2,1,0:T(8,128)(2,1)S(1)}, bf16[4,256,128]{2,1,0:T(8,128)(2,1)}, u32[]{:S(2)}, u32[]{:S(2)}) collective-permute-start(bf16[4,256,128]{2,1,0:T(8,128)(2,1)S(1)} %dynamic-slice_bitcast_fusion), channel_id=1, source_target_pairs={{0,64},{64,0},{1,65},{65,1},{2,66},{66,2},{3,67},{67,3},{4,68},{68... | collective-permute-start | bytes 786440 | tf_op jit(solution)/shard_map/ppermute | solution.py:289
  94.8 11.2 %all-to-all-start.1 = ((bf16[8,256,128]{2,1,0:T(8,128)(2,1)}), bf16[8,256,128]{2,1,0:T(8,128)(2,1)S(1)}, u32[]{:S(2)}, u32[]{:S(2)}) async-start(bf16[8,256,128]{2,1,0:T(8,128)(2,1)} %add_convert_fusion), calls=%async_computation.1 | async-start | bytes 1048576 | tf_op jit(solution)/shard_map/all_to_all | solution.py:284
  99.9 6.2 %collective-permute-start.14 = (bf16[256,128]{1,0:T(8,128)(2,1)S(1)}, bf16[256,128]{1,0:T(8,128)(2,1)S(1)}, u32[]{:S(2)}, u32[]{:S(2)}) collective-permute-start(bf16[256,128]{1,0:T(8,128)(2,1)S(1)} %get-tuple-element.71), channel_id=1, source_target_pairs={{0,2},{2,4},{4,6},{6,0},{1,3},{3,5},{5,7},{7,1},{8,10},{10,12},{12... | collective-permute-start | bytes 196616 | tf_op jit(solution)/shard_map/ppermute | solution.py:253
  100.0 6.1 %collective-permute-start.15 = (bf16[256,128]{1,0:T(8,128)(2,1)S(1)}, bf16[256,128]{1,0:T(8,128)(2,1)S(1)}, u32[]{:S(2)}, u32[]{:S(2)}) collective-permute-start(bf16[256,128]{1,0:T(8,128)(2,1)S(1)} %get-tuple-element.73), channel_id=1, source_target_pairs={{0,6},{2,0},{4,2},{6,4},{1,7},{3,1},{5,3},{7,5},{8,14},{10,8},{12,... | collective-permute-start | bytes 196616 | tf_op jit(solution)/shard_map/ppermute | solution.py:253
  102.7 4.9 %collective-permute-start.16 = (bf16[256,128]{1,0:T(8,128)(2,1)S(1)}, bf16[256,128]{1,0:T(8,128)(2,1)S(1)}, u32[]{:S(2)}, u32[]{:S(2)}) collective-permute-start(bf16[256,128]{1,0:T(8,128)(2,1)S(1)} %get-tuple-element.72), channel_id=1, source_target_pairs={{0,4},{2,6},{4,0},{6,2},{1,5},{3,7},{5,1},{7,3},{8,12},{10,14},{12... | collective-permute-start | bytes 196616 | tf_op jit(solution)/shard_map/ppermute | solution.py:253
  107.7 6.0 %collective-permute-start.20 = (bf16[2,256,128]{2,1,0:T(8,128)(2,1)S(1)}, bf16[2,256,128]{2,1,0:T(8,128)(2,1)S(1)}, u32[]{:S(2)}, u32[]{:S(2)}) collective-permute-start(bf16[2,256,128]{2,1,0:T(8,128)(2,1)S(1)} %pad_maximum_fusion.1), channel_id=1, source_target_pairs={{0,1},{1,0},{2,3},{3,2},{4,5},{5,4},{6,7},{7,6},{8,9},{9,8},{10,11... | collective-permute-start | bytes 393224 | tf_op jit(solution)/shard_map/ppermute | solution.py:296
  113.7 4.1 %collective-permute-start.21 = (bf16[2,256,128]{2,1,0:T(8,128)(2,1)S(1)}, bf16[2,256,128]{2,1,0:T(8,128)(2,1)S(1)}, u32[]{:S(2)}, u32[]{:S(2)}) collective-permute-start(bf16[2,256,128]{2,1,0:T(8,128)(2,1)S(1)} %add_convert_fusion.2), channel_id=1, source_target_pairs={{0,6},{2,0},{4,2},{6,4},{1,7},{3,1},{5,3},{7,5},{8,14},{10,8},{12,... | collective-permute-start | bytes 393224 | tf_op jit(solution)/shard_map/ppermute | solution.py:253
  114.1 5.0 %collective-permute-start.22 = (bf16[2,256,128]{2,1,0:T(8,128)(2,1)S(1)}, bf16[2,256,128]{2,1,0:T(8,128)(2,1)S(1)}, u32[]{:S(2)}, u32[]{:S(2)}) collective-permute-start(bf16[2,256,128]{2,1,0:T(8,128)(2,1)S(1)} %add_convert_fusion.2), channel_id=1, source_target_pairs={{0,2},{2,4},{4,6},{6,0},{1,3},{3,5},{5,7},{7,1},{8,10},{10,12},{12... | collective-permute-start | bytes 393224 | tf_op jit(solution)/shard_map/ppermute | solution.py:253
  115.2 5.3 %collective-permute-start.23 = (bf16[2,256,128]{2,1,0:T(8,128)(2,1)S(1)}, bf16[2,256,128]{2,1,0:T(8,128)(2,1)S(1)}, u32[]{:S(2)}, u32[]{:S(2)}) collective-permute-start(bf16[2,256,128]{2,1,0:T(8,128)(2,1)S(1)} %add_convert_fusion.2), channel_id=1, source_target_pairs={{0,4},{2,6},{4,0},{6,2},{1,5},{3,7},{5,1},{7,3},{8,12},{10,14},{12... | collective-permute-start | bytes 393224 | tf_op jit(solution)/shard_map/ppermute | solution.py:253
  123.9 7.4 %collective-permute-start.24 = (f32[256,128]{1,0:T(8,128)S(1)}, f32[256,128]{1,0:T(8,128)S(1)}, u32[]{:S(2)}, u32[]{:S(2)}) collective-permute-start(f32[256,128]{1,0:T(8,128)S(1)} %dynamic-slice_bitcast_fusion.1), channel_id=1, source_target_pairs={{0,8},{8,0},{1,9},{9,1},{2,10},{10,2},{3,11},{11,3},{4,12},{12,4},... | collective-permute-start | bytes 393224 | tf_op jit(solution)/shard_map/ppermute | solution.py:247
  145.1 3.7 %collective-permute-start.25 = (bf16[256,1024]{0,1:T(8,128)(2,1)S(1)}, bf16[256,1024]{0,1:T(8,128)(2,1)S(1)}, u32[]{:S(2)}, u32[]{:S(2)}) collective-permute-start(bf16[256,1024]{0,1:T(8,128)(2,1)S(1)} %bitcast.40), channel_id=1, source_target_pairs={{0,8},{8,0},{1,9},{9,1},{2,10},{10,2},{3,11},{11,3},{4,12},{12,4},... | collective-permute-start | bytes 1572872 | tf_op jit(solution)/shard_map/ppermute | solution.py:247
